TPU v7x, 128 devices: a whole 4x4x4 slice. The times are simulated.
128 devices in a mesh: dev: 128 (over x, y, z, core).
Axes of the slice: x: 4, y: 4, z: 4, core: 2. Of those that a mesh axis runs over, the one named last changes fastest.
Arguments:
- object_field: float32 [2, 16384, 2048], P(None, 'dev'), may hold values from -5 to 5
- probe: float32 [2, 4, 128, 128], replicated, may hold values from -6 to 6
- amplitudes: float32 [2048, 128, 128], P('dev'), may hold values from 0.2 to 3
- positions: int32 [2048, 2], P('dev'), may hold values from 0 to 16256, as said below
- counts: int32 [128], P('dev'), may hold values from 1 to 16, as said below
Outputs:
- new_object: float32 [2, 16384, 2048], P(None, 'dev')
- new_probe: float32 [2, 4, 128, 128], replicated
Inputs may be any that keep to these rules, and one draw needn't show every extreme that they name: `positions`: slot j's top row lies in the object rows of device j // 16: from (j // 16) * 128 to (j // 16) * 128 + 127, and the window stays inside the object; the left column is at most 1920. `counts`: slots of a device below its count are live, the others are ignored.
All inputs are finite; a program needn't handle non-finite values.
Results may differ from a plain program's by a relative error of at most 0.0003.
Values sent between devices are 32-bit elements; how exact they have to be, the bound alone decides.
No kernel may reach another device: no remote copies, remote signals or barrier semaphores. Data moves between devices by JAX's collectives and lax.ppermute only.
A program may use at most 128 MiB of HBM per device.

v0:
```python
import math

import jax
import jax.numpy as jnp
from jax import lax
from jax.sharding import PartitionSpec as P

ITERS = 2


SIGMA = 0.5


def from_behind(value, axis, steps):
    count = lax.axis_size(axis)
    leading, last = (max(0, -steps), min(count, count - steps))
    return lax.ppermute(value, axis, [(source, source + steps) for source in range(leading, last)])


def tables(length):
    index = jnp.arange(length, dtype=jnp.int32)
    phase = index[:, None] * index[None, :] % length
    angle = phase.astype(jnp.float32) * (2.0 * math.pi / length)
    factor = 1.0 / math.sqrt(length)
    return (jnp.cos(angle) * factor, -jnp.sin(angle) * factor)


def left_product(cosine, sine, real, imag):
    best = lax.Precision.HIGHEST
    cos_real = jnp.einsum("ab,...bc->...ac", cosine, real, precision=best)
    cos_imag = jnp.einsum("ab,...bc->...ac", cosine, imag, precision=best)
    sin_real = jnp.einsum("ab,...bc->...ac", sine, real, precision=best)
    sin_imag = jnp.einsum("ab,...bc->...ac", sine, imag, precision=best)
    return (cos_real - sin_imag, cos_imag + sin_real)


def right_product(real, imag, cosine, sine):
    best = lax.Precision.HIGHEST
    real_cos = jnp.einsum("...ab,bc->...ac", real, cosine, precision=best)
    imag_cos = jnp.einsum("...ab,bc->...ac", imag, cosine, precision=best)
    real_sin = jnp.einsum("...ab,bc->...ac", real, sine, precision=best)
    imag_sin = jnp.einsum("...ab,bc->...ac", imag, sine, precision=best)
    return (real_cos - imag_sin, imag_cos + real_sin)


def transform(real, imag, cosine, sine):
    mid_real, mid_imag = left_product(cosine, sine, real, imag)
    return right_product(mid_real, mid_imag, cosine, sine)


def window_terms(patches, amplitudes, live, probe, cosine, sine):
    probe_real = probe[0][None]
    probe_imag = probe[1][None]
    patch_real = patches[:, 0][:, None]
    patch_imag = patches[:, 1][:, None]
    wave_real = probe_real * patch_real - probe_imag * patch_imag
    wave_imag = probe_real * patch_imag + probe_imag * patch_real
    far_real, far_imag = transform(wave_real, wave_imag, cosine, sine)
    intensity = jnp.sum(far_real * far_real + far_imag * far_imag, axis=1)
    ratio = amplitudes / jnp.sqrt(intensity + SIGMA)
    weight = ((1.0 - ratio) * live[:, None, None])[:, None]
    back_real, back_imag = transform(far_real * weight, far_imag * weight, cosine, -sine)
    grad_real = jnp.sum(probe_real * back_real + probe_imag * back_imag, axis=1)
    grad_imag = jnp.sum(probe_real * back_imag - probe_imag * back_real, axis=1)
    power = jnp.sum(probe[0] * probe[0] + probe[1] * probe[1], axis=0)
    lit = live[:, None, None] * power[None]
    gradients = jnp.stack([grad_real, grad_imag, lit], axis=1)
    mode_real = jnp.sum(patch_real * back_real + patch_imag * back_imag, axis=0)
    mode_imag = jnp.sum(patch_real * back_imag - patch_imag * back_real, axis=0)
    weighted = live[:, None, None] * (patches[:, 0] * patches[:, 0] + patches[:, 1] * patches[:, 1])
    pnorm = jnp.sum(weighted, axis=0)
    probe_terms = jnp.concatenate([mode_real, mode_imag, pnorm[None]], axis=0)
    return (gradients, probe_terms)


def cut_windows(frame, rows, cols, length):

    def single(row, col):
        return lax.dynamic_slice(frame, (0, row, col), (frame.shape[0], length, length))

    return jax.vmap(single)(rows, cols)


def place_windows(frame, pieces, rows, cols):
    length = pieces.shape[-1]

    def add_one(index, current):
        row = rows[index]
        col = cols[index]
        old_part = lax.dynamic_slice(current, (0, row, col), (current.shape[0], length, length))
        return lax.dynamic_update_slice(current, old_part + pieces[index], (0, row, col))

    return lax.fori_loop(0, pieces.shape[0], add_one, frame)


def shards(object_field, probe, amplitudes, positions, counts):
    strip_rows = object_field.shape[1]
    columns = object_field.shape[2]
    length = probe.shape[-1]
    nmodes = probe.shape[1]
    slots = amplitudes.shape[0]
    device = lax.axis_index("dev")
    row_local = positions[:, 0] - device * strip_rows
    col_local = positions[:, 1]
    live = (jnp.arange(slots, dtype=jnp.int32) < counts[0]).astype(jnp.float32)
    cosine, sine = tables(length)
    current = object_field
    for step in range(ITERS):
        below = from_behind(current, "dev", -1)
        extended = jnp.concatenate([current, below], axis=1)
        patches = cut_windows(extended, row_local, col_local, length)
        gradients, probe_terms = window_terms(patches, amplitudes, live, probe, cosine, sine)
        empty = jnp.zeros((3, strip_rows + length, columns), jnp.float32)
        accumulated = place_windows(empty, gradients, row_local, col_local)
        incoming = from_behind(accumulated[:, strip_rows:], "dev", 1)
        total = accumulated[:, :strip_rows].at[:, :length].add(incoming)
        new_current = current - total[:2] / (total[2] + 1.0)[None]
        summed = lax.psum(probe_terms, "dev")
        grad_modes = summed[: 2 * nmodes].reshape(2, nmodes, length, length)
        probe = probe - grad_modes / (summed[2 * nmodes] + 1.0)[None, None]
        current = new_current
    return (current, probe)


def solution(mesh):
    placed = (P(None, "dev", None), P(), P("dev", None, None), P("dev", None), P("dev"))
    return jax.shard_map(
        shards, mesh=mesh, in_specs=placed, out_specs=(P(None, "dev", None), P()), check_vma=False
    )
```

profile of v0, /device:TPU:1, one launch (start us, length us, event | category | flops | bytes accessed | tf_op | source)
XLA Modules:
  0.0 1128.9 jit_solution(9020664435228499280)
XLA Ops:
  15.4 20.9 %collective-permute-done = f32[2,128,2048]{2,1,0:T(8,128)} collective-permute-done((f32[2,128,2048]{2,1,0:T(8,128)}, f32[2,128,2048]{2,1,0:T(8,128)}, u32[]{:S(2)}, u32[]{:S(2)}) %collective-permute-start) | collective-permute-done | bytes 2097184 | tf_op jit(solution)/shard_map/ppermute | solution.py:17
  40.2 57.5 %while.34 = (s32[]{:T(128)}, f32[2,256,2048]{2,1,0:T(8,128)}, s32[16,3]{0,1:T(4,128)S(1)}, f32[16,2,128,128]{3,2,0,1:T(8,128)}, s32[]{:T(128)}) while((s32[]{:T(128)}, f32[2,256,2048]{2,1,0:T(8,128)}, s32[16,3]{0,1:T(4,128)S(1)}, f32[16,2,128,128]{3,2,0,1:T(8,128)}, s32[]{:T(128)}) %tuple.114), condition=%wide.while_cond.2, body=%wide.while_body.2.sunk | while | flops 2 | bytes 263785 | solution.py:79
  106.7 7.6 fusion.36
  114.3 7.2 fusion.125
  135.5 7.6 fusion.124
  143.0 7.5 fusion.56
  150.6 7.2 add_reduce_fusion.5
  158.1 7.4 fusion.50
  165.5 7.2 fusion.48
  172.6 7.6 fusion.83
  180.2 7.3 fusion.18
  194.3 7.4 fusion.80
  208.6 11.3 %add_reduce_fusion.3 = (f32[4,128,128]{2,1,0:T(8,128)}, f32[4,128,128]{2,1,0:T(8,128)}, f32[16,128,128]{2,1,0:T(8,128)S(1)}, f32[16,128,128]{2,1,0:T(8,128)S(1)}) fusion(f32[16,4,128,128]{3,2,1,0:T(8,128)S(1)} %fusion.62, f32[16,128,128]{2,1,0:T(8,128)S(1)} %get-tuple-element.303, f32[16,128,128]{2,1,0:T(8,128)S(1)} %get-tuple-element.302, ...), kind=kOutput, calls=%fused_computation.52 | convolution fusion | flops 1628061696 | bytes 17825792 | tf_op jit(solution)/shard_map/...ab,bc->...ac/dot_general | solution.py:41
  223.6 156.3 %while.32 = (s32[]{:T(128)}, f32[3,256,2048]{2,1,0:T(8,128)}, s32[16]{0:T(128)S(1)}, s32[16]{0:T(128)S(1)}, f32[16,3,128,128]{3,2,1,0:T(8,128)S(1)}, /*index=5*/s32[]{:T(128)}, s32[]{:T(128)}, s32[]{:T(128)}, s32[]{:T(128)}) while((s32[]{:T(128)}, f32[3,256,2048]{2,1,0:T(8,128)}, s32[16]{0:T(128)S(1)}, s32[16]{0:T(128)S(1)}, ...), condition=%wide.region_5.6_spmd, body=%wide.region_4.5_spmd.sunk | while | flops 49160 | bytes 983241 | solution.py:93
  384.4 34.2 %collective-permute-done.1 = f32[3,128,2048]{2,1,0:T(8,128)S(1)} collective-permute-done((f32[3,128,2048]{2,1,0:T(8,128)S(1)}, f32[3,128,2048]{2,1,0:T(8,128)S(1)}, u32[]{:S(2)}, u32[]{:S(2)}) %collective-permute-start.1) | collective-permute-done | bytes 3145760 | tf_op jit(solution)/shard_map/ppermute | solution.py:17
  421.8 26.3 %collective-permute-done.2 = f32[2,128,2048]{2,1,0:T(8,128)} collective-permute-done((f32[2,128,2048]{2,1,0:T(8,128)S(1)}, f32[2,128,2048]{2,1,0:T(8,128)}, u32[]{:S(2)}, u32[]{:S(2)}) %collective-permute-start.2) | collective-permute-done | bytes 2097184 | tf_op jit(solution)/shard_map/ppermute | solution.py:17
  452.0 56.2 %while.35 = (s32[]{:T(128)}, f32[2,256,2048]{2,1,0:T(8,128)}, s32[16,3]{0,1:T(4,128)S(1)}, f32[16,2,128,128]{3,2,1,0:T(8,128)}, s32[]{:T(128)}) while((s32[]{:T(128)}, f32[2,256,2048]{2,1,0:T(8,128)}, s32[16,3]{0,1:T(4,128)S(1)}, f32[16,2,128,128]{3,2,1,0:T(8,128)}, s32[]{:T(128)}) %tuple.130), condition=%wide.while_cond.3, body=%wide.while_body.3.sunk | while | flops 2 | bytes 263785 | solution.py:79
  514.8 151.7 %all-reduce.3.cloned.1.call-done = f32[9,128,128]{2,1,0:T(8,128)} async-done(((f32[9,128,128]{2,1,0:T(8,128)}), f32[9,128,128]{2,1,0:T(8,128)}) %all-reduce.3.cloned.1.call-update) | async-done | bytes 589840 | tf_op jit(solution)/shard_map/psum | solution.py:118
  668.5 7.4 fusion.33
  675.9 7.7 fusion.32
  683.6 7.4 fusion.103
  698.1 7.3 fusion.8
  705.4 7.6 fusion.102
  713.0 7.3 fusion.68
  720.3 7.2 add_reduce_fusion.2
  727.8 7.4 fusion.42
  735.3 7.2 fusion.40
  742.4 7.8 fusion.89
  764.1 7.4 fusion.86
  778.5 10.5 add_reduce_fusion
  794.6 164.4 %while.33 = (s32[]{:T(128)}, f32[3,256,2048]{2,1,0:T(8,128)}, s32[16]{0:T(128)S(1)}, s32[16]{0:T(128)S(1)}, f32[16,3,128,128]{3,2,1,0:T(8,128)}, /*index=5*/s32[]{:T(128)}, s32[]{:T(128)}, s32[]{:T(128)}, s32[]{:T(128)}) while((s32[]{:T(128)}, f32[3,256,2048]{2,1,0:T(8,128)}, s32[16]{0:T(128)S(1)}, s32[16]{0:T(128)S(1)}, ...), condition=%wide.region_15.16_spmd, body=%wide.region_14.15_spmd.sunk | while | flops 49160 | bytes 983241 | solution.py:93
  966.1 147.1 %all-reduce.5.cloned.1.call-done = f32[9,128,128]{2,1,0:T(8,128)} async-done(((f32[9,128,128]{2,1,0:T(8,128)}), f32[9,128,128]{2,1,0:T(8,128)}) %all-reduce.5.cloned.1.call-update) | async-done | bytes 589840 | tf_op jit(solution)/shard_map/psum | solution.py:118
  (304 shorter events, 437.6 us)
Async XLA Ops:
  7.2 29.2 %copy-start.3 = (f32[2,128,2048]{2,1,0:T(8,128)S(1)}, f32[2,128,2048]{2,1,0:T(8,128)}, u32[]{:S(2)}) copy-start(f32[2,128,2048]{2,1,0:T(8,128)} %param.17) | copy-start | bytes 6291460
  7.2 659.3 %all-reduce.3.cloned.1.call-start = ((), (), s32[]{:S(2)}) async-start(), calls=%async_computation | async-start | bytes 1179648 | tf_op jit(solution)/shard_map/psum | solution.py:118
  7.2 29.1 %collective-permute-start = (f32[2,128,2048]{2,1,0:T(8,128)}, f32[2,128,2048]{2,1,0:T(8,128)}, u32[]{:S(2)}, u32[]{:S(2)}) collective-permute-start(f32[2,128,2048]{2,1,0:T(8,128)} %param.17), channel_id=1, source_target_pairs={{1,0},{2,1},{3,2},{4,3},{5,4},{6,5},{7,6},{8,7},{9,8},{10,9},{11,1... | collective-permute-start | bytes 6291464 | tf_op jit(solution)/shard_map/ppermute | solution.py:17
  150.5 7.3 copy-start.6
  208.6 11.4 %copy-start.8 = (f32[16,1,128,128]{3,2,1,0:T(8,128)S(1)}, f32[16,1,128,128]{3,2,1,0:T(8,128)}, u32[]{:S(2)}) copy-start(f32[16,1,128,128]{3,2,1,0:T(8,128)} %broadcast_multiply_fusion.1) | copy-start | bytes 3145732
  379.9 38.6 %copy-start = (f32[3,256,2048]{2,1,0:T(8,128)S(1)}, f32[3,256,2048]{2,1,0:T(8,128)}, u32[]{:S(2)}) copy-start(f32[3,256,2048]{2,1,0:T(8,128)} %get-tuple-element.230) | copy-start | bytes 18874372
  382.2 37.2 %copy-start.4 = (f32[2,128,2048]{2,1,0:T(8,128)S(1)}, f32[2,128,2048]{2,1,0:T(8,128)}, u32[]{:S(2)}) copy-start(f32[2,128,2048]{2,1,0:T(8,128)} %param.17) | copy-start | bytes 6291460
  382.2 36.4 %collective-permute-start.1 = (f32[3,128,2048]{2,1,0:T(8,128)S(1)}, f32[3,128,2048]{2,1,0:T(8,128)S(1)}, u32[]{:S(2)}, u32[]{:S(2)}) collective-permute-start(f32[3,128,2048]{2,1,0:T(8,128)S(1)} %slice.127), channel_id=1, source_target_pairs={{0,1},{1,2},{2,3},{3,4},{4,5},{5,6},{6,7},{7,8},{8,9},{9,10},{10,1... | collective-permute-start | bytes 9437192 | tf_op jit(solution)/shard_map/ppermute | solution.py:17
  419.8 32.1 %copy-start.1 = (f32[2,128,2048]{2,1,0:T(8,128)}, f32[2,128,2048]{2,1,0:T(8,128)S(1)}, u32[]{:S(2)}) copy-start(f32[2,128,2048]{2,1,0:T(8,128)S(1)} %fusion.93) | copy-start | bytes 6291460
  419.8 28.2 %collective-permute-start.2 = (f32[2,128,2048]{2,1,0:T(8,128)S(1)}, f32[2,128,2048]{2,1,0:T(8,128)}, u32[]{:S(2)}, u32[]{:S(2)}) collective-permute-start(f32[2,128,2048]{2,1,0:T(8,128)S(1)} %fusion.93), channel_id=1, source_target_pairs={{1,0},{2,1},{3,2},{4,3},{5,4},{6,5},{7,6},{8,7},{9,8},{10,9},{11,1... | collective-permute-start | bytes 6291464 | tf_op jit(solution)/shard_map/ppermute | solution.py:17
  451.9 58.9 %copy-start.9 = (f32[4,128,128]{2,1,0:T(8,128)S(1)}, f32[4,128,128]{2,1,0:T(8,128)}, u32[]{:S(2)}) copy-start(f32[4,128,128]{2,1,0:T(8,128)} %get-tuple-element.250) | copy-start | bytes 786436
  451.9 58.9 %copy-start.10 = (f32[4,128,128]{2,1,0:T(8,128)S(1)}, f32[4,128,128]{2,1,0:T(8,128)}, u32[]{:S(2)}) copy-start(f32[4,128,128]{2,1,0:T(8,128)} %get-tuple-element.251) | copy-start | bytes 786436
  510.8 157.6 %copy-start.5 = (f32[2,4,128,128]{3,2,1,0:T(8,128)S(1)}, f32[2,4,128,128]{3,2,1,0:T(8,128)}, u32[]{:S(2)}) copy-start(f32[2,4,128,128]{3,2,1,0:T(8,128)} %param.18) | copy-start | bytes 1572868
  511.7 601.5 %all-reduce.5.cloned.1.call-start = ((), (), s32[]{:S(2)}) async-start(), calls=%async_computation.1 | async-start | bytes 1179648 | tf_op jit(solution)/shard_map/psum | solution.py:118
  720.3 7.3 copy-start.7
  962.9 153.1 %collective-permute-start.3 = (f32[3,128,2048]{2,1,0:T(8,128)}, f32[3,128,2048]{2,1,0:T(8,128)}, u32[]{:S(2)}, u32[]{:S(2)}) collective-permute-start(f32[3,128,2048]{2,1,0:T(8,128)} %slice.137), channel_id=1, source_target_pairs={{0,1},{1,2},{2,3},{3,4},{4,5},{5,6},{6,7},{7,8},{8,9},{9,10},{10,1... | collective-permute-start | bytes 9437192 | tf_op jit(solution)/shard_map/ppermute | solution.py:17
  1116.0 3.8 copy-start.2
Sparse Core Ops, SparseCore 0:
  511.9 154.5 all-reduce.2
  966.2 146.9 all-reduce.4
where the time goes:
time: 1150 us; the launch traced here: 1130 us
  waiting for transfers between devices  380 us (33%)
  local copies, waits for them, and re-layouts  299 us (26%)
  matrix products  240 us (21%)
  loops' own time  118 us (10%)
  other arithmetic  65.9 us (6%)
  between operations  15.7 us (1%)
    psum x2, waiting for transfers between devices, shards(): summed = lax.psum(probe_terms, 'dev')  299 us
    dynamic_update_slice x32, local copies, waits for them, and re-layouts, add_one(): lax.dynamic_update_slice(current, old_part + pieces[index], (0, row, col))  127 us
    another operation x2, loops' own time, place_windows(): return lax.fori_loop(0, pieces.shape[0], add_one, frame)  118 us
    gather x96, local copies, waits for them, and re-layouts  114 us
    ppermute x4, waiting for transfers between devices, from_behind(): lax.ppermute(value, axis, [(source, source + steps) for source in range(l...  81.3 us
    add x32, other arithmetic, add_one(): old_part + pieces[index]  38.4 us
    dot_general x4, matrix products, right_product(): real_sin = jnp.einsum('...ab,bc->...ac', real, sine, precision=best)  36.4 us
    dot_general x4, matrix products, left_product(): sin_real = jnp.einsum('ab,...bc->...ac', sine, real, precision=best)  30 us
  transfers between devices with their start and end apart: 6, of which 5 were waited for; matrix products, arithmetic and copies ran while one was open for 1% of the time, Pallas kernels for 0%

commit v1 on v0

v1 whole, which is shorter than its diff:
```python
import functools

import jax
import jax.numpy as jnp
import ml_dtypes
import numpy as np
from jax import lax
from jax.experimental import pallas as pl
from jax.experimental.pallas import tpu as pltpu
from jax.sharding import PartitionSpec as P

ITERS = 2
SIGMA = 0.5
VMEM_LIMIT = 50 * 1024 * 1024


def split_np(w):
    hi = w.astype(ml_dtypes.bfloat16)
    lo = (w - hi.astype(np.float64)).astype(ml_dtypes.bfloat16)
    return hi, lo


def dft_blocks(length):
    index = np.arange(length)
    angle = 2.0 * np.pi * ((index[:, None] * index[None, :]) % length) / length
    c = np.cos(angle) / np.sqrt(length)
    s = np.sin(angle) / np.sqrt(length)
    minus = np.block([[c, -s], [s, c]])
    plus = np.block([[c, s], [-s, c]])
    return minus, plus


def split(x):
    hi = x.astype(jnp.bfloat16)
    lo = (x - hi.astype(jnp.float32)).astype(jnp.bfloat16)
    return hi, lo


def dot(a, b):
    return lax.dot_general(a, b, (((1,), (0,)), ((), ())), preferred_element_type=jnp.float32)


def right_product(x, w_ref):
    hi, lo = split(x)
    return dot(jnp.concatenate([hi, lo, hi], axis=1), w_ref[...])


def left_product(w_ref, x):
    hi, lo = split(x)
    return dot(w_ref[...], jnp.concatenate([hi, hi, lo], axis=0))


def pattern_kernel(
    rows_ref, cols_ref, count_ref, own_ref, below_ref, probe_ref, amp_ref,
    rf_ref, rb_ref, lf_ref, lb_ref,
    gown_ref, gover_ref, terms_ref,
    frame, grad,
):
    strip = own_ref.shape[1]
    columns = own_ref.shape[2]
    nmodes, length = probe_ref.shape[1], probe_ref.shape[2]
    for t in range(columns // 128):
        frame[:, t, :strip, :] = own_ref[:, :, t * 128 : (t + 1) * 128]
        frame[:, t, strip:, :] = below_ref[:, :, t * 128 : (t + 1) * 128]
    grad[...] = jnp.zeros_like(grad)
    terms_ref[...] = jnp.zeros_like(terms_ref)
    count = count_ref[0]

    def one(slot):
        alive = (slot < count).astype(jnp.float32)
        row = rows_ref[slot]
        col = cols_ref[slot]
        tile = jnp.minimum(col // 128, columns // 128 - 2)
        shift = col - tile * 128
        back = lax.rem(256 - shift, 256)

        def cut(part):
            wide = jnp.concatenate([frame[part, tile + k, pl.ds(row, length), :] for k in range(2)], axis=1)
            return pltpu.roll(wide, back, 1)[:, :length]

        xr, xi = cut(0), cut(1)
        waves = []
        for m in range(nmodes):
            pr, pi = probe_ref[0, m], probe_ref[1, m]
            waves.append(jnp.concatenate([pr * xr - pi * xi, pr * xi + pi * xr], axis=1))
        mids = [right_product(w, rf_ref) for w in waves]
        cols_in = jnp.concatenate(
            [jnp.concatenate([y[:, :length], y[:, length:]], axis=0) for y in mids], axis=1
        )
        far = left_product(lf_ref, cols_in)
        sq = far * far
        power = sq[:length] + sq[length:]
        intensity = functools.reduce(
            lambda a, b: a + b, [power[:, m * length : (m + 1) * length] for m in range(nmodes)]
        )
        weight = (1.0 - amp_ref[slot] * lax.rsqrt(intensity + SIGMA)) * alive
        weight = jnp.concatenate([weight] * nmodes, axis=1)
        weight = jnp.concatenate([weight, weight], axis=0)
        back_mid = left_product(lb_ref, far * weight)
        gr = gi = None
        for m in range(nmodes):
            piece = back_mid[:, m * length : (m + 1) * length]
            chi = right_product(jnp.concatenate([piece[:length], piece[length:]], axis=1), rb_ref)
            cr, ci = chi[:, :length], chi[:, length:]
            pr, pi = probe_ref[0, m], probe_ref[1, m]
            a = pr * cr + pi * ci
            b = pr * ci - pi * cr
            gr = a if gr is None else gr + a
            gi = b if gi is None else gi + b
            terms_ref[m] += xr * cr + xi * ci
            terms_ref[nmodes + m] += xr * ci - xi * cr
        terms_ref[2 * nmodes] += (xr * xr + xi * xi) * alive
        pad = jnp.zeros_like(gr)
        for part, g in enumerate((gr, gi)):
            wide = pltpu.roll(jnp.concatenate([g, pad], axis=1), shift, 1)
            for k in range(2):
                grad[part, tile + k, pl.ds(row, length), :] += wide[:, k * 128 : (k + 1) * 128]

    def step(index, carry):
        one(index)
        return carry

    lax.fori_loop(0, count, step, 0)
    for t in range(columns // 128):
        gown_ref[:, :, t * 128 : (t + 1) * 128] = grad[:, t, :strip, :]
        gover_ref[:, :, t * 128 : (t + 1) * 128] = grad[:, t, strip:, :]


def vmem():
    return pl.BlockSpec(memory_space=pltpu.VMEM)


def smem():
    return pl.BlockSpec(memory_space=pltpu.SMEM)


def patterns(rows, cols, count, own, below, probe, amps):
    length, nmodes = probe.shape[-1], probe.shape[1]
    strip, columns = own.shape[1:]
    minus, plus = dft_blocks(length)
    mh, ml = split_np(minus)
    ph, plo = split_np(plus)
    rf = np.concatenate([mh, mh, ml], axis=0)
    rb = np.concatenate([ph, ph, plo], axis=0)
    lf = np.concatenate([ph, plo, ph], axis=1)
    lb = np.concatenate([mh, ml, mh], axis=1)
    slots = amps.shape[0]
    macs = slots * nmodes * 4 * length * 3 * 4 * length * length
    return pl.pallas_call(
        pattern_kernel,
        out_shape=(
            jax.ShapeDtypeStruct((2, strip, columns), jnp.float32),
            jax.ShapeDtypeStruct((2, strip, columns), jnp.float32),
            jax.ShapeDtypeStruct((2 * nmodes + 1, length, length), jnp.float32),
        ),
        in_specs=[smem()] * 3 + [vmem()] * 8,
        out_specs=(vmem(), vmem(), vmem()),
        scratch_shapes=[
            pltpu.VMEM((2, columns // 128, 2 * strip, 128), jnp.float32),
            pltpu.VMEM((2, columns // 128, 2 * strip, 128), jnp.float32),
        ],
        compiler_params=pltpu.CompilerParams(vmem_limit_bytes=VMEM_LIMIT),
        cost_estimate=pl.CostEstimate(flops=2 * macs, bytes_accessed=8 * 1024 * 1024, transcendentals=0),
        name="patterns",
    )(rows, cols, count, own, below, probe, amps, *map(jnp.asarray, (rf, rb, lf, lb)))


def light_kernel(nsets, strip, scal_ref, probe_ref, out_ref, acc):
    nmodes, length = probe_ref.shape[1], probe_ref.shape[2]
    tiles = acc.shape[0]
    acc[...] = jnp.zeros_like(acc)
    power = None
    for m in range(nmodes):
        term = probe_ref[0, m] * probe_ref[0, m] + probe_ref[1, m] * probe_ref[1, m]
        power = term if power is None else power + term
    wide0 = jnp.concatenate([power, jnp.zeros_like(power)], axis=1)
    for s in range(nsets):

        def step(slot, carry, s=s):
            row = scal_ref[s, slot] + s * strip
            col = scal_ref[s, 16 + slot]
            tile = jnp.minimum(col // 128, tiles - 2)
            wide = pltpu.roll(wide0, col - tile * 128, 1)
            for k in range(2):
                acc[tile + k, pl.ds(row, length), :] += wide[:, k * 128 : (k + 1) * 128]
            return carry

        lax.fori_loop(0, scal_ref[s, 32], step, 0)
    for s in range(nsets - 1):
        for t in range(tiles):
            out_ref[s, :, t * 128 : (t + 1) * 128] = acc[t, (s + 1) * strip : (s + 2) * strip, :]


def light(scalars, probe, strip, columns):
    nsets = scalars.shape[0]
    return pl.pallas_call(
        functools.partial(light_kernel, nsets, strip),
        out_shape=jax.ShapeDtypeStruct((nsets - 1, strip, columns), jnp.float32),
        in_specs=[smem(), vmem()],
        out_specs=vmem(),
        scratch_shapes=[pltpu.VMEM((columns // 128, (nsets + 1) * strip, 128), jnp.float32)],
        compiler_params=pltpu.CompilerParams(vmem_limit_bytes=VMEM_LIMIT),
        cost_estimate=pl.CostEstimate(flops=16 * nsets * 40000, bytes_accessed=4 * 1024 * 1024, transcendentals=0),
        name="light",
    )(scalars, probe)


def shift_by(value, steps):
    count = lax.axis_size("dev")
    return lax.ppermute(
        value, "dev", [(i, i + steps) for i in range(count) if 0 <= i + steps < count]
    )


def rotate(value, stride, extent, steps):
    count = lax.axis_size("dev")

    def target(i):
        z = (i // stride) % extent
        return i + ((z + steps) % extent - z) * stride

    return lax.ppermute(value, "dev", [(i, target(i)) for i in range(count)])


def ring_scatter(value, stride, extent):
    place = (lax.axis_index("dev") // stride) % extent
    total = lax.dynamic_index_in_dim(value, place, 0, keepdims=False)
    for k in range(1, extent):
        piece = lax.dynamic_index_in_dim(value, lax.rem(place + k, extent), 0, keepdims=False)
        total = total + rotate(piece, stride, extent, k)
    return total


def ring_sum(value, stride, extent):
    total = value
    for k in range(1, extent):
        total = total + rotate(value, stride, extent, k)
    return total


def ring_gather(value, stride, extent):
    place = (lax.axis_index("dev") // stride) % extent
    out = jnp.zeros((extent,) + value.shape, value.dtype)
    out = lax.dynamic_update_index_in_dim(out, value, place, 0)
    for k in range(1, extent):
        got = rotate(value, stride, extent, k)
        out = lax.dynamic_update_index_in_dim(out, got, lax.rem(place + extent - k, extent), 0)
    return out


def sum_all(terms):
    shape = terms.shape
    flat = terms.reshape(2, -1, 128)
    flat = ring_scatter(flat, 1, 2)
    flat = ring_scatter(flat.reshape(4, -1, 128), 2, 4)
    flat = ring_sum(flat, 8, 4)
    flat = ring_sum(flat, 32, 4)
    flat = ring_gather(flat, 2, 4).reshape(-1, 128)
    return ring_gather(flat, 1, 2).reshape(shape)


def shards(object_field, probe, amplitudes, positions, counts):
    strip, columns = object_field.shape[1:]
    nmodes, length = probe.shape[1], probe.shape[-1]
    device = lax.axis_index("dev")
    rows = positions[:, 0] - device * strip
    cols = positions[:, 1]
    mine = jnp.concatenate([rows, cols, counts])
    current = object_field
    below = shift_by(current, -1)
    prev = shift_by(mine, 1)
    following = shift_by(mine, -1)
    lit = light(jnp.stack([prev, mine, following]), probe, strip, columns)

    def new_probe(terms):
        summed = sum_all(terms)
        grad = summed[: 2 * nmodes].reshape(2, nmodes, length, length)
        return probe - grad / (summed[2 * nmodes] + 1.0)[None, None]

    gown, gover, terms = patterns(rows, cols, counts, current, below, probe, amplitudes)
    from_above = shift_by(gover, 1)
    from_below = shift_by(gown, -1)
    probe = new_probe(terms)
    current = current - (gown + from_above) / (lit[0] + 1.0)[None]
    below = below - (gover + from_below) / (lit[1] + 1.0)[None]

    gown, gover, terms = patterns(rows, cols, counts, current, below, probe, amplitudes)
    from_above = shift_by(gover, 1)
    lit = light(jnp.stack([prev, mine]), probe, strip, columns)
    probe = new_probe(terms)
    current = current - (gown + from_above) / (lit[0] + 1.0)[None]
    return (current, probe)


def solution(mesh):
    placed = (P(None, "dev", None), P(), P("dev", None, None), P("dev", None), P("dev"))
    return jax.shard_map(
        shards, mesh=mesh, in_specs=placed, out_specs=(P(None, "dev", None), P()), check_vma=False
    )
```

time: 1150 us -> 239 us (0.21); the launches traced: 1130 us -> 239 us
  waiting for transfers between devices: 380 us -> 87 us
  local copies, waits for them, and re-layouts: 299 us -> 8.2 us
  matrix products: 240 us -> 0 us
  loops' own time: 118 us -> 0 us
  starting transfers between devices: 10.4 us -> 105 us
  other arithmetic: 65.9 us -> 11.8 us
  Pallas kernels: 0 us -> 24.7 us
  between operations: 15.7 us -> 1.79 us
    psum x2 -> x0, waiting for transfers between devices: 299 us -> none  [shards(): summed = lax.psum(probe_terms, 'dev')]
    dot_general x32 -> x0, matrix products: 240 us -> none  [the longest x4 36.4 us: right_product(): real_sin = jnp.einsum('...ab,bc->...ac', real, sine, precision=best)]
    dynamic_update_slice x32 -> x10, local copies, waits for them, and re-layouts: 127 us -> 0.16 us  [the longest x8 0.11 us: ring_gather(): lax.dynamic_update_index_in_dim(out, got, lax.rem(place + extent - k, ext...]
    another operation x4 -> x0, loops' own time: 118 us -> none  [the longest x2 118 us: place_windows(): return lax.fori_loop(0, pieces.shape[0], add_one, frame)]
    gather x96 -> x0, local copies, waits for them, and re-layouts: 114 us -> none
    ppermute x4 -> x34, starting transfers between devices: 9.87 us -> 105 us  [the longest x28 84.7 us: rotate(): return lax.ppermute(value, 'dev', [(i, target(i)) for i in range(count)])]
    add x36 -> x8, other arithmetic: 44.4 us -> 1.12 us  [the longest x4 1.06 us: ring_scatter(): total = total + rotate(piece, stride, extent, k)]
    dynamic_slice x64 -> x0, local copies, waits for them, and re-layouts: 37.7 us -> none  [the longest x32 19 us: add_one(): row = rows[index]]
  transfers between devices with their start and end apart: 6 -> 34, of which waited for: 5 -> 15; matrix products, arithmetic and copies ran while one was open for 1% -> 3% of each run, Pallas kernels for 0% -> 3%
where the time goes in v1:
time: 239 us
  starting transfers between devices  105 us (44%)
  waiting for transfers between devices  87 us (36%)
  Pallas kernels  24.7 us (10%)
  other arithmetic  11.8 us (5%)
  local copies, waits for them, and re-layouts  8.2 us (3%)
    ppermute x28, starting transfers between devices, rotate(): return lax.ppermute(value, 'dev', [(i, target(i)) for i in range(count)])  84.7 us
    ppermute x28, waiting for transfers between devices, rotate(): return lax.ppermute(value, 'dev', [(i, target(i)) for i in range(count)])  62.9 us
    ppermute x6, waiting for transfers between devices, shift_by(): lax.ppermute(value, 'dev', [(i, i + steps) for i in range(count) if 0 <=...  24.1 us
    ppermute x6, starting transfers between devices, shift_by(): lax.ppermute(value, 'dev', [(i, i + steps) for i in range(count) if 0 <=...  20.3 us
    pallas_call x2, Pallas kernels, patterns(): pl.pallas_call(pattern_kernel, out_shape=(jax.ShapeDtypeStruct((2, strip,...  17.5 us
    unnamed x38, local copies, waits for them, and re-layouts  7.76 us
    pallas_call x2, Pallas kernels, light(): pl.pallas_call(functools.partial(light_kernel, nsets, strip), out_shape=j...  7.12 us
  transfers between devices with their start and end apart: 34, of which 15 were waited for; matrix products, arithmetic and copies ran while one was open for 3% of the time, Pallas kernels for 3%

profile of v1, /device:TPU:1, one launch (start us, length us, event | category | flops | bytes accessed | tf_op | source)
XLA Modules:
  0.0 238.5 jit_solution(60094879988009636)
XLA Ops:
  0.6 3.3 %collective-permute-start = (f32[2,128,2048]{2,1,0:T(8,128)}, f32[2,128,2048]{2,1,0:T(8,128)S(1)}, u32[]{:S(2)}, u32[]{:S(2)}) collective-permute-start(f32[2,128,2048]{2,1,0:T(8,128)} %own_ref.1), channel_id=1, source_target_pairs={{1,0},{2,1},{3,2},{4,3},{5,4},{6,5},{7,6},{8,7},{9,8},{10,9},{11,1... | collective-permute-start | bytes 6291464 | tf_op jit(solution)/shard_map/ppermute | solution.py:210
  5.4 24.1 %collective-permute-done.below_ref = f32[2,128,2048]{2,1,0:T(8,128)S(1)} collective-permute-done((f32[2,128,2048]{2,1,0:T(8,128)}, f32[2,128,2048]{2,1,0:T(8,128)S(1)}, u32[]{:S(2)}, u32[]{:S(2)}) %collective-permute-start) | collective-permute-done | bytes 2097184 | tf_op jit(solution)/shard_map/ppermute | solution.py:210
  37.1 8.7 %patterns.2 = (f32[2,128,2048]{2,1,0:T(8,128)}, f32[2,128,2048]{2,1,0:T(8,128)}, f32[9,128,128]{2,1,0:T(8,128)S(1)}) custom-call(s32[16]{0:T(128)S(1)} %get-tuple-element.27.rows_ref, s32[16]{0:T(128)S(1)} %get-tuple-element.26.cols_ref, s32[1]{0:T(128)S(6)} %copy.27.count_ref, f32[2,128,2048]{2,1,0:T(8,128)} %own_ref.1, f32[2,128,2048]{2,1,0:T(8,128)} %copy-done.14, ...), custom_call_target="tpu_custom_call" | custom-call | flops 12884901888 | bytes 8388608 | tf_op jit(solution)/shard_map/patterns/pallas_call | solution.py:149
  50.1 13.4 %collective-permute-start.6 = (f32[144,128]{1,0:T(8,128)S(1)}, f32[144,128]{1,0:T(8,128)S(1)}, u32[]{:S(2)}, u32[]{:S(2)}) collective-permute-start(f32[144,128]{1,0:T(8,128)S(1)} %get-tuple-element.23), channel_id=1, source_target_pairs={{0,2},{1,3},{2,4},{3,5},{4,6},{5,7},{6,0},{7,1},{8,10},{9,11},{10,... | collective-permute-start | bytes 221192 | tf_op jit(solution)/shard_map/ppermute | solution.py:222
  63.5 2.5 %collective-permute-start.8 = (f32[144,128]{1,0:T(8,128)S(1)}, f32[144,128]{1,0:T(8,128)S(1)}, u32[]{:S(2)}, u32[]{:S(2)}) collective-permute-start(f32[144,128]{1,0:T(8,128)S(1)} %get-tuple-element.24), channel_id=1, source_target_pairs={{0,6},{1,7},{2,0},{3,1},{4,2},{5,3},{6,4},{7,5},{8,14},{9,15},{10,... | collective-permute-start | bytes 221192 | tf_op jit(solution)/shard_map/ppermute | solution.py:222
  66.0 2.2 collective-permute-done.7
  68.2 11.2 %collective-permute-start.10 = (f32[144,128]{1,0:T(8,128)S(1)}, f32[144,128]{1,0:T(8,128)S(1)}, u32[]{:S(2)}, u32[]{:S(2)}) collective-permute-start(f32[144,128]{1,0:T(8,128)S(1)} %fusion.5), channel_id=1, source_target_pairs={{0,16},{1,17},{2,18},{3,19},{4,20},{5,21},{6,22},{7,23},{8,24},{9,... | collective-permute-start | bytes 221192 | tf_op jit(solution)/shard_map/ppermute | solution.py:222
  79.5 2.5 %collective-permute-start.11 = (f32[144,128]{1,0:T(8,128)S(1)}, f32[144,128]{1,0:T(8,128)S(1)}, u32[]{:S(2)}, u32[]{:S(2)}) collective-permute-start(f32[144,128]{1,0:T(8,128)S(1)} %fusion.5), channel_id=1, source_target_pairs={{0,24},{1,25},{2,26},{3,27},{4,28},{5,29},{6,30},{7,31},{8,0},{9,1... | collective-permute-start | bytes 221192 | tf_op jit(solution)/shard_map/ppermute | solution.py:222
  81.9 2.4 %collective-permute-done.11 = f32[144,128]{1,0:T(8,128)S(1)} collective-permute-done((f32[144,128]{1,0:T(8,128)S(1)}, f32[144,128]{1,0:T(8,128)S(1)}, u32[]{:S(2)}, u32[]{:S(2)}) %collective-permute-start.11) | collective-permute-done | bytes 73760 | tf_op jit(solution)/shard_map/ppermute | solution.py:222
  86.3 2.9 %collective-permute-start.12 = (f32[144,128]{1,0:T(8,128)S(1)}, f32[144,128]{1,0:T(8,128)S(1)}, u32[]{:S(2)}, u32[]{:S(2)}) collective-permute-start(f32[144,128]{1,0:T(8,128)S(1)} %add_add_fusion.3), channel_id=1, source_target_pairs={{0,32},{1,33},{2,34},{3,35},{4,36},{5,37},{6,38},{7,39},{8,40},{9,... | collective-permute-start | bytes 221192 | tf_op jit(solution)/shard_map/ppermute | solution.py:222
  90.8 2.0 collective-permute-start.14
  92.9 5.9 %collective-permute-start.2 = (s32[33]{0:T(128)S(1)}, s32[33]{0:T(128)S(1)}, u32[]{:S(2)}, u32[]{:S(2)}) collective-permute-start(s32[33]{0:T(128)S(1)} %pad_add_fusion.2), channel_id=1, source_target_pairs={{0,1},{1,2},{2,3},{3,4},{4,5},{5,6},{6,7},{7,8},{8,9},{9,10},{10,1... | collective-permute-start | bytes 404 | tf_op jit(solution)/shard_map/ppermute | solution.py:210
  104.6 4.2 %light.2 = f32[2,128,2048]{2,1,0:T(8,128)S(1)} custom-call(s32[3,33]{1,0:T(4,128)S(1)} %pad_add_fusion.scal_ref, f32[2,4,128,128]{3,2,1,0:T(8,128)S(1)} %copy-done.1), custom_call_target="tpu_custom_call" | custom-call | flops 1920000 | bytes 4194304 | tf_op jit(solution)/shard_map/light/pallas_call | solution.py:196
  110.8 2.1 collective-permute-start.16
  112.9 2.2 collective-permute-start.17
  115.1 22.9 %collective-permute-done.16 = f32[144,128]{1,0:T(8,128)S(1)} collective-permute-done((f32[144,128]{1,0:T(8,128)S(1)}, f32[144,128]{1,0:T(8,128)S(1)}, u32[]{:S(2)}, u32[]{:S(2)}) %collective-permute-start.16) | collective-permute-done | bytes 73760 | tf_op jit(solution)/shard_map/ppermute | solution.py:222
  140.0 4.4 %divide_subtract_fusion.1.below_ref = f32[2,128,2048]{2,1,0:T(8,128)} fusion(f32[2,128,2048]{2,1,0:T(8,128)S(1)} %copy-done.15, f32[2,128,2048]{2,1,0:T(8,128)} %get-tuple-element.9, f32[2,128,2048]{2,1,0:T(8,128)} %collective-permute-done.4, f32[128,2048]{1,0:T(8,128)S(1)} %get-tuple-element.18), kind=kLoop, calls=%fused_computation.1 | loop fusion | flops 1572864 | bytes 9437184 | tf_op jit(solution)/shard_map/sub | solution.py:285
  144.4 2.0 divide_subtract_fusion.2.own_ref
  146.5 8.8 %patterns.3 = (f32[2,128,2048]{2,1,0:T(8,128)}, f32[2,128,2048]{2,1,0:T(8,128)}, f32[9,128,128]{2,1,0:T(8,128)S(1)}) custom-call(s32[16]{0:T(128)S(1)} %get-tuple-element.27.rows_ref, s32[16]{0:T(128)S(1)} %get-tuple-element.26.cols_ref, s32[1]{0:T(128)S(6)} %copy.27.count_ref, f32[2,128,2048]{2,1,0:T(8,128)} %divide_subtract_fusion.2.own_ref, ...), custom_call_target="tpu_custom_call" | custom-call | flops 12884901888 | bytes 8388608 | tf_op jit(solution)/shard_map/patterns/pallas_call | solution.py:149
  155.4 23.3 %collective-permute-start.20 = (f32[576,128]{1,0:T(8,128)S(1)}, f32[576,128]{1,0:T(8,128)S(1)}, u32[]{:S(2)}, u32[]{:S(2)}) collective-permute-start(f32[576,128]{1,0:T(8,128)S(1)} %dynamic-slice_bitcast_fusion), channel_id=1, source_target_pairs={{0,1},{1,0},{2,3},{3,2},{4,5},{5,4},{6,7},{7,6},{8,9},{9,8},{10,11... | collective-permute-start | bytes 884744 | tf_op jit(solution)/shard_map/ppermute | solution.py:222
  180.1 2.6 %collective-permute-start.23 = (f32[144,128]{1,0:T(8,128)S(1)}, f32[144,128]{1,0:T(8,128)S(1)}, u32[]{:S(2)}, u32[]{:S(2)}) collective-permute-start(f32[144,128]{1,0:T(8,128)S(1)} %get-tuple-element.21), channel_id=1, source_target_pairs={{0,6},{1,7},{2,0},{3,1},{4,2},{5,3},{6,4},{7,5},{8,14},{9,15},{10,... | collective-permute-start | bytes 221192 | tf_op jit(solution)/shard_map/ppermute | solution.py:222
  182.7 3.9 %collective-permute-done.21 = f32[144,128]{1,0:T(8,128)S(1)} collective-permute-done((f32[144,128]{1,0:T(8,128)S(1)}, f32[144,128]{1,0:T(8,128)S(1)}, u32[]{:S(2)}, u32[]{:S(2)}) %collective-permute-start.21) | collective-permute-done | bytes 73760 | tf_op jit(solution)/shard_map/ppermute | solution.py:222
  191.2 2.1 collective-permute-done.25
  194.2 2.4 collective-permute-start.27
  196.5 2.5 %collective-permute-start.29 = (f32[144,128]{1,0:T(8,128)S(1)}, f32[144,128]{1,0:T(8,128)S(1)}, u32[]{:S(2)}, u32[]{:S(2)}) collective-permute-start(f32[144,128]{1,0:T(8,128)S(1)} %add_add_fusion.1), channel_id=1, source_target_pairs={{0,96},{1,97},{2,98},{3,99},{4,100},{5,101},{6,102},{7,103},{8,104... | collective-permute-start | bytes 221192 | tf_op jit(solution)/shard_map/ppermute | solution.py:222
  199.0 5.4 %collective-permute-start.19 = (f32[2,128,2048]{2,1,0:T(8,128)S(1)}, f32[2,128,2048]{2,1,0:T(8,128)S(1)}, u32[]{:S(2)}, u32[]{:S(2)}) collective-permute-start(f32[2,128,2048]{2,1,0:T(8,128)S(1)} %copy-done.18), channel_id=1, source_target_pairs={{0,1},{1,2},{2,3},{3,4},{4,5},{5,6},{6,7},{7,8},{8,9},{9,10},{10,1... | collective-permute-start | bytes 6291464 | tf_op jit(solution)/shard_map/ppermute | solution.py:210
  204.6 2.9 %light.3 = f32[1,128,2048]{2,1,0:T(8,128)S(1)} custom-call(s32[2,33]{1,0:T(2,128)S(1)} %pad_add_fusion.1.scal_ref, f32[2,4,128,128]{3,2,1,0:T(8,128)S(1)} %divide_subtract_fusion.4.probe_ref), custom_call_target="tpu_custom_call" | custom-call | flops 1280000 | bytes 4194304 | tf_op jit(solution)/shard_map/light/pallas_call | solution.py:196
  207.5 3.1 %collective-permute-start.31 = (f32[144,128]{1,0:T(8,128)S(1)}, f32[144,128]{1,0:T(8,128)S(1)}, u32[]{:S(2)}, u32[]{:S(2)}) collective-permute-start(f32[144,128]{1,0:T(8,128)S(1)} %get-tuple-element.15), channel_id=1, source_target_pairs={{0,4},{1,5},{2,6},{3,7},{4,0},{5,1},{6,2},{7,3},{8,12},{9,13},{10,... | collective-permute-start | bytes 221192 | tf_op jit(solution)/shard_map/ppermute | solution.py:222
  210.6 2.1 collective-permute-start.32
  212.7 17.0 %collective-permute-done.30 = f32[144,128]{1,0:T(8,128)S(1)} collective-permute-done((f32[144,128]{1,0:T(8,128)S(1)}, f32[144,128]{1,0:T(8,128)S(1)}, u32[]{:S(2)}, u32[]{:S(2)}) %collective-permute-start.30) | collective-permute-done | bytes 73760 | tf_op jit(solution)/shard_map/ppermute | solution.py:222
  229.7 4.1 %collective-permute-done.31 = f32[144,128]{1,0:T(8,128)S(1)} collective-permute-done((f32[144,128]{1,0:T(8,128)S(1)}, f32[144,128]{1,0:T(8,128)S(1)}, u32[]{:S(2)}, u32[]{:S(2)}) %collective-permute-start.31) | collective-permute-done | bytes 73760 | tf_op jit(solution)/shard_map/ppermute | solution.py:222
  236.5 2.0 divide_subtract_fusion
  (119 shorter events, 35.7 us)
Async XLA Ops:
  0.6 28.9 %collective-permute-start = (f32[2,128,2048]{2,1,0:T(8,128)}, f32[2,128,2048]{2,1,0:T(8,128)S(1)}, u32[]{:S(2)}, u32[]{:S(2)}) collective-permute-start(f32[2,128,2048]{2,1,0:T(8,128)} %own_ref.1), channel_id=1, source_target_pairs={{1,0},{2,1},{3,2},{4,3},{5,4},{6,5},{7,6},{8,7},{9,8},{10,9},{11,1... | collective-permute-start | bytes 6291464 | tf_op jit(solution)/shard_map/ppermute | solution.py:210
  45.8 3.3 %collective-permute-start.5 = (f32[576,128]{1,0:T(8,128)S(1)}, f32[576,128]{1,0:T(8,128)}, u32[]{:S(2)}, u32[]{:S(2)}) collective-permute-start(f32[576,128]{1,0:T(8,128)S(1)} %dynamic-slice_bitcast_fusion.1), channel_id=1, source_target_pairs={{0,1},{1,0},{2,3},{3,2},{4,5},{5,4},{6,7},{7,6},{8,9},{9,8},{10,11... | collective-permute-start | bytes 884744 | tf_op jit(solution)/shard_map/ppermute | solution.py:222
  50.1 15.9 %collective-permute-start.6 = (f32[144,128]{1,0:T(8,128)S(1)}, f32[144,128]{1,0:T(8,128)S(1)}, u32[]{:S(2)}, u32[]{:S(2)}) collective-permute-start(f32[144,128]{1,0:T(8,128)S(1)} %get-tuple-element.23), channel_id=1, source_target_pairs={{0,2},{1,3},{2,4},{3,5},{4,6},{5,7},{6,0},{7,1},{8,10},{9,11},{10,... | collective-permute-start | bytes 221192 | tf_op jit(solution)/shard_map/ppermute | solution.py:222
  63.5 4.7 %collective-permute-start.7 = (f32[144,128]{1,0:T(8,128)S(1)}, f32[144,128]{1,0:T(8,128)S(1)}, u32[]{:S(2)}, u32[]{:S(2)}) collective-permute-start(f32[144,128]{1,0:T(8,128)S(1)} %get-tuple-element.25), channel_id=1, source_target_pairs={{0,4},{1,5},{2,6},{3,7},{4,0},{5,1},{6,2},{7,3},{8,12},{9,13},{10,... | collective-permute-start | bytes 221192 | tf_op jit(solution)/shard_map/ppermute | solution.py:222
  63.5 4.7 %collective-permute-start.8 = (f32[144,128]{1,0:T(8,128)S(1)}, f32[144,128]{1,0:T(8,128)S(1)}, u32[]{:S(2)}, u32[]{:S(2)}) collective-permute-start(f32[144,128]{1,0:T(8,128)S(1)} %get-tuple-element.24), channel_id=1, source_target_pairs={{0,6},{1,7},{2,0},{3,1},{4,2},{5,3},{6,4},{7,5},{8,14},{9,15},{10,... | collective-permute-start | bytes 221192 | tf_op jit(solution)/shard_map/ppermute | solution.py:222
  68.2 13.7 %collective-permute-start.10 = (f32[144,128]{1,0:T(8,128)S(1)}, f32[144,128]{1,0:T(8,128)S(1)}, u32[]{:S(2)}, u32[]{:S(2)}) collective-permute-start(f32[144,128]{1,0:T(8,128)S(1)} %fusion.5), channel_id=1, source_target_pairs={{0,16},{1,17},{2,18},{3,19},{4,20},{5,21},{6,22},{7,23},{8,24},{9,... | collective-permute-start | bytes 221192 | tf_op jit(solution)/shard_map/ppermute | solution.py:222
  79.5 4.9 %collective-permute-start.11 = (f32[144,128]{1,0:T(8,128)S(1)}, f32[144,128]{1,0:T(8,128)S(1)}, u32[]{:S(2)}, u32[]{:S(2)}) collective-permute-start(f32[144,128]{1,0:T(8,128)S(1)} %fusion.5), channel_id=1, source_target_pairs={{0,24},{1,25},{2,26},{3,27},{4,28},{5,29},{6,30},{7,31},{8,0},{9,1... | collective-permute-start | bytes 221192 | tf_op jit(solution)/shard_map/ppermute | solution.py:222
  81.9 4.4 %collective-permute-start.9 = (f32[144,128]{1,0:T(8,128)S(1)}, f32[144,128]{1,0:T(8,128)S(1)}, u32[]{:S(2)}, u32[]{:S(2)}) collective-permute-start(f32[144,128]{1,0:T(8,128)S(1)} %fusion.5), channel_id=1, source_target_pairs={{0,8},{1,9},{2,10},{3,11},{4,12},{5,13},{6,14},{7,15},{8,16},{9,17... | collective-permute-start | bytes 221192 | tf_op jit(solution)/shard_map/ppermute | solution.py:222
  86.3 14.3 %collective-permute-start.12 = (f32[144,128]{1,0:T(8,128)S(1)}, f32[144,128]{1,0:T(8,128)S(1)}, u32[]{:S(2)}, u32[]{:S(2)}) collective-permute-start(f32[144,128]{1,0:T(8,128)S(1)} %add_add_fusion.3), channel_id=1, source_target_pairs={{0,32},{1,33},{2,34},{3,35},{4,36},{5,37},{6,38},{7,39},{8,40},{9,... | collective-permute-start | bytes 221192 | tf_op jit(solution)/shard_map/ppermute | solution.py:222
  89.2 13.4 %collective-permute-start.13 = (f32[144,128]{1,0:T(8,128)S(1)}, f32[144,128]{1,0:T(8,128)S(1)}, u32[]{:S(2)}, u32[]{:S(2)}) collective-permute-start(f32[144,128]{1,0:T(8,128)S(1)} %add_add_fusion.3), channel_id=1, source_target_pairs={{0,64},{1,65},{2,66},{3,67},{4,68},{5,69},{6,70},{7,71},{8,72},{9,... | collective-permute-start | bytes 221192 | tf_op jit(solution)/shard_map/ppermute | solution.py:222
  90.8 11.8 %collective-permute-start.14 = (f32[144,128]{1,0:T(8,128)S(1)}, f32[144,128]{1,0:T(8,128)S(1)}, u32[]{:S(2)}, u32[]{:S(2)}) collective-permute-start(f32[144,128]{1,0:T(8,128)S(1)} %add_add_fusion.3), channel_id=1, source_target_pairs={{0,96},{1,97},{2,98},{3,99},{4,100},{5,101},{6,102},{7,103},{8,104... | collective-permute-start | bytes 221192 | tf_op jit(solution)/shard_map/ppermute | solution.py:222
  92.9 11.7 %collective-permute-start.2 = (s32[33]{0:T(128)S(1)}, s32[33]{0:T(128)S(1)}, u32[]{:S(2)}, u32[]{:S(2)}) collective-permute-start(s32[33]{0:T(128)S(1)} %pad_add_fusion.2), channel_id=1, source_target_pairs={{0,1},{1,2},{2,3},{3,4},{4,5},{5,6},{6,7},{7,8},{8,9},{9,10},{10,1... | collective-permute-start | bytes 404 | tf_op jit(solution)/shard_map/ppermute | solution.py:210
  98.7 5.9 %collective-permute-start.3 = (s32[33]{0:T(128)S(1)}, s32[33]{0:T(128)S(1)}, u32[]{:S(2)}, u32[]{:S(2)}) collective-permute-start(s32[33]{0:T(128)S(1)} %pad_add_fusion.2), channel_id=1, source_target_pairs={{1,0},{2,1},{3,2},{4,3},{5,4},{6,5},{7,6},{8,7},{9,8},{10,9},{11,1... | collective-permute-start | bytes 404 | tf_op jit(solution)/shard_map/ppermute | solution.py:210
  100.7 39.1 %collective-permute-start.4 = (f32[2,128,2048]{2,1,0:T(8,128)S(1)}, f32[2,128,2048]{2,1,0:T(8,128)}, u32[]{:S(2)}, u32[]{:S(2)}) collective-permute-start(f32[2,128,2048]{2,1,0:T(8,128)S(1)} %copy-done.16), channel_id=1, source_target_pairs={{1,0},{2,1},{3,2},{4,3},{5,4},{6,5},{7,6},{8,7},{9,8},{10,9},{11,1... | collective-permute-start | bytes 6291464 | tf_op jit(solution)/shard_map/ppermute | solution.py:210
  102.7 12.4 %collective-permute-start.15 = (f32[144,128]{1,0:T(8,128)S(1)}, f32[144,128]{1,0:T(8,128)S(1)}, u32[]{:S(2)}, u32[]{:S(2)}) collective-permute-start(f32[144,128]{1,0:T(8,128)S(1)} %get-tuple-element.17), channel_id=1, source_target_pairs={{0,2},{1,3},{2,4},{3,5},{4,6},{5,7},{6,0},{7,1},{8,10},{9,11},{10,... | collective-permute-start | bytes 221192 | tf_op jit(solution)/shard_map/ppermute | solution.py:222
  108.9 35.5 %collective-permute-start.1 = (f32[2,128,2048]{2,1,0:T(8,128)}, f32[2,128,2048]{2,1,0:T(8,128)S(1)}, u32[]{:S(2)}, u32[]{:S(2)}) collective-permute-start(f32[2,128,2048]{2,1,0:T(8,128)} %get-tuple-element.9), channel_id=1, source_target_pairs={{0,1},{1,2},{2,3},{3,4},{4,5},{5,6},{6,7},{7,8},{8,9},{9,10},{10,1... | collective-permute-start | bytes 6291464 | tf_op jit(solution)/shard_map/ppermute | solution.py:210
  110.8 27.2 %collective-permute-start.16 = (f32[144,128]{1,0:T(8,128)S(1)}, f32[144,128]{1,0:T(8,128)S(1)}, u32[]{:S(2)}, u32[]{:S(2)}) collective-permute-start(f32[144,128]{1,0:T(8,128)S(1)} %get-tuple-element.17), channel_id=1, source_target_pairs={{0,4},{1,5},{2,6},{3,7},{4,0},{5,1},{6,2},{7,3},{8,12},{9,13},{10,... | collective-permute-start | bytes 221192 | tf_op jit(solution)/shard_map/ppermute | solution.py:222
  112.9 25.1 %collective-permute-start.17 = (f32[144,128]{1,0:T(8,128)S(1)}, f32[144,128]{1,0:T(8,128)S(1)}, u32[]{:S(2)}, u32[]{:S(2)}) collective-permute-start(f32[144,128]{1,0:T(8,128)S(1)} %get-tuple-element.17), channel_id=1, source_target_pairs={{0,6},{1,7},{2,0},{3,1},{4,2},{5,3},{6,4},{7,5},{8,14},{9,15},{10,... | collective-permute-start | bytes 221192 | tf_op jit(solution)/shard_map/ppermute | solution.py:222
  155.4 24.5 %collective-permute-start.20 = (f32[576,128]{1,0:T(8,128)S(1)}, f32[576,128]{1,0:T(8,128)S(1)}, u32[]{:S(2)}, u32[]{:S(2)}) collective-permute-start(f32[576,128]{1,0:T(8,128)S(1)} %dynamic-slice_bitcast_fusion), channel_id=1, source_target_pairs={{0,1},{1,0},{2,3},{3,2},{4,5},{5,4},{6,7},{7,6},{8,9},{9,8},{10,11... | collective-permute-start | bytes 884744 | tf_op jit(solution)/shard_map/ppermute | solution.py:222
  180.0 6.7 %collective-permute-start.21 = (f32[144,128]{1,0:T(8,128)S(1)}, f32[144,128]{1,0:T(8,128)S(1)}, u32[]{:S(2)}, u32[]{:S(2)}) collective-permute-start(f32[144,128]{1,0:T(8,128)S(1)} %get-tuple-element.20), channel_id=1, source_target_pairs={{0,2},{1,3},{2,4},{3,5},{4,6},{5,7},{6,0},{7,1},{8,10},{9,11},{10,... | collective-permute-start | bytes 221192 | tf_op jit(solution)/shard_map/ppermute | solution.py:222
  180.0 6.6 %collective-permute-start.22 = (f32[144,128]{1,0:T(8,128)S(1)}, f32[144,128]{1,0:T(8,128)S(1)}, u32[]{:S(2)}, u32[]{:S(2)}) collective-permute-start(f32[144,128]{1,0:T(8,128)S(1)} %get-tuple-element.22), channel_id=1, source_target_pairs={{0,4},{1,5},{2,6},{3,7},{4,0},{5,1},{6,2},{7,3},{8,12},{9,13},{10,... | collective-permute-start | bytes 221192 | tf_op jit(solution)/shard_map/ppermute | solution.py:222
  180.1 6.5 %collective-permute-start.23 = (f32[144,128]{1,0:T(8,128)S(1)}, f32[144,128]{1,0:T(8,128)S(1)}, u32[]{:S(2)}, u32[]{:S(2)}) collective-permute-start(f32[144,128]{1,0:T(8,128)S(1)} %get-tuple-element.21), channel_id=1, source_target_pairs={{0,6},{1,7},{2,0},{3,1},{4,2},{5,3},{6,4},{7,5},{8,14},{9,15},{10,... | collective-permute-start | bytes 221192 | tf_op jit(solution)/shard_map/ppermute | solution.py:222
  186.7 4.5 %collective-permute-start.24 = (f32[144,128]{1,0:T(8,128)S(1)}, f32[144,128]{1,0:T(8,128)S(1)}, u32[]{:S(2)}, u32[]{:S(2)}) collective-permute-start(f32[144,128]{1,0:T(8,128)S(1)} %fusion.3), channel_id=1, source_target_pairs={{0,8},{1,9},{2,10},{3,11},{4,12},{5,13},{6,14},{7,15},{8,16},{9,17... | collective-permute-start | bytes 221192 | tf_op jit(solution)/shard_map/ppermute | solution.py:222
  188.4 4.8 %collective-permute-start.25 = (f32[144,128]{1,0:T(8,128)S(1)}, f32[144,128]{1,0:T(8,128)S(1)}, u32[]{:S(2)}, u32[]{:S(2)}) collective-permute-start(f32[144,128]{1,0:T(8,128)S(1)} %fusion.3), channel_id=1, source_target_pairs={{0,16},{1,17},{2,18},{3,19},{4,20},{5,21},{6,22},{7,23},{8,24},{9,... | collective-permute-start | bytes 221192 | tf_op jit(solution)/shard_map/ppermute | solution.py:222
  190.4 3.8 %collective-permute-start.26 = (f32[144,128]{1,0:T(8,128)S(1)}, f32[144,128]{1,0:T(8,128)S(1)}, u32[]{:S(2)}, u32[]{:S(2)}) collective-permute-start(f32[144,128]{1,0:T(8,128)S(1)} %fusion.3), channel_id=1, source_target_pairs={{0,24},{1,25},{2,26},{3,27},{4,28},{5,29},{6,30},{7,31},{8,0},{9,1... | collective-permute-start | bytes 221192 | tf_op jit(solution)/shard_map/ppermute | solution.py:222
  194.2 10.3 %collective-permute-start.27 = (f32[144,128]{1,0:T(8,128)S(1)}, f32[144,128]{1,0:T(8,128)S(1)}, u32[]{:S(2)}, u32[]{:S(2)}) collective-permute-start(f32[144,128]{1,0:T(8,128)S(1)} %add_add_fusion.1), channel_id=1, source_target_pairs={{0,32},{1,33},{2,34},{3,35},{4,36},{5,37},{6,38},{7,39},{8,40},{9,... | collective-permute-start | bytes 221192 | tf_op jit(solution)/shard_map/ppermute | solution.py:222
  196.5 7.9 %collective-permute-start.28 = (f32[144,128]{1,0:T(8,128)S(1)}, f32[144,128]{1,0:T(8,128)S(1)}, u32[]{:S(2)}, u32[]{:S(2)}) collective-permute-start(f32[144,128]{1,0:T(8,128)S(1)} %add_add_fusion.1), channel_id=1, source_target_pairs={{0,64},{1,65},{2,66},{3,67},{4,68},{5,69},{6,70},{7,71},{8,72},{9,... | collective-permute-start | bytes 221192 | tf_op jit(solution)/shard_map/ppermute | solution.py:222
  196.5 7.9 %collective-permute-start.29 = (f32[144,128]{1,0:T(8,128)S(1)}, f32[144,128]{1,0:T(8,128)S(1)}, u32[]{:S(2)}, u32[]{:S(2)}) collective-permute-start(f32[144,128]{1,0:T(8,128)S(1)} %add_add_fusion.1), channel_id=1, source_target_pairs={{0,96},{1,97},{2,98},{3,99},{4,100},{5,101},{6,102},{7,103},{8,104... | collective-permute-start | bytes 221192 | tf_op jit(solution)/shard_map/ppermute | solution.py:222
  199.0 37.5 %collective-permute-start.19 = (f32[2,128,2048]{2,1,0:T(8,128)S(1)}, f32[2,128,2048]{2,1,0:T(8,128)S(1)}, u32[]{:S(2)}, u32[]{:S(2)}) collective-permute-start(f32[2,128,2048]{2,1,0:T(8,128)S(1)} %copy-done.18), channel_id=1, source_target_pairs={{0,1},{1,2},{2,3},{3,4},{4,5},{5,6},{6,7},{7,8},{8,9},{9,10},{10,1... | collective-permute-start | bytes 6291464 | tf_op jit(solution)/shard_map/ppermute | solution.py:210
  204.5 25.2 %collective-permute-start.30 = (f32[144,128]{1,0:T(8,128)S(1)}, f32[144,128]{1,0:T(8,128)S(1)}, u32[]{:S(2)}, u32[]{:S(2)}) collective-permute-start(f32[144,128]{1,0:T(8,128)S(1)} %get-tuple-element.15), channel_id=1, source_target_pairs={{0,2},{1,3},{2,4},{3,5},{4,6},{5,7},{6,0},{7,1},{8,10},{9,11},{10,... | collective-permute-start | bytes 221192 | tf_op jit(solution)/shard_map/ppermute | solution.py:222
  207.5 26.3 %collective-permute-start.31 = (f32[144,128]{1,0:T(8,128)S(1)}, f32[144,128]{1,0:T(8,128)S(1)}, u32[]{:S(2)}, u32[]{:S(2)}) collective-permute-start(f32[144,128]{1,0:T(8,128)S(1)} %get-tuple-element.15), channel_id=1, source_target_pairs={{0,4},{1,5},{2,6},{3,7},{4,0},{5,1},{6,2},{7,3},{8,12},{9,13},{10,... | collective-permute-start | bytes 221192 | tf_op jit(solution)/shard_map/ppermute | solution.py:222
  210.6 23.2 %collective-permute-start.32 = (f32[144,128]{1,0:T(8,128)S(1)}, f32[144,128]{1,0:T(8,128)S(1)}, u32[]{:S(2)}, u32[]{:S(2)}) collective-permute-start(f32[144,128]{1,0:T(8,128)S(1)} %get-tuple-element.15), channel_id=1, source_target_pairs={{0,6},{1,7},{2,0},{3,1},{4,2},{5,3},{6,4},{7,5},{8,14},{9,15},{10,... | collective-permute-start | bytes 221192 | tf_op jit(solution)/shard_map/ppermute | solution.py:222
  (21 other events, 189.5 us)

commit v2 on v1

v2 whole, which is shorter than its diff:
```python
import functools

import jax
import jax.numpy as jnp
import ml_dtypes
import numpy as np
from jax import lax
from jax.experimental import pallas as pl
from jax.experimental.pallas import tpu as pltpu
from jax.sharding import PartitionSpec as P

SIGMA = 0.5
NSLOT, OFF_SLOT, OFF_PAIR = 2, 1, 0
STEP_TILES = 4
VMEM_LIMIT = 56 * 1024 * 1024


def split_np(w):
    hi = w.astype(ml_dtypes.bfloat16)
    lo = (w - hi.astype(np.float64)).astype(ml_dtypes.bfloat16)
    return hi, lo


def dft_blocks(length):
    index = np.arange(length)
    angle = 2.0 * np.pi * ((index[:, None] * index[None, :]) % length) / length
    c = np.cos(angle) / np.sqrt(length)
    s = np.sin(angle) / np.sqrt(length)
    minus = np.block([[c, -s], [s, c]])
    plus = np.block([[c, s], [-s, c]])
    return minus, plus


def split(x):
    hi = x.astype(jnp.bfloat16)
    lo = (x - hi.astype(jnp.float32)).astype(jnp.bfloat16)
    return hi, lo


def dot(a, b):
    return lax.dot_general(a, b, (((1,), (0,)), ((), ())), preferred_element_type=jnp.float32)


def right_product(x, w_ref):
    hi, lo = split(x)
    return dot(jnp.concatenate([hi, lo, hi], axis=1), w_ref[...])


def left_product(w_ref, x):
    n = x.shape[0]
    hi, lo = split(x)
    both = dot(w_ref[...], hi)
    return both[:n] + both[n:] + dot(w_ref[:n], lo)


def load_columns(ref, frame, rows, sems):
    return [
        pltpu.make_async_copy(ref.at[:, :, pl.ds(t * 128, 128)], frame.at[:, t, pl.ds(rows[0], rows[1] - rows[0]), :], sems.at[t])
        for t in range(frame.shape[1])
    ]


def start_all(copies):
    for copy in copies:
        copy.start()


def wait_all(copies):
    for copy in copies:
        copy.wait()


def pattern_kernel(stage, scal_ref, *refs):
    refs = list(refs)
    take = lambda n: [refs.pop(0) for _ in range(n)]
    objects = take({"own": 2, "above": 2, "both": 4}[stage])
    before = take(2) if stage == "above" else None
    amps = take(2 if stage == "both" else 1)
    whole = take(5)
    outs = take({"own": 2, "above": 4, "both": 6}[stage])
    frame, grad, terms_ref, amp_ref, probe_ref, rf_ref, rb_ref, lf_ref, lb_ref, order, in_sems, tile_sems, out_sems = take(13)
    tiles, strip = frame.shape[1], frame.shape[2] // 2
    quarter = strip // 2
    nmodes, length = probe_ref.shape[1], probe_ref.shape[2]
    slots = amp_ref.shape[0] // len(amps)
    width = 2 * slots + 2
    owners = {"own": (0,), "above": (1,), "both": (0, 1)}[stage]

    moves = list(zip(whole, (probe_ref, rf_ref, rb_ref, lf_ref, lb_ref)))
    moves += [(ref, amp_ref.at[pl.ds(k * slots, slots)]) for k, ref in enumerate(amps)]
    if stage == "both":
        share, extra = take(2)
        moves += [(objects[0], frame), (objects[1], share)]
        moves += [(objects[2 + k], extra.at[:, :, pl.ds(k * strip, strip)]) for k in range(2)]
        copies = []
    elif stage == "own":
        copies = load_columns(objects[0], frame, (quarter, 3 * quarter), tile_sems.at[0])
        copies += load_columns(objects[1], frame, (3 * quarter, 4 * quarter), tile_sems.at[1])
    else:
        copies = load_columns(objects[0], frame, (0, quarter), tile_sems.at[0])
        copies += load_columns(objects[1], frame, (quarter, 3 * quarter), tile_sems.at[1])
        moves += [(before[0], grad.at[:, :, pl.ds(quarter, 3 * quarter)]), (before[1], terms_ref)]
    copies += [pltpu.make_async_copy(src, dst, in_sems.at[k]) for k, (src, dst) in enumerate(moves)]
    start_all(copies)
    if stage == "above":
        grad[:, :, :quarter] = jnp.zeros((2, tiles, quarter, 128), jnp.float32)
    else:
        grad[...] = jnp.zeros_like(grad)
        terms_ref[...] = jnp.zeros_like(terms_ref)
    chosen = jnp.int32(0)
    for k, owner in enumerate(owners):
        for local in range(slots):
            order[chosen] = k * slots + local
            low = scal_ref[owner * width + local] >= quarter
            inside = (local < scal_ref[owner * width + 2 * slots]) & (low if owner else jnp.logical_not(low))
            chosen = chosen + inside.astype(jnp.int32)
    wait_all(copies)
    late = []
    if stage == "both":

        def add_share(t, carry):
            for part in range(2):
                frame[part, t] -= extra[part, t] * share[t]
            return carry

        lax.fori_loop(0, tiles, add_share, 0)
        late.append(pltpu.make_async_copy(frame.at[:, :, pl.ds(quarter, strip)], outs[5], out_sems.at[5]))
        start_all(late)
    h = length // 2
    pairs = nmodes // 2

    def place(slot):
        owner = slot // slots if len(owners) > 1 else owners[0]
        at = owner * width + slot % slots
        col = scal_ref[at + slots]
        tile = jnp.minimum(col // 128, tiles - 2)
        return scal_ref[at] + quarter - owner * strip, tile, col - tile * 128

    def stream(slot, shared, p):
        row, tile, shift = shared["place"]
        if p == 0:
            back = lax.rem(256 - shift, 256)

            def cut(part):
                wide = jnp.concatenate([frame[part, tile + k, pl.ds(row, length), :] for k in range(2)], axis=1)
                return pltpu.roll(wide, back, 1)[:, :length]

            shared["x"] = (cut(0), cut(1))
        xr, xi = shared["x"]
        modes = (2 * p, 2 * p + 1)
        waves = []
        for m in modes:
            pr, pi = probe_ref[0, m], probe_ref[1, m]
            waves.append(split(jnp.concatenate([pr * xr - pi * xi, pr * xi + pi * xr], axis=1)))
        yield
        mids = [dot(jnp.concatenate([hi, lo, hi], axis=1), rf_ref[...]) for hi, lo in waves]
        yield
        top = jnp.concatenate([jnp.concatenate([y[:h, :length] for y in mids], axis=1), jnp.concatenate([y[:h, length:] for y in mids], axis=1)], axis=0)
        low = jnp.concatenate([jnp.concatenate([y[h:, :length] for y in mids], axis=1), jnp.concatenate([y[h:, length:] for y in mids], axis=1)], axis=0)
        sums = [jnp.concatenate(split(v), axis=0) for v in (top + low, top - low)]
        yield
        fars = [dot(lf_ref[k], v) for k, v in enumerate(sums)]
        yield
        fars = [f[:length] + f[length:] for f in fars]
        sq = [f * f for f in fars]
        sq = [q[:h] + q[h:] for q in sq]
        shared.setdefault("power", []).extend(q[:, k * length : (k + 1) * length] for k in range(2) for q in [jnp.concatenate(sq, axis=0)])
        yield
        while len(shared["power"]) < nmodes:
            yield
        if "weight" not in shared:
            intensity = functools.reduce(lambda a, b: a + b, shared["power"])
            amp = jnp.concatenate([amp_ref[slot, pl.ds(k, h, stride=2), :] for k in range(2)], axis=0)
            shared["weight"] = (1.0 - amp * lax.rsqrt(intensity + SIGMA)) * shared["alive"]
        w = jnp.concatenate([shared["weight"]] * 2, axis=1)
        ins = [split(f * jnp.concatenate([wk, wk], axis=0)) for f, wk in zip(fars, (w[:h], w[h:]))]
        yield
        u, v = [dot(lb_ref[k], jnp.concatenate(x, axis=0)) for k, x in enumerate(ins)]
        yield
        u, v = u[:length] + u[length:], v[:length] + v[length:]
        a, b = u + v, u - v
        ins = []
        for k in range(2):
            c = slice(k * length, (k + 1) * length)
            re = jnp.concatenate([a[:h, c], b[:h, c]], axis=0)
            im = jnp.concatenate([a[h:, c], b[h:, c]], axis=0)
            ins.append(split(jnp.concatenate([re, im], axis=1)))
        yield
        chis = [dot(jnp.concatenate([hi, lo, hi], axis=1), rb_ref[...]) for hi, lo in ins]
        yield
        for m, chi in zip(modes, chis):
            cr, ci = chi[:, :length], chi[:, length:]
            pr, pi = probe_ref[0, m], probe_ref[1, m]
            a = pr * cr + pi * ci
            b = pr * ci - pi * cr
            g = shared.get("g")
            shared["g"] = (a, b) if g is None else (g[0] + a, g[1] + b)
            terms_ref[m * length : (m + 1) * length] += xr * cr + xi * ci
            terms_ref[(nmodes + m) * length : (nmodes + m + 1) * length] += xr * ci - xi * cr
        shared["done"] = shared.get("done", 0) + 1
        if shared["done"] == pairs:
            terms_ref[2 * nmodes * length :] += (xr * xr + xi * xi) * shared["alive"]
            pad = jnp.zeros((length, 128), jnp.float32)
            for part, g in enumerate(shared["g"]):
                wide = pltpu.roll(jnp.concatenate([g, pad], axis=1), shift, 1)
                for k in range(2):
                    grad[part, tile + k, pl.ds(row, length), :] += wide[:, k * 128 : (k + 1) * 128]
        yield

    def step(index, carry):
        streams = []
        for k in range(NSLOT):
            slot = order[jnp.minimum(NSLOT * index + k, jnp.maximum(chosen - 1, 0))]
            shared = {"place": place(slot), "alive": (NSLOT * index + k < chosen).astype(jnp.float32)}
            for p in range(pairs):
                streams.append([OFF_SLOT * k + OFF_PAIR * p, stream(slot, shared, p)])
        tick = 0
        while streams:
            for entry in list(streams):
                if tick >= entry[0]:
                    try:
                        next(entry[1])
                    except StopIteration:
                        streams.remove(entry)
            tick += 1
        return carry

    lax.fori_loop(0, (chosen + NSLOT - 1) // NSLOT, step, 0)
    if stage == "own":
        moves = [(grad.at[:, :, pl.ds(quarter, 3 * quarter)], outs[0]), (terms_ref, outs[1])]
    else:
        if stage == "above":
            moves = [(grad.at[:, :, pl.ds(k * strip, strip)], outs[k]) for k in range(2)]
        else:
            cuts = ((0, quarter), (3 * quarter, quarter), (quarter, strip))
            moves = [(grad.at[:, :, pl.ds(first, rows)], out) for (first, rows), out in zip(cuts, outs)]
        half = terms_ref.shape[0] // 2
        core = scal_ref[2 * slots + 1]
        k = len(moves)
        moves.append((terms_ref.at[pl.ds(pl.multiple_of(core * half, 8), half)], outs[k]))
        moves.append((terms_ref.at[pl.ds(pl.multiple_of((1 - core) * half, 8), half)], outs[k + 1]))
    copies = [pltpu.make_async_copy(src, dst, out_sems.at[k]) for k, (src, dst) in enumerate(moves)]
    start_all(copies)
    wait_all(copies + late)


def half_product(w_ref, which, x):
    n = x.shape[0]
    hi, lo = split(x)
    both = dot(w_ref[which], jnp.concatenate([hi, lo], axis=0))
    return both[:n] + both[n:]


def half_blocks(length):
    n = np.arange(length // 2)
    forward, backward = [], []
    for parity in range(2):
        angle = 2.0 * np.pi * (((2 * n[:, None] + parity) * n[None, :]) % length) / length
        c, s = np.cos(angle) / np.sqrt(length), np.sin(angle) / np.sqrt(length)
        forward.append(np.block([[c, s], [-s, c]]))
        backward.append(np.block([[c.T, -s.T], [s.T, c.T]]))
    out = []
    for mats in (forward, backward):
        both = []
        for w in mats:
            hi, lo = split_np(w)
            both.append(np.block([[hi, hi], [lo, lo]]))
        out.append(np.stack(both))
    return out


def vmem():
    return pl.BlockSpec(memory_space=pltpu.VMEM)


def smem():
    return pl.BlockSpec(memory_space=pltpu.SMEM)


def anywhere():
    return pl.BlockSpec(memory_space=pl.ANY)


def f32(*shape):
    return jax.ShapeDtypeStruct(shape, jnp.float32)


def patterns(stage, scalars, objects, before, amps, probe, tiles, flops):
    length, nmodes = probe.shape[-1], probe.shape[1]
    slots = amps[0].shape[0]
    strip = length
    minus, plus = dft_blocks(length)
    mh, ml = split_np(minus)
    ph, plo = split_np(plus)
    mats = (np.concatenate([mh, mh, ml], axis=0), np.concatenate([ph, ph, plo], axis=0)) + tuple(half_blocks(length))
    rows = (2 * nmodes + 1) * length
    half = f32(rows // 2, length)
    frame = (2, tiles, 2 * strip, 128)
    grads = [f32(2, tiles, n, 128) for n in (strip // 2, strip, 3 * strip // 2)]
    out_shape = {
        "own": (grads[2], f32(rows, length)),
        "above": (grads[1], grads[1], half, half),
        "both": (grads[0], grads[0], grads[1], half, half, grads[1]),
    }[stage]
    arrays = list(objects) + list(before or ()) + list(amps) + [probe]
    out_specs = tuple(vmem() if shape is half else anywhere() for shape in out_shape)
    return pl.pallas_call(
        functools.partial(pattern_kernel, stage),
        out_shape=out_shape,
        in_specs=[smem()] + [anywhere()] * (len(arrays) + len(mats)),
        out_specs=out_specs,
        scratch_shapes=[
            pltpu.VMEM(frame, jnp.float32),
            pltpu.VMEM(frame, jnp.float32),
            pltpu.VMEM((rows, length), jnp.float32),
            pltpu.VMEM((len(amps) * slots,) + amps[0].shape[1:], jnp.float32),
            pltpu.VMEM(probe.shape, jnp.float32),
        ]
        + [pltpu.VMEM(m.shape, jnp.bfloat16) for m in mats]
        + [
            pltpu.SMEM((2 * slots + 1,), jnp.int32),
            pltpu.SemaphoreType.DMA((11,)),
            pltpu.SemaphoreType.DMA((2, tiles)),
            pltpu.SemaphoreType.DMA((6,)),
        ]
        + ([pltpu.VMEM(frame[1:], jnp.float32), pltpu.VMEM(frame, jnp.float32)] if stage == "both" else []),
        compiler_params=pltpu.CompilerParams(vmem_limit_bytes=VMEM_LIMIT),
        cost_estimate=pl.CostEstimate(flops=flops, bytes_accessed=1024, transcendentals=0),
        name="patterns_" + stage,
    )(scalars, *arrays, *map(jnp.asarray, mats))


def light_kernel(nsets, strip, first, natural, scal_ref, probe_hbm, *refs):
    objects, grads = refs[: 3 if natural else 1], refs[3 if natural else 1 : 5 if natural else 2]
    pre_ref, share_ref, acc, frame, grad, probe_ref, tile_sems, sems = refs[len(objects) + len(grads) :]
    tiles = acc.shape[0]
    rows = frame.shape[2]
    length, nmodes = probe_ref.shape[2], probe_ref.shape[1]
    if natural:
        half = strip // 2
        spans = ((0, half), (half, 3 * half), (3 * half, 4 * half))
        copies = [c for k, (ref, span) in enumerate(zip(objects, spans)) for c in load_columns(ref, frame, span, tile_sems.at[k])]
        moves = [(ref, grad.at[:, :, pl.ds(k * strip, strip)]) for k, ref in enumerate(grads)]
    else:
        copies = []
        moves = [(objects[0], frame), (grads[0], grad)]
    load = pltpu.make_async_copy(probe_hbm, probe_ref, sems.at[0])
    copies += [pltpu.make_async_copy(src, dst, sems.at[1 + k]) for k, (src, dst) in enumerate(moves)]
    start_all([load] + copies)
    acc[...] = jnp.zeros_like(acc)
    load.wait()
    power = None
    for m in range(nmodes):
        term = probe_ref[0, m] * probe_ref[0, m] + probe_ref[1, m] * probe_ref[1, m]
        power = term if power is None else power + term
    wide0 = jnp.concatenate([power, jnp.zeros_like(power)], axis=1)
    width = scal_ref.shape[0] // nsets
    for s in range(nsets):

        def step(slot, carry, s=s):
            row = scal_ref[s * width + slot] + s * strip
            col = scal_ref[s * width + 16 + slot]
            tile = jnp.minimum(col // 128, tiles - 2)
            wide = pltpu.roll(wide0, col - tile * 128, 1)
            for k in range(2):
                acc[tile + k, pl.ds(row, length), :] += wide[:, k * 128 : (k + 1) * 128]
            return carry

        lax.fori_loop(0, scal_ref[s * width + 32], step, 0)
    wait_all(copies)

    def combine(t, carry):
        share = 1.0 / (acc[t, first : first + rows] + 1.0)
        acc[t, first : first + rows] = share
        for part in range(2):
            frame[part, t] -= grad[part, t] * share
        return carry

    lax.fori_loop(0, tiles, combine, 0)
    stores = [
        pltpu.make_async_copy(frame, pre_ref, sems.at[3]),
        pltpu.make_async_copy(acc.at[:, pl.ds(first, rows)], share_ref, sems.at[4]),
    ]
    start_all(stores)
    wait_all(stores)


def light(scalars, probe, objects, grads, nsets, strip, tiles, first, rows):
    natural = len(objects) == 3
    return pl.pallas_call(
        functools.partial(light_kernel, nsets, strip, first, natural),
        out_shape=(f32(2, tiles, rows, 128), f32(tiles, rows, 128)),
        in_specs=[smem()] + [anywhere()] * (1 + len(objects) + len(grads)),
        out_specs=(anywhere(), anywhere()),
        scratch_shapes=[
            pltpu.VMEM((tiles, (nsets + 1) * strip, 128), jnp.float32),
            pltpu.VMEM((2, tiles, rows, 128), jnp.float32),
            pltpu.VMEM((2, tiles, rows, 128), jnp.float32),
            pltpu.VMEM(probe.shape, jnp.float32),
            pltpu.SemaphoreType.DMA((3, tiles)),
            pltpu.SemaphoreType.DMA((5,)),
        ],
        compiler_params=pltpu.CompilerParams(vmem_limit_bytes=VMEM_LIMIT),
        cost_estimate=pl.CostEstimate(flops=16 * nsets * 40000, bytes_accessed=16 * 1024 * 1024, transcendentals=0),
        name="light",
    )(scalars, probe, *objects, *grads)


def last_kernel(pre, share, above_in, below_in, out):
    half = above_in.shape[2]
    for t in range(pre.shape[1]):
        c = slice(t * 128, (t + 1) * 128)
        for part in range(2):
            for k, got in enumerate((above_in, below_in)):
                r = slice(k * half, (k + 1) * half)
                out[part, r, c] = pre[part, t, r] - got[part, t] * share[t, r]


def last(pre, share, above_in, below_in):
    tiles, strip = pre.shape[1:3]

    def block(rows):
        return pl.BlockSpec((2, STEP_TILES, rows, 128), lambda j: (0, j, 0, 0))

    return pl.pallas_call(
        last_kernel,
        out_shape=f32(2, strip, tiles * 128),
        grid=(tiles // STEP_TILES,),
        in_specs=[block(strip), pl.BlockSpec((STEP_TILES, strip, 128), lambda j: (j, 0, 0)), block(strip // 2), block(strip // 2)],
        out_specs=pl.BlockSpec((2, strip, STEP_TILES * 128), lambda j: (0, 0, j)),
        compiler_params=pltpu.CompilerParams(vmem_limit_bytes=VMEM_LIMIT),
        cost_estimate=pl.CostEstimate(flops=4 * strip * tiles * 128, bytes_accessed=7 * 1024 * 1024, transcendentals=0),
        name="last",
    )(pre, share, above_in, below_in)


def shift_by(value, steps):
    count = lax.axis_size("dev")
    return lax.ppermute(
        value, "dev", [(i, i + steps) for i in range(count) if 0 <= i + steps < count]
    )


def rotate(value, stride, extent, steps):
    count = lax.axis_size("dev")

    def target(i):
        z = (i // stride) % extent
        return i + ((z + steps) % extent - z) * stride

    return lax.ppermute(value, "dev", [(i, target(i)) for i in range(count)])


def ring_scatter(value, stride, extent):
    place = (lax.axis_index("dev") // stride) % extent
    total = lax.dynamic_index_in_dim(value, place, 0, keepdims=False)
    for k in range(1, extent):
        piece = lax.dynamic_index_in_dim(value, lax.rem(place + k, extent), 0, keepdims=False)
        total = total + rotate(piece, stride, extent, k)
    return total


def ring_sum(value, stride, extent):
    total = value
    for k in range(1, extent):
        total = total + rotate(value, stride, extent, k)
    return total


def ring_gather(value, stride, extent):
    place = (lax.axis_index("dev") // stride) % extent
    out = jnp.zeros((extent,) + value.shape, value.dtype)
    out = lax.dynamic_update_index_in_dim(out, value, place, 0)
    for k in range(1, extent):
        got = rotate(value, stride, extent, k)
        out = lax.dynamic_update_index_in_dim(out, got, lax.rem(place + extent - k, extent), 0)
    return out


def sum_parts(keep, send):
    part = keep + rotate(send, 1, 2, 1)
    part = ring_scatter(part.reshape(4, -1, 128), 32, 4)
    part = ring_sum(part, 8, 4)
    return ring_sum(part, 2, 4)


def shards(object_field, probe, amplitudes, positions, counts):
    strip, columns = object_field.shape[1:]
    nmodes, length = probe.shape[1], probe.shape[-1]
    half, tiles = strip // 2, columns // 128
    barrier = lax.optimization_barrier
    device = lax.axis_index("dev")
    mine = jnp.concatenate([positions[:, 0] - device * strip, positions[:, 1], counts, (device % 2)[None]])

    def moved(probe, part):
        summed = ring_gather(part, 1, 2).reshape(2 * nmodes + 1, length, length)
        grad = summed[: 2 * nmodes].reshape(2, nmodes, length, length)
        return probe - grad / (summed[2 * nmodes] + 1.0)[None, None]

    def reduced(keep, send):
        part = sum_parts(keep, send)
        return ring_gather(part, 32, 4).reshape(-1, 128)

    below = shift_by(object_field[:, :half], -1)
    prev = shift_by(mine, 1)
    second = shift_by(mine, 2)
    following = shift_by(mine, -1)
    above = shift_by(object_field[:, half:], 1)
    amps = (amplitudes, shift_by(amplitudes, 1))
    before = patterns("own", mine, (object_field, below), None, amps[:1], probe, tiles, 1000)
    prev, second, following, above, got, before = barrier((prev, second, following, above, amps[1], before))
    amps = (amplitudes, got)
    scalars = jnp.concatenate([mine, prev])
    gtop, gbot, keep, send = patterns("above", scalars, (above, object_field), before, amps[1:], probe, tiles, 10**9)
    above_in = shift_by(gbot, 1)
    below_in = shift_by(gtop, -1)
    near = jnp.concatenate([second, prev, mine, following])
    pre, share = light(near, probe, (above, object_field, below), (gtop, gbot), 4, strip, tiles, strip + half, 2 * strip)
    above_in, below_in, pre, share, keep, send = barrier((above_in, below_in, pre, share, keep, send))
    probe = moved(probe, reduced(keep, send))

    gtop, gbot, gmid, keep, send, mid = patterns("both", scalars, (pre, share, above_in, below_in), None, amps, probe, tiles, 10**9)
    above_in = shift_by(gbot, 1)
    below_in = shift_by(gtop, -1)
    pre, share = light(jnp.concatenate([prev, mine]), probe, (mid,), (gmid,), 2, strip, tiles, strip, strip)
    above_in, below_in, pre, share, keep, send = barrier((above_in, below_in, pre, share, keep, send))
    part = sum_parts(keep, send)
    current = last(pre, share, above_in, below_in)
    part = ring_gather(part, 32, 4).reshape(-1, 128)
    current, part = barrier((current, part))
    return (current, moved(probe, part))


def solution(mesh):
    placed = (P(None, "dev", None), P(), P("dev", None, None), P("dev", None), P("dev"))
    return jax.shard_map(
        shards, mesh=mesh, in_specs=placed, out_specs=(P(None, "dev", None), P()), check_vma=False
    )
```

time: 239 us -> 223 us (0.933); the launches traced: 239 us -> 227 us
  Pallas kernels: 24.7 us -> 64.4 us
  waiting for transfers between devices: 87 us -> 51.7 us
  other arithmetic: 11.8 us -> 2.01 us
  starting transfers between devices: 105 us -> 101 us
    pallas_call x4 -> x6, Pallas kernels: 24.7 us -> 64.4 us  [the longest x3 44.8 us: patterns(): pl.pallas_call(functools.partial(pattern_kernel, stage), out_shape=out_sh...]
    ppermute x28, waiting for transfers between devices: 62.9 us -> 27.7 us  [rotate(): return lax.ppermute(value, 'dev', [(i, target(i)) for i in range(count)])]
    ppermute x28, starting transfers between devices: 84.7 us -> 74.4 us  [rotate(): return lax.ppermute(value, 'dev', [(i, target(i)) for i in range(count)])]
    sub x5 -> x2, other arithmetic: 9.42 us -> 1.71 us  [moved(): return probe - grad / (summed[2 * nmodes] + 1.0)[None, None]]
    unnamed x38 -> x26, local copies, waits for them, and re-layouts: 7.76 us -> 0.6 us
    ppermute x6 -> x10, starting transfers between devices: 20.3 us -> 26.7 us  [shift_by(): lax.ppermute(value, 'dev', [(i, i + steps) for i in range(count) if 0 <=...]
    slice x2 -> x3, local copies, waits for them, and re-layouts: 0.07 us -> 3.16 us  [the longest x1 3.09 us: shards(): below = shift_by(object_field[:, :half], -1)]
    ppermute x6 -> x10, waiting for transfers between devices: 24.1 us -> 24.1 us  [shift_by(): lax.ppermute(value, 'dev', [(i, i + steps) for i in range(count) if 0 <=...]
  transfers between devices with their start and end apart: 34 -> 38, of which waited for: 15 -> 27; matrix products, arithmetic and copies ran while one was open for 3% -> 1% of each run, Pallas kernels for 3% -> 13%
where the time goes in v2:
time: 223 us; the launch traced here: 227 us
  starting transfers between devices  101 us (45%)
  Pallas kernels  64.4 us (29%)
  waiting for transfers between devices  51.7 us (23%)
  local copies, waits for them, and re-layouts  6.21 us (3%)
    ppermute x28, starting transfers between devices, rotate(): return lax.ppermute(value, 'dev', [(i, target(i)) for i in range(count)])  74.4 us
    pallas_call x3, Pallas kernels, patterns(): pl.pallas_call(functools.partial(pattern_kernel, stage), out_shape=out_sh...  44.8 us
    ppermute x28, waiting for transfers between devices, rotate(): return lax.ppermute(value, 'dev', [(i, target(i)) for i in range(count)])  27.7 us
    ppermute x10, starting transfers between devices, shift_by(): lax.ppermute(value, 'dev', [(i, i + steps) for i in range(count) if 0 <=...  26.7 us
    ppermute x10, waiting for transfers between devices, shift_by(): lax.ppermute(value, 'dev', [(i, i + steps) for i in range(count) if 0 <=...  24.1 us
    pallas_call x2, Pallas kernels, light(): pl.pallas_call(functools.partial(light_kernel, nsets, strip, first, natur...  15.3 us
  transfers between devices with their start and end apart: 38, of which 27 were waited for; matrix products, arithmetic and copies ran while one was open for 1% of the time, Pallas kernels for 13%

profile of v2, /device:TPU:1, one launch (start us, length us, event | category | flops | bytes accessed | tf_op | source)
XLA Modules:
  0.0 227.2 jit_solution(12253865482791493474)
XLA Ops:
  0.6 3.1 %fusion.6 = (f32[2,64,2048]{2,1,0:T(8,128)}, f32[2,64,2048]{2,1,0:T(8,128)}) fusion(f32[2,128,2048]{2,1,0:T(8,128)} %refs_1_.3), kind=kLoop, calls=%fused_computation.37 | loop fusion | bytes 4194304 | tf_op jit(solution)/shard_map/slice | solution.py:504
  3.7 3.3 %collective-permute-start.5 = (f32[2,64,2048]{2,1,0:T(8,128)}, f32[2,64,2048]{2,1,0:T(8,128)}, u32[]{:S(2)}, u32[]{:S(2)}) collective-permute-start(f32[2,64,2048]{2,1,0:T(8,128)} %get-tuple-element.80), channel_id=1, source_target_pairs={{1,0},{2,1},{3,2},{4,3},{5,4},{6,5},{7,6},{8,7},{9,8},{10,9},{11,1... | collective-permute-start | bytes 3145736 | tf_op jit(solution)/shard_map/ppermute | solution.py:439
  7.1 3.5 %collective-permute-start.3 = (f32[2,64,2048]{2,1,0:T(8,128)}, f32[2,64,2048]{2,1,0:T(8,128)S(1)}, u32[]{:S(2)}, u32[]{:S(2)}) collective-permute-start(f32[2,64,2048]{2,1,0:T(8,128)} %get-tuple-element.81), channel_id=1, source_target_pairs={{0,1},{1,2},{2,3},{3,4},{4,5},{5,6},{6,7},{7,8},{8,9},{9,10},{10,1... | collective-permute-start | bytes 3145736 | tf_op jit(solution)/shard_map/ppermute | solution.py:439
  10.6 2.4 %collective-permute-start.4 = (f32[16,128,128]{2,1,0:T(8,128)}, f32[16,128,128]{2,1,0:T(8,128)S(1)}, u32[]{:S(2)}, u32[]{:S(2)}) collective-permute-start(f32[16,128,128]{2,1,0:T(8,128)} %refs_4_.2), channel_id=1, source_target_pairs={{0,1},{1,2},{2,3},{3,4},{4,5},{5,6},{6,7},{7,8},{8,9},{9,10},{10,1... | collective-permute-start | bytes 3145736 | tf_op jit(solution)/shard_map/ppermute | solution.py:439
  13.8 3.4 %collective-permute-start = (s32[34]{0:T(128)S(1)}, s32[34]{0:T(128)S(1)}, u32[]{:S(2)}, u32[]{:S(2)}) collective-permute-start(s32[34]{0:T(128)S(1)} %pad_add_fusion.scal_ref), channel_id=1, source_target_pairs={{0,1},{1,2},{2,3},{3,4},{4,5},{5,6},{6,7},{7,8},{8,9},{9,10},{10,1... | collective-permute-start | bytes 416 | tf_op jit(solution)/shard_map/ppermute | solution.py:439
  17.2 3.2 %collective-permute-start.1 = (s32[34]{0:T(128)S(1)}, s32[34]{0:T(128)S(1)}, u32[]{:S(2)}, u32[]{:S(2)}) collective-permute-start(s32[34]{0:T(128)S(1)} %pad_add_fusion.scal_ref), channel_id=1, source_target_pairs={{0,2},{1,3},{2,4},{3,5},{4,6},{5,7},{6,8},{7,9},{8,10},{9,11},{10,... | collective-permute-start | bytes 416 | tf_op jit(solution)/shard_map/ppermute | solution.py:439
  23.4 9.7 %patterns_own.1 = (f32[2,16,192,128]{3,2,1,0:T(8,128)}, f32[1152,128]{1,0:T(8,128)}) custom-call(s32[34]{0:T(128)} %copy-done.9, f32[2,128,2048]{2,1,0:T(8,128)} %refs_1_.3, f32[2,64,2048]{2,1,0:T(8,128)} %collective-permute-done.5.refs_1_.refs_2_, f32[16,128,128]{2,1,0:T(8,128)} %refs_4_.2, f32[2,4,128,128]{3,2,1,0:T(8,128)} %probe_hbm.1, ...), custom_call_target="tpu_custom_call" | custom-call | flops 1000 | bytes 1024 | tf_op jit(solution)/shard_map/patterns_own/pallas_call | solution.py:307
  35.2 15.6 %patterns_above.1 = (f32[2,16,128,128]{3,2,1,0:T(8,128)}, f32[2,16,128,128]{3,2,1,0:T(8,128)}, f32[576,128]{1,0:T(8,128)}, f32[576,128]{1,0:T(8,128)}) custom-call(s32[68]{0:T(128)} %concatenate.16.scal_ref, f32[2,64,2048]{2,1,0:T(8,128)} %copy-done.3, f32[2,128,2048]{2,1,0:T(8,128)} %refs_1_.3, f32[2,16,192,128]{3,2,1,0:T(8,128)} %get-tuple-element.43.refs_2_, ...), custom_call_target="tpu_custom_call" | custom-call | flops 1000000000 | bytes 1024 | tf_op jit(solution)/shard_map/patterns_above/pallas_call | solution.py:307
  52.8 2.5 %collective-permute-start.7 = (f32[2,16,128,128]{3,2,1,0:T(8,128)}, f32[2,16,128,128]{3,2,1,0:T(8,128)}, u32[]{:S(2)}, u32[]{:S(2)}) collective-permute-start(f32[2,16,128,128]{3,2,1,0:T(8,128)} %get-tuple-element.47.refs_3_), channel_id=1, source_target_pairs={{1,0},{2,1},{3,2},{4,3},{5,4},{6,5},{7,6},{8,7},{9,8},{10,9},{11,1... | collective-permute-start | bytes 6291464 | tf_op jit(solution)/shard_map/ppermute | solution.py:439
  56.0 8.5 %light.2 = (f32[2,16,256,128]{3,2,1,0:T(8,128)}, f32[16,256,128]{2,1,0:T(8,128)}) custom-call(s32[136]{0:T(256)} %concatenate.17.scal_ref, f32[2,4,128,128]{3,2,1,0:T(8,128)} %probe_hbm.1, f32[2,64,2048]{2,1,0:T(8,128)} %copy-done.3, f32[2,128,2048]{2,1,0:T(8,128)} %refs_1_.3, f32[2,64,2048]{2,1,0:T(8,128)} %collective-permute-done.5.refs_1_.refs_2_, ...), custom_call_target="tpu_custom_call" | custom-call | flops 2560000 | bytes 16777216 | tf_op jit(solution)/shard_map/light/pallas_call | solution.py:390
  64.5 11.6 %collective-permute-done.6.refs_2_ = f32[2,16,128,128]{3,2,1,0:T(8,128)S(1)} collective-permute-done((f32[2,16,128,128]{3,2,1,0:T(8,128)}, f32[2,16,128,128]{3,2,1,0:T(8,128)S(1)}, u32[]{:S(2)}, u32[]{:S(2)}) %collective-permute-start.6) | collective-permute-done | bytes 2097184 | tf_op jit(solution)/shard_map/ppermute | solution.py:439
  76.1 4.4 %collective-permute-done.7.refs_3_ = f32[2,16,128,128]{3,2,1,0:T(8,128)} collective-permute-done((f32[2,16,128,128]{3,2,1,0:T(8,128)}, f32[2,16,128,128]{3,2,1,0:T(8,128)}, u32[]{:S(2)}, u32[]{:S(2)}) %collective-permute-start.7) | collective-permute-done | bytes 2097184 | tf_op jit(solution)/shard_map/ppermute | solution.py:439
  82.1 16.1 %collective-permute-start.10 = (f32[144,128]{1,0:T(8,128)S(1)}, f32[144,128]{1,0:T(8,128)S(1)}, u32[]{:S(2)}, u32[]{:S(2)}) collective-permute-start(f32[144,128]{1,0:T(8,128)S(1)} %get-tuple-element.87), channel_id=1, source_target_pairs={{0,64},{1,65},{2,66},{3,67},{4,68},{5,69},{6,70},{7,71},{8,72},{9,... | collective-permute-start | bytes 221192 | tf_op jit(solution)/shard_map/ppermute | solution.py:451
  98.2 4.0 %collective-permute-start.11 = (f32[144,128]{1,0:T(8,128)S(1)}, f32[144,128]{1,0:T(8,128)S(1)}, u32[]{:S(2)}, u32[]{:S(2)}) collective-permute-start(f32[144,128]{1,0:T(8,128)S(1)} %get-tuple-element.86), channel_id=1, source_target_pairs={{0,96},{1,97},{2,98},{3,99},{4,100},{5,101},{6,102},{7,103},{8,104... | collective-permute-start | bytes 221192 | tf_op jit(solution)/shard_map/ppermute | solution.py:451
  102.7 3.3 %collective-permute-done.11 = f32[144,128]{1,0:T(8,128)S(1)} collective-permute-done((f32[144,128]{1,0:T(8,128)S(1)}, f32[144,128]{1,0:T(8,128)S(1)}, u32[]{:S(2)}, u32[]{:S(2)}) %collective-permute-start.11) | collective-permute-done | bytes 73760 | tf_op jit(solution)/shard_map/ppermute | solution.py:451
  106.8 2.6 %collective-permute-start.14 = (f32[144,128]{1,0:T(8,128)S(1)}, f32[144,128]{1,0:T(8,128)S(1)}, u32[]{:S(2)}, u32[]{:S(2)}) collective-permute-start(f32[144,128]{1,0:T(8,128)S(1)} %fusion.3), channel_id=1, source_target_pairs={{0,24},{1,25},{2,26},{3,27},{4,28},{5,29},{6,30},{7,31},{8,0},{9,1... | collective-permute-start | bytes 221192 | tf_op jit(solution)/shard_map/ppermute | solution.py:451
  109.4 2.5 %collective-permute-done.12 = f32[144,128]{1,0:T(8,128)S(1)} collective-permute-done((f32[144,128]{1,0:T(8,128)S(1)}, f32[144,128]{1,0:T(8,128)S(1)}, u32[]{:S(2)}, u32[]{:S(2)}) %collective-permute-start.12) | collective-permute-done | bytes 73760 | tf_op jit(solution)/shard_map/ppermute | solution.py:451
  112.6 7.1 %collective-permute-start.16 = (f32[144,128]{1,0:T(8,128)S(1)}, f32[144,128]{1,0:T(8,128)S(1)}, u32[]{:S(2)}, u32[]{:S(2)}) collective-permute-start(f32[144,128]{1,0:T(8,128)S(1)} %add_add_fusion.3), channel_id=1, source_target_pairs={{0,4},{1,5},{2,6},{3,7},{4,0},{5,1},{6,2},{7,3},{8,12},{9,13},{10,... | collective-permute-start | bytes 221192 | tf_op jit(solution)/shard_map/ppermute | solution.py:451
  123.6 2.2 collective-permute-start.19
  129.2 5.3 %collective-permute-start.21 = (f32[576,128]{1,0:T(8,128)S(1)}, f32[576,128]{1,0:T(8,128)S(1)}, u32[]{:S(2)}, u32[]{:S(2)}) collective-permute-start(f32[576,128]{1,0:T(8,128)S(1)} %bitcast.78), channel_id=1, source_target_pairs={{0,1},{1,0},{2,3},{3,2},{4,5},{5,4},{6,7},{7,6},{8,9},{9,8},{10,11... | collective-permute-start | bytes 884744 | tf_op jit(solution)/shard_map/ppermute | solution.py:451
  136.7 19.4 %patterns_both.1 = (f32[2,16,64,128]{3,2,1,0:T(8,128)}, f32[2,16,64,128]{3,2,1,0:T(8,128)}, f32[2,16,128,128]{3,2,1,0:T(8,128)}, f32[576,128]{1,0:T(8,128)}, f32...) custom-call(s32[68]{0:T(128)} %concatenate.16.scal_ref, f32[2,16,256,128]{3,2,1,0:T(8,128)} %get-tuple-element.54.refs_0_, ...), custom_call_target="tpu_custom_call" | custom-call | flops 1000000000 | bytes 1024 | tf_op jit(solution)/shard_map/patterns_both/pallas_call | solution.py:307
  158.0 2.5 %collective-permute-start.23 = (f32[2,16,64,128]{3,2,1,0:T(8,128)}, f32[2,16,64,128]{3,2,1,0:T(8,128)S(1)}, u32[]{:S(2)}, u32[]{:S(2)}) collective-permute-start(f32[2,16,64,128]{3,2,1,0:T(8,128)} %get-tuple-element.61), channel_id=1, source_target_pairs={{1,0},{2,1},{3,2},{4,3},{5,4},{6,5},{7,6},{8,7},{9,8},{10,9},{11,1... | collective-permute-start | bytes 3145736 | tf_op jit(solution)/shard_map/ppermute | solution.py:439
  161.2 6.8 %light.3 = (f32[2,16,128,128]{3,2,1,0:T(8,128)}, f32[16,128,128]{2,1,0:T(8,128)}) custom-call(s32[68]{0:T(128)} %concatenate.18.scal_ref, f32[2,4,128,128]{3,2,1,0:T(8,128)} %divide_subtract_fusion.1.refs_6_.probe_hbm, f32[2,16,128,128]{3,2,1,0:T(8,128)} %get-tuple-element.62.refs_0_, f32[2,16,128,128]{3,2,1,0:T(8,128)} %get-tuple-element.63.refs_1_), custom_call_target="tpu_custom_call" | custom-call | flops 1280000 | bytes 16777216 | tf_op jit(solution)/shard_map/light/pallas_call | solution.py:390
  170.1 4.3 %collective-permute-done.23.below_in = f32[2,16,64,128]{3,2,1,0:T(8,128)S(1)} collective-permute-done((f32[2,16,64,128]{3,2,1,0:T(8,128)}, f32[2,16,64,128]{3,2,1,0:T(8,128)S(1)}, u32[]{:S(2)}, u32[]{:S(2)}) %collective-permute-start.23) | collective-permute-done | bytes 1048608 | tf_op jit(solution)/shard_map/ppermute | solution.py:439
  176.0 3.4 %collective-permute-start.25 = (f32[144,128]{1,0:T(8,128)S(1)}, f32[144,128]{1,0:T(8,128)S(1)}, u32[]{:S(2)}, u32[]{:S(2)}) collective-permute-start(f32[144,128]{1,0:T(8,128)S(1)} %get-tuple-element.82), channel_id=1, source_target_pairs={{0,32},{1,33},{2,34},{3,35},{4,36},{5,37},{6,38},{7,39},{8,40},{9,... | collective-permute-start | bytes 221192 | tf_op jit(solution)/shard_map/ppermute | solution.py:451
  179.4 8.6 %collective-permute-start.26 = (f32[144,128]{1,0:T(8,128)S(1)}, f32[144,128]{1,0:T(8,128)S(1)}, u32[]{:S(2)}, u32[]{:S(2)}) collective-permute-start(f32[144,128]{1,0:T(8,128)S(1)} %get-tuple-element.84), channel_id=1, source_target_pairs={{0,64},{1,65},{2,66},{3,67},{4,68},{5,69},{6,70},{7,71},{8,72},{9,... | collective-permute-start | bytes 221192 | tf_op jit(solution)/shard_map/ppermute | solution.py:451
  191.6 3.2 %collective-permute-start.28 = (f32[144,128]{1,0:T(8,128)S(1)}, f32[144,128]{1,0:T(8,128)S(1)}, u32[]{:S(2)}, u32[]{:S(2)}) collective-permute-start(f32[144,128]{1,0:T(8,128)S(1)} %fusion.1), channel_id=1, source_target_pairs={{0,8},{1,9},{2,10},{3,11},{4,12},{5,13},{6,14},{7,15},{8,16},{9,17... | collective-permute-start | bytes 221192 | tf_op jit(solution)/shard_map/ppermute | solution.py:451
  194.8 2.5 %collective-permute-start.30 = (f32[144,128]{1,0:T(8,128)S(1)}, f32[144,128]{1,0:T(8,128)S(1)}, u32[]{:S(2)}, u32[]{:S(2)}) collective-permute-start(f32[144,128]{1,0:T(8,128)S(1)} %fusion.1), channel_id=1, source_target_pairs={{0,24},{1,25},{2,26},{3,27},{4,28},{5,29},{6,30},{7,31},{8,0},{9,1... | collective-permute-start | bytes 221192 | tf_op jit(solution)/shard_map/ppermute | solution.py:451
  199.6 5.6 %collective-permute-start.32 = (f32[144,128]{1,0:T(8,128)S(1)}, f32[144,128]{1,0:T(8,128)S(1)}, u32[]{:S(2)}, u32[]{:S(2)}) collective-permute-start(f32[144,128]{1,0:T(8,128)S(1)} %add_add_fusion.1), channel_id=1, source_target_pairs={{0,4},{1,5},{2,6},{3,7},{4,0},{5,1},{6,2},{7,3},{8,12},{9,13},{10,... | collective-permute-start | bytes 221192 | tf_op jit(solution)/shard_map/ppermute | solution.py:451
  209.2 4.4 %last.1 = f32[2,128,2048]{2,1,0:T(8,128)} custom-call(f32[2,16,128,128]{3,2,1,0:T(8,128)} %get-tuple-element.68.pre, f32[16,128,128]{2,1,0:T(8,128)} %get-tuple-element.69.share, f32[2,16,64,128]{3,2,1,0:T(8,128)} %copy-done.5, f32[2,16,64,128]{3,2,1,0:T(8,128)} %copy-done.6), custom_call_target="tpu_custom_call" | custom-call | flops 1048576 | bytes 7340032 | tf_op jit(solution)/shard_map/last/pallas_call | solution.py:425
  213.5 4.1 %collective-permute-start.35 = (f32[144,128]{1,0:T(8,128)S(1)}, f32[144,128]{1,0:T(8,128)S(1)}, u32[]{:S(2)}, u32[]{:S(2)}) collective-permute-start(f32[144,128]{1,0:T(8,128)S(1)} %get-tuple-element.77), channel_id=1, source_target_pairs={{0,64},{1,65},{2,66},{3,67},{4,68},{5,69},{6,70},{7,71},{8,72},{9,... | collective-permute-start | bytes 221192 | tf_op jit(solution)/shard_map/ppermute | solution.py:451
  220.8 4.3 %collective-permute-start.37 = (f32[576,128]{1,0:T(8,128)S(1)}, f32[576,128]{1,0:T(8,128)S(1)}, u32[]{:S(2)}, u32[]{:S(2)}) collective-permute-start(f32[576,128]{1,0:T(8,128)S(1)} %bitcast.76), channel_id=1, source_target_pairs={{0,1},{1,0},{2,3},{3,2},{4,5},{5,4},{6,7},{7,6},{8,9},{9,8},{10,11... | collective-permute-start | bytes 884744 | tf_op jit(solution)/shard_map/ppermute | solution.py:451
  (112 shorter events, 42.0 us)
Async XLA Ops:
  3.7 17.7 %collective-permute-start.5 = (f32[2,64,2048]{2,1,0:T(8,128)}, f32[2,64,2048]{2,1,0:T(8,128)}, u32[]{:S(2)}, u32[]{:S(2)}) collective-permute-start(f32[2,64,2048]{2,1,0:T(8,128)} %get-tuple-element.80), channel_id=1, source_target_pairs={{1,0},{2,1},{3,2},{4,3},{5,4},{6,5},{7,6},{8,7},{9,8},{10,9},{11,1... | collective-permute-start | bytes 3145736 | tf_op jit(solution)/shard_map/ppermute | solution.py:439
  7.1 26.8 %collective-permute-start.3 = (f32[2,64,2048]{2,1,0:T(8,128)}, f32[2,64,2048]{2,1,0:T(8,128)S(1)}, u32[]{:S(2)}, u32[]{:S(2)}) collective-permute-start(f32[2,64,2048]{2,1,0:T(8,128)} %get-tuple-element.81), channel_id=1, source_target_pairs={{0,1},{1,2},{2,3},{3,4},{4,5},{5,6},{6,7},{7,8},{8,9},{9,10},{10,1... | collective-permute-start | bytes 3145736 | tf_op jit(solution)/shard_map/ppermute | solution.py:439
  10.6 23.3 %collective-permute-start.4 = (f32[16,128,128]{2,1,0:T(8,128)}, f32[16,128,128]{2,1,0:T(8,128)S(1)}, u32[]{:S(2)}, u32[]{:S(2)}) collective-permute-start(f32[16,128,128]{2,1,0:T(8,128)} %refs_4_.2), channel_id=1, source_target_pairs={{0,1},{1,2},{2,3},{3,4},{4,5},{5,6},{6,7},{7,8},{8,9},{9,10},{10,1... | collective-permute-start | bytes 3145736 | tf_op jit(solution)/shard_map/ppermute | solution.py:439
  13.8 20.1 %collective-permute-start = (s32[34]{0:T(128)S(1)}, s32[34]{0:T(128)S(1)}, u32[]{:S(2)}, u32[]{:S(2)}) collective-permute-start(s32[34]{0:T(128)S(1)} %pad_add_fusion.scal_ref), channel_id=1, source_target_pairs={{0,1},{1,2},{2,3},{3,4},{4,5},{5,6},{6,7},{7,8},{8,9},{9,10},{10,1... | collective-permute-start | bytes 416 | tf_op jit(solution)/shard_map/ppermute | solution.py:439
  17.2 16.7 %collective-permute-start.1 = (s32[34]{0:T(128)S(1)}, s32[34]{0:T(128)S(1)}, u32[]{:S(2)}, u32[]{:S(2)}) collective-permute-start(s32[34]{0:T(128)S(1)} %pad_add_fusion.scal_ref), channel_id=1, source_target_pairs={{0,2},{1,3},{2,4},{3,5},{4,6},{5,7},{6,8},{7,9},{8,10},{9,11},{10,... | collective-permute-start | bytes 416 | tf_op jit(solution)/shard_map/ppermute | solution.py:439
  21.4 12.4 %collective-permute-start.2 = (s32[34]{0:T(128)S(1)}, s32[34]{0:T(128)S(1)}, u32[]{:S(2)}, u32[]{:S(2)}) collective-permute-start(s32[34]{0:T(128)S(1)} %pad_add_fusion.scal_ref), channel_id=1, source_target_pairs={{1,0},{2,1},{3,2},{4,3},{5,4},{6,5},{7,6},{8,7},{9,8},{10,9},{11,1... | collective-permute-start | bytes 416 | tf_op jit(solution)/shard_map/ppermute | solution.py:439
  50.9 25.2 %collective-permute-start.6 = (f32[2,16,128,128]{3,2,1,0:T(8,128)}, f32[2,16,128,128]{3,2,1,0:T(8,128)S(1)}, u32[]{:S(2)}, u32[]{:S(2)}) collective-permute-start(f32[2,16,128,128]{3,2,1,0:T(8,128)} %get-tuple-element.46.refs_4_), channel_id=1, source_target_pairs={{0,1},{1,2},{2,3},{3,4},{4,5},{5,6},{6,7},{7,8},{8,9},{9,10},{10,1... | collective-permute-start | bytes 6291464 | tf_op jit(solution)/shard_map/ppermute | solution.py:439
  52.8 27.7 %collective-permute-start.7 = (f32[2,16,128,128]{3,2,1,0:T(8,128)}, f32[2,16,128,128]{3,2,1,0:T(8,128)}, u32[]{:S(2)}, u32[]{:S(2)}) collective-permute-start(f32[2,16,128,128]{3,2,1,0:T(8,128)} %get-tuple-element.47.refs_3_), channel_id=1, source_target_pairs={{1,0},{2,1},{3,2},{4,3},{5,4},{6,5},{7,6},{8,7},{9,8},{10,9},{11,1... | collective-permute-start | bytes 6291464 | tf_op jit(solution)/shard_map/ppermute | solution.py:439
  82.1 20.6 %collective-permute-start.10 = (f32[144,128]{1,0:T(8,128)S(1)}, f32[144,128]{1,0:T(8,128)S(1)}, u32[]{:S(2)}, u32[]{:S(2)}) collective-permute-start(f32[144,128]{1,0:T(8,128)S(1)} %get-tuple-element.87), channel_id=1, source_target_pairs={{0,64},{1,65},{2,66},{3,67},{4,68},{5,69},{6,70},{7,71},{8,72},{9,... | collective-permute-start | bytes 221192 | tf_op jit(solution)/shard_map/ppermute | solution.py:451
  98.2 7.8 %collective-permute-start.11 = (f32[144,128]{1,0:T(8,128)S(1)}, f32[144,128]{1,0:T(8,128)S(1)}, u32[]{:S(2)}, u32[]{:S(2)}) collective-permute-start(f32[144,128]{1,0:T(8,128)S(1)} %get-tuple-element.86), channel_id=1, source_target_pairs={{0,96},{1,97},{2,98},{3,99},{4,100},{5,101},{6,102},{7,103},{8,104... | collective-permute-start | bytes 221192 | tf_op jit(solution)/shard_map/ppermute | solution.py:451
  102.2 4.4 %collective-permute-start.9 = (f32[144,128]{1,0:T(8,128)S(1)}, f32[144,128]{1,0:T(8,128)S(1)}, u32[]{:S(2)}, u32[]{:S(2)}) collective-permute-start(f32[144,128]{1,0:T(8,128)S(1)} %get-tuple-element.85), channel_id=1, source_target_pairs={{0,32},{1,33},{2,34},{3,35},{4,36},{5,37},{6,38},{7,39},{8,40},{9,... | collective-permute-start | bytes 221192 | tf_op jit(solution)/shard_map/ppermute | solution.py:451
  106.7 5.3 %collective-permute-start.12 = (f32[144,128]{1,0:T(8,128)S(1)}, f32[144,128]{1,0:T(8,128)S(1)}, u32[]{:S(2)}, u32[]{:S(2)}) collective-permute-start(f32[144,128]{1,0:T(8,128)S(1)} %fusion.3), channel_id=1, source_target_pairs={{0,8},{1,9},{2,10},{3,11},{4,12},{5,13},{6,14},{7,15},{8,16},{9,17... | collective-permute-start | bytes 221192 | tf_op jit(solution)/shard_map/ppermute | solution.py:451
  106.7 5.2 %collective-permute-start.13 = (f32[144,128]{1,0:T(8,128)S(1)}, f32[144,128]{1,0:T(8,128)S(1)}, u32[]{:S(2)}, u32[]{:S(2)}) collective-permute-start(f32[144,128]{1,0:T(8,128)S(1)} %fusion.3), channel_id=1, source_target_pairs={{0,16},{1,17},{2,18},{3,19},{4,20},{5,21},{6,22},{7,23},{8,24},{9,... | collective-permute-start | bytes 221192 | tf_op jit(solution)/shard_map/ppermute | solution.py:451
  106.8 5.7 %collective-permute-start.14 = (f32[144,128]{1,0:T(8,128)S(1)}, f32[144,128]{1,0:T(8,128)S(1)}, u32[]{:S(2)}, u32[]{:S(2)}) collective-permute-start(f32[144,128]{1,0:T(8,128)S(1)} %fusion.3), channel_id=1, source_target_pairs={{0,24},{1,25},{2,26},{3,27},{4,28},{5,29},{6,30},{7,31},{8,0},{9,1... | collective-permute-start | bytes 221192 | tf_op jit(solution)/shard_map/ppermute | solution.py:451
  112.5 7.7 %collective-permute-start.15 = (f32[144,128]{1,0:T(8,128)S(1)}, f32[144,128]{1,0:T(8,128)S(1)}, u32[]{:S(2)}, u32[]{:S(2)}) collective-permute-start(f32[144,128]{1,0:T(8,128)S(1)} %add_add_fusion.3), channel_id=1, source_target_pairs={{0,2},{1,3},{2,4},{3,5},{4,6},{5,7},{6,0},{7,1},{8,10},{9,11},{10,... | collective-permute-start | bytes 221192 | tf_op jit(solution)/shard_map/ppermute | solution.py:451
  112.6 9.7 %collective-permute-start.16 = (f32[144,128]{1,0:T(8,128)S(1)}, f32[144,128]{1,0:T(8,128)S(1)}, u32[]{:S(2)}, u32[]{:S(2)}) collective-permute-start(f32[144,128]{1,0:T(8,128)S(1)} %add_add_fusion.3), channel_id=1, source_target_pairs={{0,4},{1,5},{2,6},{3,7},{4,0},{5,1},{6,2},{7,3},{8,12},{9,13},{10,... | collective-permute-start | bytes 221192 | tf_op jit(solution)/shard_map/ppermute | solution.py:451
  123.4 5.3 %collective-permute-start.18 = (f32[144,128]{1,0:T(8,128)S(1)}, f32[144,128]{1,0:T(8,128)S(1)}, u32[]{:S(2)}, u32[]{:S(2)}) collective-permute-start(f32[144,128]{1,0:T(8,128)S(1)} %get-tuple-element.79), channel_id=1, source_target_pairs={{0,32},{1,33},{2,34},{3,35},{4,36},{5,37},{6,38},{7,39},{8,40},{9,... | collective-permute-start | bytes 221192 | tf_op jit(solution)/shard_map/ppermute | solution.py:451
  123.6 5.1 %collective-permute-start.19 = (f32[144,128]{1,0:T(8,128)S(1)}, f32[144,128]{1,0:T(8,128)S(1)}, u32[]{:S(2)}, u32[]{:S(2)}) collective-permute-start(f32[144,128]{1,0:T(8,128)S(1)} %get-tuple-element.79), channel_id=1, source_target_pairs={{0,64},{1,65},{2,66},{3,67},{4,68},{5,69},{6,70},{7,71},{8,72},{9,... | collective-permute-start | bytes 221192 | tf_op jit(solution)/shard_map/ppermute | solution.py:451
  129.2 6.5 %collective-permute-start.21 = (f32[576,128]{1,0:T(8,128)S(1)}, f32[576,128]{1,0:T(8,128)S(1)}, u32[]{:S(2)}, u32[]{:S(2)}) collective-permute-start(f32[576,128]{1,0:T(8,128)S(1)} %bitcast.78), channel_id=1, source_target_pairs={{0,1},{1,0},{2,3},{3,2},{4,5},{5,4},{6,7},{7,6},{8,9},{9,8},{10,11... | collective-permute-start | bytes 884744 | tf_op jit(solution)/shard_map/ppermute | solution.py:451
  156.1 14.0 %collective-permute-start.22 = (f32[2,16,64,128]{3,2,1,0:T(8,128)}, f32[2,16,64,128]{3,2,1,0:T(8,128)S(1)}, u32[]{:S(2)}, u32[]{:S(2)}) collective-permute-start(f32[2,16,64,128]{3,2,1,0:T(8,128)} %get-tuple-element.60), channel_id=1, source_target_pairs={{0,1},{1,2},{2,3},{3,4},{4,5},{5,6},{6,7},{7,8},{8,9},{9,10},{10,1... | collective-permute-start | bytes 3145736 | tf_op jit(solution)/shard_map/ppermute | solution.py:439
  158.0 16.3 %collective-permute-start.23 = (f32[2,16,64,128]{3,2,1,0:T(8,128)}, f32[2,16,64,128]{3,2,1,0:T(8,128)S(1)}, u32[]{:S(2)}, u32[]{:S(2)}) collective-permute-start(f32[2,16,64,128]{3,2,1,0:T(8,128)} %get-tuple-element.61), channel_id=1, source_target_pairs={{1,0},{2,1},{3,2},{4,3},{5,4},{6,5},{7,6},{8,7},{9,8},{10,9},{11,1... | collective-permute-start | bytes 3145736 | tf_op jit(solution)/shard_map/ppermute | solution.py:439
  176.0 13.2 %collective-permute-start.25 = (f32[144,128]{1,0:T(8,128)S(1)}, f32[144,128]{1,0:T(8,128)S(1)}, u32[]{:S(2)}, u32[]{:S(2)}) collective-permute-start(f32[144,128]{1,0:T(8,128)S(1)} %get-tuple-element.82), channel_id=1, source_target_pairs={{0,32},{1,33},{2,34},{3,35},{4,36},{5,37},{6,38},{7,39},{8,40},{9,... | collective-permute-start | bytes 221192 | tf_op jit(solution)/shard_map/ppermute | solution.py:451
  179.4 11.9 %collective-permute-start.26 = (f32[144,128]{1,0:T(8,128)S(1)}, f32[144,128]{1,0:T(8,128)S(1)}, u32[]{:S(2)}, u32[]{:S(2)}) collective-permute-start(f32[144,128]{1,0:T(8,128)S(1)} %get-tuple-element.84), channel_id=1, source_target_pairs={{0,64},{1,65},{2,66},{3,67},{4,68},{5,69},{6,70},{7,71},{8,72},{9,... | collective-permute-start | bytes 221192 | tf_op jit(solution)/shard_map/ppermute | solution.py:451
  191.6 5.7 %collective-permute-start.28 = (f32[144,128]{1,0:T(8,128)S(1)}, f32[144,128]{1,0:T(8,128)S(1)}, u32[]{:S(2)}, u32[]{:S(2)}) collective-permute-start(f32[144,128]{1,0:T(8,128)S(1)} %fusion.1), channel_id=1, source_target_pairs={{0,8},{1,9},{2,10},{3,11},{4,12},{5,13},{6,14},{7,15},{8,16},{9,17... | collective-permute-start | bytes 221192 | tf_op jit(solution)/shard_map/ppermute | solution.py:451
  194.8 4.7 %collective-permute-start.29 = (f32[144,128]{1,0:T(8,128)S(1)}, f32[144,128]{1,0:T(8,128)S(1)}, u32[]{:S(2)}, u32[]{:S(2)}) collective-permute-start(f32[144,128]{1,0:T(8,128)S(1)} %fusion.1), channel_id=1, source_target_pairs={{0,16},{1,17},{2,18},{3,19},{4,20},{5,21},{6,22},{7,23},{8,24},{9,... | collective-permute-start | bytes 221192 | tf_op jit(solution)/shard_map/ppermute | solution.py:451
  194.8 4.7 %collective-permute-start.30 = (f32[144,128]{1,0:T(8,128)S(1)}, f32[144,128]{1,0:T(8,128)S(1)}, u32[]{:S(2)}, u32[]{:S(2)}) collective-permute-start(f32[144,128]{1,0:T(8,128)S(1)} %fusion.1), channel_id=1, source_target_pairs={{0,24},{1,25},{2,26},{3,27},{4,28},{5,29},{6,30},{7,31},{8,0},{9,1... | collective-permute-start | bytes 221192 | tf_op jit(solution)/shard_map/ppermute | solution.py:451
  199.5 7.4 %collective-permute-start.31 = (f32[144,128]{1,0:T(8,128)S(1)}, f32[144,128]{1,0:T(8,128)S(1)}, u32[]{:S(2)}, u32[]{:S(2)}) collective-permute-start(f32[144,128]{1,0:T(8,128)S(1)} %add_add_fusion.1), channel_id=1, source_target_pairs={{0,2},{1,3},{2,4},{3,5},{4,6},{5,7},{6,0},{7,1},{8,10},{9,11},{10,... | collective-permute-start | bytes 221192 | tf_op jit(solution)/shard_map/ppermute | solution.py:451
  199.6 8.1 %collective-permute-start.32 = (f32[144,128]{1,0:T(8,128)S(1)}, f32[144,128]{1,0:T(8,128)S(1)}, u32[]{:S(2)}, u32[]{:S(2)}) collective-permute-start(f32[144,128]{1,0:T(8,128)S(1)} %add_add_fusion.1), channel_id=1, source_target_pairs={{0,4},{1,5},{2,6},{3,7},{4,0},{5,1},{6,2},{7,3},{8,12},{9,13},{10,... | collective-permute-start | bytes 221192 | tf_op jit(solution)/shard_map/ppermute | solution.py:451
  205.2 3.8 %collective-permute-start.33 = (f32[144,128]{1,0:T(8,128)S(1)}, f32[144,128]{1,0:T(8,128)S(1)}, u32[]{:S(2)}, u32[]{:S(2)}) collective-permute-start(f32[144,128]{1,0:T(8,128)S(1)} %add_add_fusion.1), channel_id=1, source_target_pairs={{0,6},{1,7},{2,0},{3,1},{4,2},{5,3},{6,4},{7,5},{8,14},{9,15},{10,... | collective-permute-start | bytes 221192 | tf_op jit(solution)/shard_map/ppermute | solution.py:451
  209.0 8.6 %collective-permute-start.34 = (f32[144,128]{1,0:T(8,128)S(1)}, f32[144,128]{1,0:T(8,128)S(1)}, u32[]{:S(2)}, u32[]{:S(2)}) collective-permute-start(f32[144,128]{1,0:T(8,128)S(1)} %get-tuple-element.77), channel_id=1, source_target_pairs={{0,32},{1,33},{2,34},{3,35},{4,36},{5,37},{6,38},{7,39},{8,40},{9,... | collective-permute-start | bytes 221192 | tf_op jit(solution)/shard_map/ppermute | solution.py:451
  213.5 5.8 %collective-permute-start.35 = (f32[144,128]{1,0:T(8,128)S(1)}, f32[144,128]{1,0:T(8,128)S(1)}, u32[]{:S(2)}, u32[]{:S(2)}) collective-permute-start(f32[144,128]{1,0:T(8,128)S(1)} %get-tuple-element.77), channel_id=1, source_target_pairs={{0,64},{1,65},{2,66},{3,67},{4,68},{5,69},{6,70},{7,71},{8,72},{9,... | collective-permute-start | bytes 221192 | tf_op jit(solution)/shard_map/ppermute | solution.py:451
  220.8 5.5 %collective-permute-start.37 = (f32[576,128]{1,0:T(8,128)S(1)}, f32[576,128]{1,0:T(8,128)S(1)}, u32[]{:S(2)}, u32[]{:S(2)}) collective-permute-start(f32[576,128]{1,0:T(8,128)S(1)} %bitcast.76), channel_id=1, source_target_pairs={{0,1},{1,0},{2,3},{3,2},{4,5},{5,4},{6,7},{7,6},{8,9},{9,8},{10,11... | collective-permute-start | bytes 884744 | tf_op jit(solution)/shard_map/ppermute | solution.py:451
  (19 other events, 288.8 us)

commit v3 on v2

--- a/solution.py
+++ b/solution.py
@@ -12,7 +12,9 @@
 SIGMA = 0.5
 NSLOT, OFF_SLOT, OFF_PAIR = 2, 1, 0
 STEP_TILES = 4
-VMEM_LIMIT = 56 * 1024 * 1024
+MIB = 1024 * 1024
+PATTERN_LIMITS = {"own": 20 * MIB, "above": 24 * MIB, "both": 30 * MIB}
+VMEM_LIMIT = 20 * MIB
 
 
 def split_np(w):
@@ -55,7 +57,7 @@
 
 def load_columns(ref, frame, rows, sems):
     return [
-        pltpu.make_async_copy(ref.at[:, :, pl.ds(t * 128, 128)], frame.at[:, t, pl.ds(rows[0], rows[1] - rows[0]), :], sems.at[t])
+        pltpu.make_async_copy(ref.at[:, pl.ds(0, rows[1] - rows[0]), pl.ds(t * 128, 128)], frame.at[:, t, pl.ds(rows[0], rows[1] - rows[0]), :], sems.at[t])
         for t in range(frame.shape[1])
     ]
 
@@ -70,40 +72,51 @@
         copy.wait()
 
 
-def pattern_kernel(stage, scal_ref, *refs):
+def pattern_kernel(stage, *refs):
     refs = list(refs)
     take = lambda n: [refs.pop(0) for _ in range(n)]
-    objects = take({"own": 2, "above": 2, "both": 4}[stage])
+    scals = take(1 if stage == "own" else 2)
+    objects = take({"own": 2, "above": 2, "both": 1}[stage])
     before = take(2) if stage == "above" else None
     amps = take(2 if stage == "both" else 1)
-    whole = take(5)
-    outs = take({"own": 2, "above": 4, "both": 6}[stage])
-    frame, grad, terms_ref, amp_ref, probe_ref, rf_ref, rb_ref, lf_ref, lb_ref, order, in_sems, tile_sems, out_sems = take(13)
+    whole = take(2)
+    outs = take({"own": 2, "above": 4, "both": 5}[stage])
+    frame, grad, terms_ref, order, tile_sems, out_sems = take(6)
+    mats_ref = take(1)[0]
+    moves = [(whole[1], mats_ref)]
+    if stage == "own":
+        grad, terms_ref = outs
+        moves += list(zip(whole[:1] + amps, refs))
+        whole, amps = refs[:1], refs[1:]
+    probe_ref = whole[0]
+    size = mats_ref.shape[1]
+    rf_ref, rb_ref = (mats_ref.at[pl.ds(3 * size * k, 3 * size)] for k in range(2))
+    lf_ref, lb_ref = ([mats_ref.at[pl.ds(size * (6 + 2 * k + n), size)] for n in range(2)] for k in range(2))
     tiles, strip = frame.shape[1], frame.shape[2] // 2
     quarter = strip // 2
     nmodes, length = probe_ref.shape[1], probe_ref.shape[2]
-    slots = amp_ref.shape[0] // len(amps)
-    width = 2 * slots + 2
+    slots = amps[0].shape[0]
     owners = {"own": (0,), "above": (1,), "both": (0, 1)}[stage]
 
-    moves = list(zip(whole, (probe_ref, rf_ref, rb_ref, lf_ref, lb_ref)))
-    moves += [(ref, amp_ref.at[pl.ds(k * slots, slots)]) for k, ref in enumerate(amps)]
-    if stage == "both":
-        share, extra = take(2)
-        moves += [(objects[0], frame), (objects[1], share)]
-        moves += [(objects[2 + k], extra.at[:, :, pl.ds(k * strip, strip)]) for k in range(2)]
-        copies = []
-    elif stage == "own":
+    copies = []
+    if stage == "own":
         copies = load_columns(objects[0], frame, (quarter, 3 * quarter), tile_sems.at[0])
         copies += load_columns(objects[1], frame, (3 * quarter, 4 * quarter), tile_sems.at[1])
-    else:
+    elif stage == "above":
         copies = load_columns(objects[0], frame, (0, quarter), tile_sems.at[0])
         copies += load_columns(objects[1], frame, (quarter, 3 * quarter), tile_sems.at[1])
-        moves += [(before[0], grad.at[:, :, pl.ds(quarter, 3 * quarter)]), (before[1], terms_ref)]
-    copies += [pltpu.make_async_copy(src, dst, in_sems.at[k]) for k, (src, dst) in enumerate(moves)]
+    else:
+        copies = [pltpu.make_async_copy(objects[0], frame, tile_sems.at[0, 0])]
+    copies += [pltpu.make_async_copy(src, dst, out_sems.at[k]) for k, (src, dst) in enumerate(moves)]
     start_all(copies)
     if stage == "above":
-        grad[:, :, :quarter] = jnp.zeros((2, tiles, quarter, 128), jnp.float32)
+
+        def take_over(t, carry):
+            grad[:, t] = before[0][:, t]
+            return carry
+
+        lax.fori_loop(0, tiles, take_over, 0)
+        terms_ref[...] = before[1][...]
     else:
         grad[...] = jnp.zeros_like(grad)
         terms_ref[...] = jnp.zeros_like(terms_ref)
@@ -111,30 +124,30 @@
     for k, owner in enumerate(owners):
         for local in range(slots):
             order[chosen] = k * slots + local
-            low = scal_ref[owner * width + local] >= quarter
-            inside = (local < scal_ref[owner * width + 2 * slots]) & (low if owner else jnp.logical_not(low))
+            low = scals[owner][local] >= quarter
+            inside = (local < scals[owner][2 * slots]) & (low if owner else jnp.logical_not(low))
             chosen = chosen + inside.astype(jnp.int32)
     wait_all(copies)
-    late = []
-    if stage == "both":
-
-        def add_share(t, carry):
-            for part in range(2):
-                frame[part, t] -= extra[part, t] * share[t]
-            return carry
-
-        lax.fori_loop(0, tiles, add_share, 0)
-        late.append(pltpu.make_async_copy(frame.at[:, :, pl.ds(quarter, strip)], outs[5], out_sems.at[5]))
-        start_all(late)
+    def amplitude(slot, k, h):
+        if len(amps) == 1:
+            return amps[0][slot, pl.ds(k, h, stride=2), :]
+        local = slot % slots
+        return jnp.where(slot < slots, amps[0][local, pl.ds(k, h, stride=2), :], amps[1][local, pl.ds(k, h, stride=2), :])
+
     h = length // 2
     pairs = nmodes // 2
 
     def place(slot):
-        owner = slot // slots if len(owners) > 1 else owners[0]
-        at = owner * width + slot % slots
-        col = scal_ref[at + slots]
+        if len(owners) == 1:
+            row, col = (scals[owners[0]][slot + k * slots] for k in range(2))
+            row = row - owners[0] * strip
+        else:
+            local = slot % slots
+            first = slot < slots
+            row, col = (jnp.where(first, scals[0][local + k * slots], scals[1][local + k * slots]) for k in range(2))
+            row = jnp.where(first, row, row - strip)
         tile = jnp.minimum(col // 128, tiles - 2)
-        return scal_ref[at] + quarter - owner * strip, tile, col - tile * 128
+        return row + quarter, tile, col - tile * 128
 
     def stream(slot, shared, p):
         row, tile, shift = shared["place"]
@@ -159,7 +172,7 @@
         low = jnp.concatenate([jnp.concatenate([y[h:, :length] for y in mids], axis=1), jnp.concatenate([y[h:, length:] for y in mids], axis=1)], axis=0)
         sums = [jnp.concatenate(split(v), axis=0) for v in (top + low, top - low)]
         yield
-        fars = [dot(lf_ref[k], v) for k, v in enumerate(sums)]
+        fars = [dot(lf_ref[k][...], v) for k, v in enumerate(sums)]
         yield
         fars = [f[:length] + f[length:] for f in fars]
         sq = [f * f for f in fars]
@@ -170,12 +183,12 @@
             yield
         if "weight" not in shared:
             intensity = functools.reduce(lambda a, b: a + b, shared["power"])
-            amp = jnp.concatenate([amp_ref[slot, pl.ds(k, h, stride=2), :] for k in range(2)], axis=0)
+            amp = jnp.concatenate([amplitude(slot, k, h) for k in range(2)], axis=0)
             shared["weight"] = (1.0 - amp * lax.rsqrt(intensity + SIGMA)) * shared["alive"]
         w = jnp.concatenate([shared["weight"]] * 2, axis=1)
         ins = [split(f * jnp.concatenate([wk, wk], axis=0)) for f, wk in zip(fars, (w[:h], w[h:]))]
         yield
-        u, v = [dot(lb_ref[k], jnp.concatenate(x, axis=0)) for k, x in enumerate(ins)]
+        u, v = [dot(lb_ref[k][...], jnp.concatenate(x, axis=0)) for k, x in enumerate(ins)]
         yield
         u, v = u[:length] + u[length:], v[:length] + v[length:]
         a, b = u + v, u - v
@@ -227,21 +240,19 @@
 
     lax.fori_loop(0, (chosen + NSLOT - 1) // NSLOT, step, 0)
     if stage == "own":
-        moves = [(grad.at[:, :, pl.ds(quarter, 3 * quarter)], outs[0]), (terms_ref, outs[1])]
+        return
+    half = terms_ref.shape[0] // 2
+    core = scals[0][2 * slots + 1]
+    if stage == "above":
+        moves = [(grad.at[:, :, pl.ds(k * strip, strip)], outs[k]) for k in range(2)]
     else:
-        if stage == "above":
-            moves = [(grad.at[:, :, pl.ds(k * strip, strip)], outs[k]) for k in range(2)]
-        else:
-            cuts = ((0, quarter), (3 * quarter, quarter), (quarter, strip))
-            moves = [(grad.at[:, :, pl.ds(first, rows)], out) for (first, rows), out in zip(cuts, outs)]
-        half = terms_ref.shape[0] // 2
-        core = scal_ref[2 * slots + 1]
-        k = len(moves)
-        moves.append((terms_ref.at[pl.ds(pl.multiple_of(core * half, 8), half)], outs[k]))
-        moves.append((terms_ref.at[pl.ds(pl.multiple_of((1 - core) * half, 8), half)], outs[k + 1]))
+        cuts = ((0, quarter), (3 * quarter, quarter), (quarter, strip))
+        moves = [(grad.at[:, :, pl.ds(first, rows)], out) for (first, rows), out in zip(cuts, outs)]
     copies = [pltpu.make_async_copy(src, dst, out_sems.at[k]) for k, (src, dst) in enumerate(moves)]
+    copies.append(pltpu.make_async_copy(terms_ref.at[pl.ds(pl.multiple_of((1 - core) * half, 8), half)], outs[-1], out_sems.at[5]))
     start_all(copies)
-    wait_all(copies + late)
+    outs[len(moves)][...] = terms_ref[pl.ds(pl.multiple_of(core * half, 8), half), :]
+    wait_all(copies)
 
 
 def half_product(w_ref, which, x):
@@ -277,6 +288,10 @@
     return pl.BlockSpec(memory_space=pltpu.SMEM)
 
 
+def hbm():
+    return pl.BlockSpec(memory_space=pltpu.HBM)
+
+
 def anywhere():
     return pl.BlockSpec(memory_space=pl.ANY)
 
@@ -292,45 +307,44 @@
     minus, plus = dft_blocks(length)
     mh, ml = split_np(minus)
     ph, plo = split_np(plus)
-    mats = (np.concatenate([mh, mh, ml], axis=0), np.concatenate([ph, ph, plo], axis=0)) + tuple(half_blocks(length))
+    mats = np.concatenate([mh, mh, ml, ph, ph, plo] + [m.reshape(-1, 2 * length) for m in half_blocks(length)], axis=0)
     rows = (2 * nmodes + 1) * length
     half = f32(rows // 2, length)
     frame = (2, tiles, 2 * strip, 128)
     grads = [f32(2, tiles, n, 128) for n in (strip // 2, strip, 3 * strip // 2)]
     out_shape = {
-        "own": (grads[2], f32(rows, length)),
+        "own": (f32(*frame), f32(rows, length)),
         "above": (grads[1], grads[1], half, half),
-        "both": (grads[0], grads[0], grads[1], half, half, grads[1]),
+        "both": (grads[0], grads[0], grads[1], half, half),
     }[stage]
     arrays = list(objects) + list(before or ()) + list(amps) + [probe]
-    out_specs = tuple(vmem() if shape is half else anywhere() for shape in out_shape)
+    out_specs = tuple(vmem() if shape is half or stage == "own" else anywhere() for shape in out_shape)
+    if stage != "own":
+        out_specs = out_specs[:-1] + (hbm(),)
+    kinds = [hbm() if stage == "both" else anywhere()] * len(objects)
+    kinds += [anywhere() if stage == "own" else vmem()] * (len(arrays) - len(objects)) + [hbm()]
+    small = [pltpu.VMEM((8, 128), jnp.float32)] * 2
     return pl.pallas_call(
         functools.partial(pattern_kernel, stage),
         out_shape=out_shape,
-        in_specs=[smem()] + [anywhere()] * (len(arrays) + len(mats)),
+        in_specs=[smem()] * len(scalars) + kinds,
         out_specs=out_specs,
-        scratch_shapes=[
-            pltpu.VMEM(frame, jnp.float32),
-            pltpu.VMEM(frame, jnp.float32),
-            pltpu.VMEM((rows, length), jnp.float32),
-            pltpu.VMEM((len(amps) * slots,) + amps[0].shape[1:], jnp.float32),
-            pltpu.VMEM(probe.shape, jnp.float32),
-        ]
-        + [pltpu.VMEM(m.shape, jnp.bfloat16) for m in mats]
+        scratch_shapes=[pltpu.VMEM(frame, jnp.float32)]
+        + (small if stage == "own" else [pltpu.VMEM(frame, jnp.float32), pltpu.VMEM((rows, length), jnp.float32)])
         + [
             pltpu.SMEM((2 * slots + 1,), jnp.int32),
-            pltpu.SemaphoreType.DMA((11,)),
             pltpu.SemaphoreType.DMA((2, tiles)),
             pltpu.SemaphoreType.DMA((6,)),
         ]
-        + ([pltpu.VMEM(frame[1:], jnp.float32), pltpu.VMEM(frame, jnp.float32)] if stage == "both" else []),
-        compiler_params=pltpu.CompilerParams(vmem_limit_bytes=VMEM_LIMIT),
+        + [pltpu.VMEM(a.shape, a.dtype) for a in [mats] + ([probe] + list(amps) if stage == "own" else [])],
+        compiler_params=pltpu.CompilerParams(vmem_limit_bytes=PATTERN_LIMITS[stage]),
         cost_estimate=pl.CostEstimate(flops=flops, bytes_accessed=1024, transcendentals=0),
         name="patterns_" + stage,
-    )(scalars, *arrays, *map(jnp.asarray, mats))
-
-
-def light_kernel(nsets, strip, first, natural, scal_ref, probe_hbm, *refs):
+    )(*scalars, *arrays, jnp.asarray(mats))
+
+
+def light_kernel(nsets, strip, first, natural, *refs):
+    scals, probe_hbm, refs = refs[:nsets], refs[nsets], refs[nsets + 1 :]
     objects, grads = refs[: 3 if natural else 1], refs[3 if natural else 1 : 5 if natural else 2]
     pre_ref, share_ref, acc, frame, grad, probe_ref, tile_sems, sems = refs[len(objects) + len(grads) :]
     tiles = acc.shape[0]
@@ -343,7 +357,7 @@
         moves = [(ref, grad.at[:, :, pl.ds(k * strip, strip)]) for k, ref in enumerate(grads)]
     else:
         copies = []
-        moves = [(objects[0], frame), (grads[0], grad)]
+        moves = [(objects[0].at[:, :, pl.ds(strip // 2, rows)], frame), (grads[0], grad)]
     load = pltpu.make_async_copy(probe_hbm, probe_ref, sems.at[0])
     copies += [pltpu.make_async_copy(src, dst, sems.at[1 + k]) for k, (src, dst) in enumerate(moves)]
     start_all([load] + copies)
@@ -354,19 +368,18 @@
         term = probe_ref[0, m] * probe_ref[0, m] + probe_ref[1, m] * probe_ref[1, m]
         power = term if power is None else power + term
     wide0 = jnp.concatenate([power, jnp.zeros_like(power)], axis=1)
-    width = scal_ref.shape[0] // nsets
     for s in range(nsets):
 
         def step(slot, carry, s=s):
-            row = scal_ref[s * width + slot] + s * strip
-            col = scal_ref[s * width + 16 + slot]
+            row = scals[s][slot] + s * strip
+            col = scals[s][16 + slot]
             tile = jnp.minimum(col // 128, tiles - 2)
             wide = pltpu.roll(wide0, col - tile * 128, 1)
             for k in range(2):
                 acc[tile + k, pl.ds(row, length), :] += wide[:, k * 128 : (k + 1) * 128]
             return carry
 
-        lax.fori_loop(0, scal_ref[s * width + 32], step, 0)
+        lax.fori_loop(0, scals[s][32], step, 0)
     wait_all(copies)
 
     def combine(t, carry):
@@ -385,12 +398,13 @@
     wait_all(stores)
 
 
-def light(scalars, probe, objects, grads, nsets, strip, tiles, first, rows):
+def light(scalars, probe, objects, grads, strip, tiles, first, rows):
     natural = len(objects) == 3
+    nsets = len(scalars)
     return pl.pallas_call(
         functools.partial(light_kernel, nsets, strip, first, natural),
         out_shape=(f32(2, tiles, rows, 128), f32(tiles, rows, 128)),
-        in_specs=[smem()] + [anywhere()] * (1 + len(objects) + len(grads)),
+        in_specs=[smem()] * nsets + [anywhere()] * (1 + len(objects) + len(grads)),
         out_specs=(anywhere(), anywhere()),
         scratch_shapes=[
             pltpu.VMEM((tiles, (nsets + 1) * strip, 128), jnp.float32),
@@ -403,7 +417,35 @@
         compiler_params=pltpu.CompilerParams(vmem_limit_bytes=VMEM_LIMIT),
         cost_estimate=pl.CostEstimate(flops=16 * nsets * 40000, bytes_accessed=16 * 1024 * 1024, transcendentals=0),
         name="light",
-    )(scalars, probe, *objects, *grads)
+    )(*scalars, probe, *objects, *grads)
+
+
+def meet_kernel(pre, share, above_in, below_in, out, frame, sems):
+    strip = above_in.shape[2]
+
+    def tile(t, carry):
+        for part in range(2):
+            for k, got in enumerate((above_in, below_in)):
+                r = pl.ds(k * strip, strip)
+                frame[part, t, r, :] = pre[part, t, r, :] - got[part, t] * share[t, r, :]
+        pltpu.make_async_copy(frame.at[:, t], out.at[:, t], sems.at[t]).start()
+        return carry
+
+    lax.fori_loop(0, frame.shape[1], tile, 0)
+    wait_all([pltpu.make_async_copy(frame.at[:, t], out.at[:, t], sems.at[t]) for t in range(frame.shape[1])])
+
+
+def meet(pre, share, above_in, below_in):
+    return pl.pallas_call(
+        meet_kernel,
+        out_shape=f32(*pre.shape),
+        in_specs=[vmem()] * 4,
+        out_specs=hbm(),
+        scratch_shapes=[pltpu.VMEM(pre.shape, jnp.float32), pltpu.SemaphoreType.DMA((pre.shape[1],))],
+        compiler_params=pltpu.CompilerParams(vmem_limit_bytes=VMEM_LIMIT),
+        cost_estimate=pl.CostEstimate(flops=1000, bytes_accessed=16 * 1024 * 1024, transcendentals=0),
+        name="meet",
+    )(pre, share, above_in, below_in)
 
 
 def last_kernel(pre, share, above_in, below_in, out):
@@ -451,37 +493,56 @@
     return lax.ppermute(value, "dev", [(i, target(i)) for i in range(count)])
 
 
-def ring_scatter(value, stride, extent):
-    place = (lax.axis_index("dev") // stride) % extent
-    total = lax.dynamic_index_in_dim(value, place, 0, keepdims=False)
-    for k in range(1, extent):
-        piece = lax.dynamic_index_in_dim(value, lax.rem(place + k, extent), 0, keepdims=False)
-        total = total + rotate(piece, stride, extent, k)
+def small_call(kernel, out_shape, operands, scratch=()):
+    several = isinstance(out_shape, tuple)
+    return pl.pallas_call(
+        kernel,
+        out_shape=out_shape,
+        in_specs=[smem()] + [vmem()] * (len(operands) - 1),
+        out_specs=(vmem(),) * len(out_shape) if several else vmem(),
+        scratch_shapes=list(scratch),
+        compiler_params=pltpu.CompilerParams(vmem_limit_bytes=8 * MIB),
+        cost_estimate=pl.CostEstimate(flops=1000, bytes_accessed=1000, transcendentals=0),
+        name=kernel.__name__,
+    )(*operands)
+
+
+PLACE = 34
+
+
+def deal_kernel(scal_ref, keep, got, *outs):
+    rows = outs[0].shape[0]
+    for k, out in enumerate(outs):
+        r = pl.ds(pl.multiple_of(lax.rem(scal_ref[PLACE] + k, len(outs)) * rows, 8), rows)
+        out[...] = keep[r, :] + got[r, :]
+
+
+def gather_kernel(scal_ref, *refs):
+    pieces, out = refs[:-1], refs[-1]
+    rows, count = pieces[0].shape[0], len(pieces)
+    for k, piece in enumerate(pieces):
+        r = pl.ds(pl.multiple_of(lax.rem(scal_ref[PLACE] + count - k, count) * rows, 8), rows)
+        out[r, :] = piece[...]
+
+
+def probe_kernel(scal_ref, mine, other, probe, out, summed):
+    half = mine.shape[0]
+    core = scal_ref[PLACE - 1]
+    summed[pl.ds(pl.multiple_of(core * half, 8), half), :] = mine[...]
+    summed[pl.ds(pl.multiple_of((1 - core) * half, 8), half), :] = other[...]
+    parts, nmodes, length = probe.shape[:3]
+    share = 1.0 / (summed[parts * nmodes * length :, :] + 1.0)
+    for part in range(parts):
+        for m in range(nmodes):
+            first = (part * nmodes + m) * length
+            out[part, m] = probe[part, m] - summed[first : first + length, :] * share
+
+
+def ring_sum(own, pieces, stride):
+    total = own
+    for k, piece in enumerate(pieces):
+        total = total + rotate(piece, stride, 4, k + 1)
     return total
-
-
-def ring_sum(value, stride, extent):
-    total = value
-    for k in range(1, extent):
-        total = total + rotate(value, stride, extent, k)
-    return total
-
-
-def ring_gather(value, stride, extent):
-    place = (lax.axis_index("dev") // stride) % extent
-    out = jnp.zeros((extent,) + value.shape, value.dtype)
-    out = lax.dynamic_update_index_in_dim(out, value, place, 0)
-    for k in range(1, extent):
-        got = rotate(value, stride, extent, k)
-        out = lax.dynamic_update_index_in_dim(out, got, lax.rem(place + extent - k, extent), 0)
-    return out
-
-
-def sum_parts(keep, send):
-    part = keep + rotate(send, 1, 2, 1)
-    part = ring_scatter(part.reshape(4, -1, 128), 32, 4)
-    part = ring_sum(part, 8, 4)
-    return ring_sum(part, 2, 4)
 
 
 def shards(object_field, probe, amplitudes, positions, counts):
@@ -490,45 +551,48 @@
     half, tiles = strip // 2, columns // 128
     barrier = lax.optimization_barrier
     device = lax.axis_index("dev")
-    mine = jnp.concatenate([positions[:, 0] - device * strip, positions[:, 1], counts, (device % 2)[None]])
-
-    def moved(probe, part):
-        summed = ring_gather(part, 1, 2).reshape(2 * nmodes + 1, length, length)
-        grad = summed[: 2 * nmodes].reshape(2, nmodes, length, length)
-        return probe - grad / (summed[2 * nmodes] + 1.0)[None, None]
-
-    def reduced(keep, send):
-        part = sum_parts(keep, send)
-        return ring_gather(part, 32, 4).reshape(-1, 128)
-
-    below = shift_by(object_field[:, :half], -1)
-    prev = shift_by(mine, 1)
+    mine = jnp.concatenate([positions[:, 0] - device * strip, positions[:, 1], counts, (device % 2)[None], (device // 32 % 4)[None]])
+
+    def scattered(keep, send):
+        pieces = small_call(deal_kernel, (f32(keep.shape[0] // 4, length),) * 4, (mine, keep, rotate(send, 1, 2, 1)))
+        return ring_sum(pieces[0], pieces[1:], 32)
+
+    def gathered(part):
+        for stride in (8, 2):
+            part = ring_sum(part, (part,) * 3, stride)
+        pieces = [part] + [rotate(part, 32, 4, k) for k in (1, 2, 3)]
+        return small_call(gather_kernel, f32(4 * part.shape[0], length), [mine] + pieces)
+
+    def moved(probe, half):
+        terms = pltpu.VMEM((2 * half.shape[0], length), jnp.float32)
+        return small_call(probe_kernel, f32(*probe.shape), (mine, half, rotate(half, 1, 2, 1), probe), (terms,))
+
+    extra = jnp.pad(mine.astype(jnp.float32)[None, None], ((0, 1), (0, 7), (0, columns - mine.shape[0])))
+    below = shift_by(jnp.concatenate([object_field[:, :half], extra], axis=1), -1)
+    above = shift_by(jnp.concatenate([object_field[:, half:], extra], axis=1), 1)
     second = shift_by(mine, 2)
-    following = shift_by(mine, -1)
-    above = shift_by(object_field[:, half:], 1)
     amps = (amplitudes, shift_by(amplitudes, 1))
-    before = patterns("own", mine, (object_field, below), None, amps[:1], probe, tiles, 1000)
-    prev, second, following, above, got, before = barrier((prev, second, following, above, amps[1], before))
+    before = patterns("own", (mine,), (object_field, below), None, amps[:1], probe, tiles, 1000)
+    second, above, got, before = barrier((second, above, amps[1], before))
     amps = (amplitudes, got)
-    scalars = jnp.concatenate([mine, prev])
+    prev, following = (a[0, half, : mine.shape[0]].astype(jnp.int32) for a in (above, below))
+    scalars = (mine, prev)
     gtop, gbot, keep, send = patterns("above", scalars, (above, object_field), before, amps[1:], probe, tiles, 10**9)
     above_in = shift_by(gbot, 1)
     below_in = shift_by(gtop, -1)
-    near = jnp.concatenate([second, prev, mine, following])
-    pre, share = light(near, probe, (above, object_field, below), (gtop, gbot), 4, strip, tiles, strip + half, 2 * strip)
-    above_in, below_in, pre, share, keep, send = barrier((above_in, below_in, pre, share, keep, send))
-    probe = moved(probe, reduced(keep, send))
-
-    gtop, gbot, gmid, keep, send, mid = patterns("both", scalars, (pre, share, above_in, below_in), None, amps, probe, tiles, 10**9)
+    near = (second, prev, mine, following)
+    pre, share = light(near, probe, (above, object_field, below), (gtop, gbot), strip, tiles, strip + half, 2 * strip)
+    above_in, below_in, pre, share, part = barrier((above_in, below_in, pre, share, scattered(keep, send)))
+    frame, part = barrier((meet(pre, share, above_in, below_in), part))
+    probe = moved(probe, gathered(part))
+
+    gtop, gbot, gmid, keep, send = patterns("both", scalars, (frame,), None, amps, probe, tiles, 10**9)
     above_in = shift_by(gbot, 1)
     below_in = shift_by(gtop, -1)
-    pre, share = light(jnp.concatenate([prev, mine]), probe, (mid,), (gmid,), 2, strip, tiles, strip, strip)
-    above_in, below_in, pre, share, keep, send = barrier((above_in, below_in, pre, share, keep, send))
-    part = sum_parts(keep, send)
-    current = last(pre, share, above_in, below_in)
-    part = ring_gather(part, 32, 4).reshape(-1, 128)
-    current, part = barrier((current, part))
-    return (current, moved(probe, part))
+    pre, share = light((prev, mine), probe, (frame,), (gmid,), strip, tiles, strip, strip)
+    above_in, below_in, pre, share, part = barrier((above_in, below_in, pre, share, scattered(keep, send)))
+    current, part = barrier((last(pre, share, above_in, below_in), part))
+    return (current, moved(probe, gathered(part)))
 
 
 def solution(mesh):

time: 223 us -> 200 us (0.90); the launches traced: 227 us -> 200 us
  waiting for transfers between devices: 51.7 us -> 33.4 us
  starting transfers between devices: 101 us -> 89.2 us
  Pallas kernels: 64.4 us -> 69.8 us
  local copies, waits for them, and re-layouts: 6.21 us -> 2.92 us
    ppermute x10 -> x8, waiting for transfers between devices: 24.1 us -> 6.8 us  [shift_by(): lax.ppermute(value, 'dev', [(i, i + steps) for i in range(count) if 0 <=...]
    ppermute x28, starting transfers between devices: 74.4 us -> 67.4 us  [rotate(): return lax.ppermute(value, 'dev', [(i, target(i)) for i in range(count)])]
    pallas_call x0 -> x7, Pallas kernels: none -> 5.6 us  [the longest x6 4.39 us: small_call(): pl.pallas_call(kernel, out_shape=out_shape, in_specs=[smem()] + [vmem()]...]
    ppermute x10 -> x8, starting transfers between devices: 26.7 us -> 21.8 us  [shift_by(): lax.ppermute(value, 'dev', [(i, i + steps) for i in range(count) if 0 <=...]
    pallas_call x3, Pallas kernels: 44.8 us -> 48.9 us  [patterns(): pl.pallas_call(functools.partial(pattern_kernel, stage), out_shape=out_sh...]
  transfers between devices with their start and end apart: 38 -> 36, of which waited for: 27 -> 20; matrix products, arithmetic and copies ran while one was open for 1% -> 0% of each run, Pallas kernels for 13% -> 14%
where the time goes in v3:
time: 200 us
  starting transfers between devices  89.2 us (45%)
  Pallas kernels  69.8 us (35%)
  waiting for transfers between devices  33.4 us (17%)
  other arithmetic  3.29 us (2%)
  local copies, waits for them, and re-layouts  2.92 us (1%)
    ppermute x28, starting transfers between devices, rotate(): return lax.ppermute(value, 'dev', [(i, target(i)) for i in range(count)])  67.4 us
    pallas_call x3, Pallas kernels, patterns(): pl.pallas_call(functools.partial(pattern_kernel, stage), out_shape=out_sh...  48.9 us
    ppermute x28, waiting for transfers between devices, rotate(): return lax.ppermute(value, 'dev', [(i, target(i)) for i in range(count)])  26.6 us
    ppermute x8, starting transfers between devices, shift_by(): lax.ppermute(value, 'dev', [(i, i + steps) for i in range(count) if 0 <=...  21.8 us
    pallas_call x2, Pallas kernels, light(): pl.pallas_call(functools.partial(light_kernel, nsets, strip, first, natur...  13.1 us
    ppermute x8, waiting for transfers between devices, shift_by(): lax.ppermute(value, 'dev', [(i, i + steps) for i in range(count) if 0 <=...  6.8 us
    pallas_call x6, Pallas kernels, small_call(): pl.pallas_call(kernel, out_shape=out_shape, in_specs=[smem()] + [vmem()]...  4.39 us
  transfers between devices with their start and end apart: 36, of which 20 were waited for; matrix products, arithmetic and copies ran while one was open for 0% of the time, Pallas kernels for 14%

profile of v3, /device:TPU:1, one launch (start us, length us, event | category | flops | bytes accessed | tf_op | source)
XLA Modules:
  0.0 200.3 jit_solution(16134108878616347460)
XLA Ops:
  5.6 3.5 %collective-permute-start.3 = (f32[2,72,2048]{2,1,0:T(8,128)}, f32[2,72,2048]{2,1,0:T(8,128)}, u32[]{:S(2)}, u32[]{:S(2)}) collective-permute-start(f32[2,72,2048]{2,1,0:T(8,128)} %get-tuple-element.92), channel_id=1, source_target_pairs={{1,0},{2,1},{3,2},{4,3},{5,4},{6,5},{7,6},{8,7},{9,8},{10,9},{11,1... | collective-permute-start | bytes 3538952 | tf_op jit(solution)/shard_map/ppermute | solution.py:481
  9.1 3.5 %collective-permute-start.1 = (f32[2,72,2048]{2,1,0:T(8,128)}, f32[2,72,2048]{2,1,0:T(8,128)}, u32[]{:S(2)}, u32[]{:S(2)}) collective-permute-start(f32[2,72,2048]{2,1,0:T(8,128)} %get-tuple-element.93), channel_id=1, source_target_pairs={{0,1},{1,2},{2,3},{3,4},{4,5},{5,6},{6,7},{7,8},{8,9},{9,10},{10,1... | collective-permute-start | bytes 3538952 | tf_op jit(solution)/shard_map/ppermute | solution.py:481
  12.6 2.4 %collective-permute-start.2 = (f32[16,128,128]{2,1,0:T(8,128)}, f32[16,128,128]{2,1,0:T(8,128)}, u32[]{:S(2)}, u32[]{:S(2)}) collective-permute-start(f32[16,128,128]{2,1,0:T(8,128)} %refs_3_.5), channel_id=1, source_target_pairs={{0,1},{1,2},{2,3},{3,4},{4,5},{5,6},{6,7},{7,8},{8,9},{9,10},{10,1... | collective-permute-start | bytes 3145736 | tf_op jit(solution)/shard_map/ppermute | solution.py:481
  15.1 3.5 %collective-permute-start = (s32[35]{0:T(128)S(1)}, s32[35]{0:T(128)S(1)}, u32[]{:S(2)}, u32[]{:S(2)}) collective-permute-start(s32[35]{0:T(128)S(1)} %concatenate.28.refs_0_.refs_2_.scal_ref.refs_1_), channel_id=1, source_target_pairs={{0,2},{1,3},{2,4},{3,5},{4,6},{5,7},{6,8},{7,9},{8,10},{9,11},{10,... | collective-permute-start | bytes 428 | tf_op jit(solution)/shard_map/ppermute | solution.py:481
  18.6 6.2 %collective-permute-done.3.refs_2_.refs_7_ = f32[2,72,2048]{2,1,0:T(8,128)} collective-permute-done((f32[2,72,2048]{2,1,0:T(8,128)}, f32[2,72,2048]{2,1,0:T(8,128)}, u32[]{:S(2)}, u32[]{:S(2)}) %collective-permute-start.3) | collective-permute-done | bytes 1179680 | tf_op jit(solution)/shard_map/ppermute | solution.py:481
  25.9 14.5 %patterns_own.1 = (f32[2,16,256,128]{3,2,1,0:T(8,128)S(1)}, f32[1152,128]{1,0:T(8,128)S(1)}) custom-call(s32[35]{0:T(128)S(1)} %concatenate.28.refs_0_.refs_2_.scal_ref.refs_1_, f32[2,128,2048]{2,1,0:T(8,128)S(1)} %copy-done, f32[2,72,2048]{2,1,0:T(8,128)} %collective-permute-done.3.refs_2_.refs_7_, f32[16,128,128]{2,1,0:T(8,128)} %refs_3_.5, ...), custom_call_target="tpu_custom_call" | custom-call | flops 1000 | bytes 1024 | tf_op jit(solution)/shard_map/patterns_own/pallas_call | solution.py:327
  41.1 11.3 %patterns_above.1 = (f32[2,16,128,128]{3,2,1,0:T(8,128)S(1)}, f32[2,16,128,128]{3,2,1,0:T(8,128)S(1)}, f32[576,128]{1,0:T(8,128)S(1)}, f32[576,128]{1,0:T(8,128)S(1)}) custom-call(s32[35]{0:T(128)S(1)} %concatenate.28.refs_0_.refs_2_.scal_ref.refs_1_, s32[35]{0:T(128)S(1)} %get-tuple-element.95.refs_1_.refs_0_, ...), custom_call_target="tpu_custom_call" | custom-call | flops 1000000000 | bytes 1024 | tf_op jit(solution)/shard_map/patterns_above/pallas_call | solution.py:327
  54.4 2.5 %collective-permute-start.5 = (f32[2,16,128,128]{3,2,1,0:T(8,128)S(1)}, f32[2,16,128,128]{3,2,1,0:T(8,128)S(1)}, u32[]{:S(2)}, u32[]{:S(2)}) collective-permute-start(f32[2,16,128,128]{3,2,1,0:T(8,128)S(1)} %get-tuple-element.51.refs_8_), channel_id=1, source_target_pairs={{1,0},{2,1},{3,2},{4,3},{5,4},{6,5},{7,6},{8,7},{9,8},{10,9},{11,1... | collective-permute-start | bytes 6291464 | tf_op jit(solution)/shard_map/ppermute | solution.py:481
  57.0 4.1 %collective-permute-done.6.got = f32[576,128]{1,0:T(8,128)S(1)} collective-permute-done((f32[576,128]{1,0:T(8,128)S(1)}, f32[576,128]{1,0:T(8,128)S(1)}, u32[]{:S(2)}, u32[]{:S(2)}) %collective-permute-start.6) | collective-permute-done | bytes 294944 | tf_op jit(solution)/shard_map/ppermute | solution.py:493
  61.7 8.9 %collective-permute-start.7 = (f32[144,128]{1,0:T(8,128)S(1)}, f32[144,128]{1,0:T(8,128)S(1)}, u32[]{:S(2)}, u32[]{:S(2)}) collective-permute-start(f32[144,128]{1,0:T(8,128)S(1)} %get-tuple-element.58), channel_id=1, source_target_pairs={{0,32},{1,33},{2,34},{3,35},{4,36},{5,37},{6,38},{7,39},{8,40},{9,... | collective-permute-start | bytes 221192 | tf_op jit(solution)/shard_map/ppermute | solution.py:493
  70.6 5.4 %collective-permute-start.8 = (f32[144,128]{1,0:T(8,128)S(1)}, f32[144,128]{1,0:T(8,128)S(1)}, u32[]{:S(2)}, u32[]{:S(2)}) collective-permute-start(f32[144,128]{1,0:T(8,128)S(1)} %get-tuple-element.59), channel_id=1, source_target_pairs={{0,64},{1,65},{2,66},{3,67},{4,68},{5,69},{6,70},{7,71},{8,72},{9,... | collective-permute-start | bytes 221192 | tf_op jit(solution)/shard_map/ppermute | solution.py:493
  76.0 7.5 %light.2 = (f32[2,16,256,128]{3,2,1,0:T(8,128)S(1)}, f32[16,256,128]{2,1,0:T(8,128)S(1)}) custom-call(s32[35]{0:T(128)S(1)} %collective-permute-done.refs_0_, s32[35]{0:T(128)S(1)} %get-tuple-element.95.refs_1_.refs_0_, s32[35]{0:T(128)S(1)} %concatenate.28.refs_0_.refs_2_.scal_ref.refs_1_, s32[35]{0:T(128)S(1)} %get-tuple-element.94.refs_3_, ...), custom_call_target="tpu_custom_call" | custom-call | flops 2560000 | bytes 16777216 | tf_op jit(solution)/shard_map/light/pallas_call | solution.py:404
  84.8 4.3 %collective-permute-start.10 = (f32[144,128]{1,0:T(8,128)S(1)}, f32[144,128]{1,0:T(8,128)S(1)}, u32[]{:S(2)}, u32[]{:S(2)}) collective-permute-start(f32[144,128]{1,0:T(8,128)S(1)} %add_add_fusion.5), channel_id=1, source_target_pairs={{0,8},{1,9},{2,10},{3,11},{4,12},{5,13},{6,14},{7,15},{8,16},{9,17... | collective-permute-start | bytes 221192 | tf_op jit(solution)/shard_map/ppermute | solution.py:493
  89.1 2.5 %collective-permute-start.12 = (f32[144,128]{1,0:T(8,128)S(1)}, f32[144,128]{1,0:T(8,128)S(1)}, u32[]{:S(2)}, u32[]{:S(2)}) collective-permute-start(f32[144,128]{1,0:T(8,128)S(1)} %add_add_fusion.5), channel_id=1, source_target_pairs={{0,24},{1,25},{2,26},{3,27},{4,28},{5,29},{6,30},{7,31},{8,0},{9,1... | collective-permute-start | bytes 221192 | tf_op jit(solution)/shard_map/ppermute | solution.py:493
  91.6 2.3 %collective-permute-done.11 = f32[144,128]{1,0:T(8,128)S(1)} collective-permute-done((f32[144,128]{1,0:T(8,128)S(1)}, f32[144,128]{1,0:T(8,128)S(1)}, u32[]{:S(2)}, u32[]{:S(2)}) %collective-permute-start.11) | collective-permute-done | bytes 73760 | tf_op jit(solution)/shard_map/ppermute | solution.py:493
  94.8 11.7 %collective-permute-start.14 = (f32[144,128]{1,0:T(8,128)S(1)}, f32[144,128]{1,0:T(8,128)S(1)}, u32[]{:S(2)}, u32[]{:S(2)}) collective-permute-start(f32[144,128]{1,0:T(8,128)S(1)} %add_add_fusion.4), channel_id=1, source_target_pairs={{0,4},{1,5},{2,6},{3,7},{4,0},{5,1},{6,2},{7,3},{8,12},{9,13},{10,... | collective-permute-start | bytes 221192 | tf_op jit(solution)/shard_map/ppermute | solution.py:493
  107.0 2.0 collective-permute-done.14
  110.2 5.5 %collective-permute-start.17 = (f32[144,128]{1,0:T(8,128)S(1)}, f32[144,128]{1,0:T(8,128)S(1)}, u32[]{:S(2)}, u32[]{:S(2)}) collective-permute-start(f32[144,128]{1,0:T(8,128)S(1)} %add_add_fusion.3.refs_0_), channel_id=1, source_target_pairs={{0,64},{1,65},{2,66},{3,67},{4,68},{5,69},{6,70},{7,71},{8,72},{9,... | collective-permute-start | bytes 221192 | tf_op jit(solution)/shard_map/ppermute | solution.py:493
  115.7 2.0 collective-permute-start.18
  119.8 4.1 %collective-permute-start.19 = (f32[576,128]{1,0:T(8,128)S(1)}, f32[576,128]{1,0:T(8,128)S(1)}, u32[]{:S(2)}, u32[]{:S(2)}) collective-permute-start(f32[576,128]{1,0:T(8,128)S(1)} %gather_kernel.2.mine), channel_id=1, source_target_pairs={{0,1},{1,0},{2,3},{3,2},{4,5},{5,4},{6,7},{7,6},{8,9},{9,8},{10,11... | collective-permute-start | bytes 884744 | tf_op jit(solution)/shard_map/ppermute | solution.py:493
  125.8 23.1 %patterns_both.1 = (f32[2,16,64,128]{3,2,1,0:T(8,128)S(1)}, f32[2,16,64,128]{3,2,1,0:T(8,128)S(1)}, f32[2,16,128,128]{3,2,1,0:T(8,128)S(1)}, f32[576,128]{1,0:T(8,128)S(1)}, f32[576,128]{1,0:T(8,128)S(1)}) custom-call(s32[35]{0:T(128)S(1)} %concatenate.28.refs_0_.refs_2_.scal_ref.refs_1_, s32[35]{0:T(128)S(1)} %get-tuple-element.95.refs_1_.refs_0_, ...), custom_call_target="tpu_custom_call" | custom-call | flops 1000000000 | bytes 1024 | tf_op jit(solution)/shard_map/patterns_both/pallas_call | solution.py:327
  150.9 2.5 %collective-permute-start.21 = (f32[2,16,64,128]{3,2,1,0:T(8,128)S(1)}, f32[2,16,64,128]{3,2,1,0:T(8,128)S(1)}, u32[]{:S(2)}, u32[]{:S(2)}) collective-permute-start(f32[2,16,64,128]{3,2,1,0:T(8,128)S(1)} %get-tuple-element.69), channel_id=1, source_target_pairs={{1,0},{2,1},{3,2},{4,3},{5,4},{6,5},{7,6},{8,7},{9,8},{10,9},{11,1... | collective-permute-start | bytes 3145736 | tf_op jit(solution)/shard_map/ppermute | solution.py:481
  153.4 2.6 %collective-permute-done.22.got = f32[576,128]{1,0:T(8,128)S(1)} collective-permute-done((f32[576,128]{1,0:T(8,128)S(1)}, f32[576,128]{1,0:T(8,128)S(1)}, u32[]{:S(2)}, u32[]{:S(2)}) %collective-permute-start.22) | collective-permute-done | bytes 294944 | tf_op jit(solution)/shard_map/ppermute | solution.py:493
  158.2 2.5 %collective-permute-start.25 = (f32[144,128]{1,0:T(8,128)S(1)}, f32[144,128]{1,0:T(8,128)S(1)}, u32[]{:S(2)}, u32[]{:S(2)}) collective-permute-start(f32[144,128]{1,0:T(8,128)S(1)} %get-tuple-element.78), channel_id=1, source_target_pairs={{0,96},{1,97},{2,98},{3,99},{4,100},{5,101},{6,102},{7,103},{8,104... | collective-permute-start | bytes 221192 | tf_op jit(solution)/shard_map/ppermute | solution.py:493
  160.7 5.7 %light.3 = (f32[2,16,128,128]{3,2,1,0:T(8,128)S(1)}, f32[16,128,128]{2,1,0:T(8,128)S(1)}) custom-call(s32[35]{0:T(128)S(1)} %get-tuple-element.95.refs_1_.refs_0_, s32[35]{0:T(128)S(1)} %concatenate.28.refs_0_.refs_2_.scal_ref.refs_1_, f32[2,4,128,128]{3,2,1,0:T(8,128)S(1)} %probe_kernel.2.refs_5_.refs_2_.probe, ...), custom_call_target="tpu_custom_call" | custom-call | flops 1280000 | bytes 16777216 | tf_op jit(solution)/shard_map/light/pallas_call | solution.py:404
  167.0 2.2 %last.1 = f32[2,128,2048]{2,1,0:T(8,128)} custom-call(f32[2,16,128,128]{3,2,1,0:T(8,128)S(1)} %get-tuple-element.79.pre, f32[16,128,128]{2,1,0:T(8,128)S(1)} %get-tuple-element.80.share, f32[2,16,64,128]{3,2,1,0:T(8,128)S(1)} %collective-permute-done.20.above_in, f32[2,16,64,128]{3,2,1,0:T(8,128)S(1)} %collective-permute-done.21.below_in), custom_call_target="tpu_custom_call" | custom-call | flops 1048576 | bytes 7340032 | tf_op jit(solution)/shard_map/last/pallas_call | solution.py:467
  169.2 2.7 %collective-permute-start.28 = (f32[144,128]{1,0:T(8,128)S(1)}, f32[144,128]{1,0:T(8,128)S(1)}, u32[]{:S(2)}, u32[]{:S(2)}) collective-permute-start(f32[144,128]{1,0:T(8,128)S(1)} %add_add_fusion.2), channel_id=1, source_target_pairs={{0,24},{1,25},{2,26},{3,27},{4,28},{5,29},{6,30},{7,31},{8,0},{9,1... | collective-permute-start | bytes 221192 | tf_op jit(solution)/shard_map/ppermute | solution.py:493
  171.8 2.5 %collective-permute-done.26 = f32[144,128]{1,0:T(8,128)S(1)} collective-permute-done((f32[144,128]{1,0:T(8,128)S(1)}, f32[144,128]{1,0:T(8,128)S(1)}, u32[]{:S(2)}, u32[]{:S(2)}) %collective-permute-start.26) | collective-permute-done | bytes 73760 | tf_op jit(solution)/shard_map/ppermute | solution.py:493
  175.0 7.8 %collective-permute-start.30 = (f32[144,128]{1,0:T(8,128)S(1)}, f32[144,128]{1,0:T(8,128)S(1)}, u32[]{:S(2)}, u32[]{:S(2)}) collective-permute-start(f32[144,128]{1,0:T(8,128)S(1)} %add_add_fusion.1), channel_id=1, source_target_pairs={{0,4},{1,5},{2,6},{3,7},{4,0},{5,1},{6,2},{7,3},{8,12},{9,13},{10,... | collective-permute-start | bytes 221192 | tf_op jit(solution)/shard_map/ppermute | solution.py:493
  186.2 2.6 %collective-permute-start.34 = (f32[144,128]{1,0:T(8,128)S(1)}, f32[144,128]{1,0:T(8,128)S(1)}, u32[]{:S(2)}, u32[]{:S(2)}) collective-permute-start(f32[144,128]{1,0:T(8,128)S(1)} %add_add_fusion.refs_0_), channel_id=1, source_target_pairs={{0,96},{1,97},{2,98},{3,99},{4,100},{5,101},{6,102},{7,103},{8,104... | collective-permute-start | bytes 221192 | tf_op jit(solution)/shard_map/ppermute | solution.py:493
  188.8 2.5 %collective-permute-done.32.refs_1_ = f32[144,128]{1,0:T(8,128)S(1)} collective-permute-done((f32[144,128]{1,0:T(8,128)S(1)}, f32[144,128]{1,0:T(8,128)S(1)}, u32[]{:S(2)}, u32[]{:S(2)}) %collective-permute-start.32) | collective-permute-done | bytes 73760 | tf_op jit(solution)/shard_map/ppermute | solution.py:493
  192.4 5.2 %collective-permute-start.35 = (f32[576,128]{1,0:T(8,128)S(1)}, f32[576,128]{1,0:T(8,128)S(1)}, u32[]{:S(2)}, u32[]{:S(2)}) collective-permute-start(f32[576,128]{1,0:T(8,128)S(1)} %gather_kernel.3.mine), channel_id=1, source_target_pairs={{0,1},{1,0},{2,3},{3,2},{4,5},{5,4},{6,7},{7,6},{8,9},{9,8},{10,11... | collective-permute-start | bytes 884744 | tf_op jit(solution)/shard_map/ppermute | solution.py:493
  (74 shorter events, 29.2 us)
Async XLA Ops:
  5.6 19.3 %collective-permute-start.3 = (f32[2,72,2048]{2,1,0:T(8,128)}, f32[2,72,2048]{2,1,0:T(8,128)}, u32[]{:S(2)}, u32[]{:S(2)}) collective-permute-start(f32[2,72,2048]{2,1,0:T(8,128)} %get-tuple-element.92), channel_id=1, source_target_pairs={{1,0},{2,1},{3,2},{4,3},{5,4},{6,5},{7,6},{8,7},{9,8},{10,9},{11,1... | collective-permute-start | bytes 3538952 | tf_op jit(solution)/shard_map/ppermute | solution.py:481
  9.1 31.4 %collective-permute-start.1 = (f32[2,72,2048]{2,1,0:T(8,128)}, f32[2,72,2048]{2,1,0:T(8,128)}, u32[]{:S(2)}, u32[]{:S(2)}) collective-permute-start(f32[2,72,2048]{2,1,0:T(8,128)} %get-tuple-element.93), channel_id=1, source_target_pairs={{0,1},{1,2},{2,3},{3,4},{4,5},{5,6},{6,7},{7,8},{8,9},{9,10},{10,1... | collective-permute-start | bytes 3538952 | tf_op jit(solution)/shard_map/ppermute | solution.py:481
  12.6 27.8 %collective-permute-start.2 = (f32[16,128,128]{2,1,0:T(8,128)}, f32[16,128,128]{2,1,0:T(8,128)}, u32[]{:S(2)}, u32[]{:S(2)}) collective-permute-start(f32[16,128,128]{2,1,0:T(8,128)} %refs_3_.5), channel_id=1, source_target_pairs={{0,1},{1,2},{2,3},{3,4},{4,5},{5,6},{6,7},{7,8},{8,9},{9,10},{10,1... | collective-permute-start | bytes 3145736 | tf_op jit(solution)/shard_map/ppermute | solution.py:481
  15.1 25.3 %collective-permute-start = (s32[35]{0:T(128)S(1)}, s32[35]{0:T(128)S(1)}, u32[]{:S(2)}, u32[]{:S(2)}) collective-permute-start(s32[35]{0:T(128)S(1)} %concatenate.28.refs_0_.refs_2_.scal_ref.refs_1_), channel_id=1, source_target_pairs={{0,2},{1,3},{2,4},{3,5},{4,6},{5,7},{6,8},{7,9},{8,10},{9,11},{10,... | collective-permute-start | bytes 428 | tf_op jit(solution)/shard_map/ppermute | solution.py:481
  52.4 31.1 %collective-permute-start.4 = (f32[2,16,128,128]{3,2,1,0:T(8,128)S(1)}, f32[2,16,128,128]{3,2,1,0:T(8,128)S(1)}, u32[]{:S(2)}, u32[]{:S(2)}) collective-permute-start(f32[2,16,128,128]{3,2,1,0:T(8,128)S(1)} %get-tuple-element.50.refs_9_), channel_id=1, source_target_pairs={{0,1},{1,2},{2,3},{3,4},{4,5},{5,6},{6,7},{7,8},{8,9},{9,10},{10,1... | collective-permute-start | bytes 6291464 | tf_op jit(solution)/shard_map/ppermute | solution.py:481
  54.4 29.2 %collective-permute-start.5 = (f32[2,16,128,128]{3,2,1,0:T(8,128)S(1)}, f32[2,16,128,128]{3,2,1,0:T(8,128)S(1)}, u32[]{:S(2)}, u32[]{:S(2)}) collective-permute-start(f32[2,16,128,128]{3,2,1,0:T(8,128)S(1)} %get-tuple-element.51.refs_8_), channel_id=1, source_target_pairs={{1,0},{2,1},{3,2},{4,3},{5,4},{6,5},{7,6},{8,7},{9,8},{10,9},{11,1... | collective-permute-start | bytes 6291464 | tf_op jit(solution)/shard_map/ppermute | solution.py:481
  56.9 4.2 %collective-permute-start.6 = (f32[576,128]{1,0:T(8,128)S(1)}, f32[576,128]{1,0:T(8,128)S(1)}, u32[]{:S(2)}, u32[]{:S(2)}) collective-permute-start(f32[576,128]{1,0:T(8,128)S(1)} %get-tuple-element.56), channel_id=1, source_target_pairs={{0,1},{1,0},{2,3},{3,2},{4,5},{5,4},{6,7},{7,6},{8,9},{9,8},{10,11... | collective-permute-start | bytes 884744 | tf_op jit(solution)/shard_map/ppermute | solution.py:493
  61.7 21.8 %collective-permute-start.7 = (f32[144,128]{1,0:T(8,128)S(1)}, f32[144,128]{1,0:T(8,128)S(1)}, u32[]{:S(2)}, u32[]{:S(2)}) collective-permute-start(f32[144,128]{1,0:T(8,128)S(1)} %get-tuple-element.58), channel_id=1, source_target_pairs={{0,32},{1,33},{2,34},{3,35},{4,36},{5,37},{6,38},{7,39},{8,40},{9,... | collective-permute-start | bytes 221192 | tf_op jit(solution)/shard_map/ppermute | solution.py:493
  70.6 12.9 %collective-permute-start.8 = (f32[144,128]{1,0:T(8,128)S(1)}, f32[144,128]{1,0:T(8,128)S(1)}, u32[]{:S(2)}, u32[]{:S(2)}) collective-permute-start(f32[144,128]{1,0:T(8,128)S(1)} %get-tuple-element.59), channel_id=1, source_target_pairs={{0,64},{1,65},{2,66},{3,67},{4,68},{5,69},{6,70},{7,71},{8,72},{9,... | collective-permute-start | bytes 221192 | tf_op jit(solution)/shard_map/ppermute | solution.py:493
  76.0 7.5 %collective-permute-start.9 = (f32[144,128]{1,0:T(8,128)S(1)}, f32[144,128]{1,0:T(8,128)S(1)}, u32[]{:S(2)}, u32[]{:S(2)}) collective-permute-start(f32[144,128]{1,0:T(8,128)S(1)} %get-tuple-element.60), channel_id=1, source_target_pairs={{0,96},{1,97},{2,98},{3,99},{4,100},{5,101},{6,102},{7,103},{8,104... | collective-permute-start | bytes 221192 | tf_op jit(solution)/shard_map/ppermute | solution.py:493
  84.8 6.8 %collective-permute-start.10 = (f32[144,128]{1,0:T(8,128)S(1)}, f32[144,128]{1,0:T(8,128)S(1)}, u32[]{:S(2)}, u32[]{:S(2)}) collective-permute-start(f32[144,128]{1,0:T(8,128)S(1)} %add_add_fusion.5), channel_id=1, source_target_pairs={{0,8},{1,9},{2,10},{3,11},{4,12},{5,13},{6,14},{7,15},{8,16},{9,17... | collective-permute-start | bytes 221192 | tf_op jit(solution)/shard_map/ppermute | solution.py:493
  89.1 4.8 %collective-permute-start.11 = (f32[144,128]{1,0:T(8,128)S(1)}, f32[144,128]{1,0:T(8,128)S(1)}, u32[]{:S(2)}, u32[]{:S(2)}) collective-permute-start(f32[144,128]{1,0:T(8,128)S(1)} %add_add_fusion.5), channel_id=1, source_target_pairs={{0,16},{1,17},{2,18},{3,19},{4,20},{5,21},{6,22},{7,23},{8,24},{9,... | collective-permute-start | bytes 221192 | tf_op jit(solution)/shard_map/ppermute | solution.py:493
  89.1 5.6 %collective-permute-start.12 = (f32[144,128]{1,0:T(8,128)S(1)}, f32[144,128]{1,0:T(8,128)S(1)}, u32[]{:S(2)}, u32[]{:S(2)}) collective-permute-start(f32[144,128]{1,0:T(8,128)S(1)} %add_add_fusion.5), channel_id=1, source_target_pairs={{0,24},{1,25},{2,26},{3,27},{4,28},{5,29},{6,30},{7,31},{8,0},{9,1... | collective-permute-start | bytes 221192 | tf_op jit(solution)/shard_map/ppermute | solution.py:493
  94.7 12.3 %collective-permute-start.13 = (f32[144,128]{1,0:T(8,128)S(1)}, f32[144,128]{1,0:T(8,128)S(1)}, u32[]{:S(2)}, u32[]{:S(2)}) collective-permute-start(f32[144,128]{1,0:T(8,128)S(1)} %add_add_fusion.4), channel_id=1, source_target_pairs={{0,2},{1,3},{2,4},{3,5},{4,6},{5,7},{6,0},{7,1},{8,10},{9,11},{10,... | collective-permute-start | bytes 221192 | tf_op jit(solution)/shard_map/ppermute | solution.py:493
  94.8 14.2 %collective-permute-start.14 = (f32[144,128]{1,0:T(8,128)S(1)}, f32[144,128]{1,0:T(8,128)S(1)}, u32[]{:S(2)}, u32[]{:S(2)}) collective-permute-start(f32[144,128]{1,0:T(8,128)S(1)} %add_add_fusion.4), channel_id=1, source_target_pairs={{0,4},{1,5},{2,6},{3,7},{4,0},{5,1},{6,2},{7,3},{8,12},{9,13},{10,... | collective-permute-start | bytes 221192 | tf_op jit(solution)/shard_map/ppermute | solution.py:493
  110.0 7.7 %collective-permute-start.16 = (f32[144,128]{1,0:T(8,128)S(1)}, f32[144,128]{1,0:T(8,128)S(1)}, u32[]{:S(2)}, u32[]{:S(2)}) collective-permute-start(f32[144,128]{1,0:T(8,128)S(1)} %add_add_fusion.3.refs_0_), channel_id=1, source_target_pairs={{0,32},{1,33},{2,34},{3,35},{4,36},{5,37},{6,38},{7,39},{8,40},{9,... | collective-permute-start | bytes 221192 | tf_op jit(solution)/shard_map/ppermute | solution.py:493
  110.2 8.0 %collective-permute-start.17 = (f32[144,128]{1,0:T(8,128)S(1)}, f32[144,128]{1,0:T(8,128)S(1)}, u32[]{:S(2)}, u32[]{:S(2)}) collective-permute-start(f32[144,128]{1,0:T(8,128)S(1)} %add_add_fusion.3.refs_0_), channel_id=1, source_target_pairs={{0,64},{1,65},{2,66},{3,67},{4,68},{5,69},{6,70},{7,71},{8,72},{9,... | collective-permute-start | bytes 221192 | tf_op jit(solution)/shard_map/ppermute | solution.py:493
  119.8 5.3 %collective-permute-start.19 = (f32[576,128]{1,0:T(8,128)S(1)}, f32[576,128]{1,0:T(8,128)S(1)}, u32[]{:S(2)}, u32[]{:S(2)}) collective-permute-start(f32[576,128]{1,0:T(8,128)S(1)} %gather_kernel.2.mine), channel_id=1, source_target_pairs={{0,1},{1,0},{2,3},{3,2},{4,5},{5,4},{6,7},{7,6},{8,9},{9,8},{10,11... | collective-permute-start | bytes 884744 | tf_op jit(solution)/shard_map/ppermute | solution.py:493
  148.9 17.5 %collective-permute-start.20 = (f32[2,16,64,128]{3,2,1,0:T(8,128)S(1)}, f32[2,16,64,128]{3,2,1,0:T(8,128)S(1)}, u32[]{:S(2)}, u32[]{:S(2)}) collective-permute-start(f32[2,16,64,128]{3,2,1,0:T(8,128)S(1)} %get-tuple-element.68), channel_id=1, source_target_pairs={{0,1},{1,2},{2,3},{3,4},{4,5},{5,6},{6,7},{7,8},{8,9},{9,10},{10,1... | collective-permute-start | bytes 3145736 | tf_op jit(solution)/shard_map/ppermute | solution.py:481
  150.9 16.1 %collective-permute-start.21 = (f32[2,16,64,128]{3,2,1,0:T(8,128)S(1)}, f32[2,16,64,128]{3,2,1,0:T(8,128)S(1)}, u32[]{:S(2)}, u32[]{:S(2)}) collective-permute-start(f32[2,16,64,128]{3,2,1,0:T(8,128)S(1)} %get-tuple-element.69), channel_id=1, source_target_pairs={{1,0},{2,1},{3,2},{4,3},{5,4},{6,5},{7,6},{8,7},{9,8},{10,9},{11,1... | collective-permute-start | bytes 3145736 | tf_op jit(solution)/shard_map/ppermute | solution.py:481
  156.6 9.7 %collective-permute-start.23 = (f32[144,128]{1,0:T(8,128)S(1)}, f32[144,128]{1,0:T(8,128)S(1)}, u32[]{:S(2)}, u32[]{:S(2)}) collective-permute-start(f32[144,128]{1,0:T(8,128)S(1)} %get-tuple-element.76), channel_id=1, source_target_pairs={{0,32},{1,33},{2,34},{3,35},{4,36},{5,37},{6,38},{7,39},{8,40},{9,... | collective-permute-start | bytes 221192 | tf_op jit(solution)/shard_map/ppermute | solution.py:493
  158.2 8.2 %collective-permute-start.24 = (f32[144,128]{1,0:T(8,128)S(1)}, f32[144,128]{1,0:T(8,128)S(1)}, u32[]{:S(2)}, u32[]{:S(2)}) collective-permute-start(f32[144,128]{1,0:T(8,128)S(1)} %get-tuple-element.77), channel_id=1, source_target_pairs={{0,64},{1,65},{2,66},{3,67},{4,68},{5,69},{6,70},{7,71},{8,72},{9,... | collective-permute-start | bytes 221192 | tf_op jit(solution)/shard_map/ppermute | solution.py:493
  158.2 8.2 %collective-permute-start.25 = (f32[144,128]{1,0:T(8,128)S(1)}, f32[144,128]{1,0:T(8,128)S(1)}, u32[]{:S(2)}, u32[]{:S(2)}) collective-permute-start(f32[144,128]{1,0:T(8,128)S(1)} %get-tuple-element.78), channel_id=1, source_target_pairs={{0,96},{1,97},{2,98},{3,99},{4,100},{5,101},{6,102},{7,103},{8,104... | collective-permute-start | bytes 221192 | tf_op jit(solution)/shard_map/ppermute | solution.py:493
  169.1 5.2 %collective-permute-start.26 = (f32[144,128]{1,0:T(8,128)S(1)}, f32[144,128]{1,0:T(8,128)S(1)}, u32[]{:S(2)}, u32[]{:S(2)}) collective-permute-start(f32[144,128]{1,0:T(8,128)S(1)} %add_add_fusion.2), channel_id=1, source_target_pairs={{0,8},{1,9},{2,10},{3,11},{4,12},{5,13},{6,14},{7,15},{8,16},{9,17... | collective-permute-start | bytes 221192 | tf_op jit(solution)/shard_map/ppermute | solution.py:493
  169.1 5.2 %collective-permute-start.27 = (f32[144,128]{1,0:T(8,128)S(1)}, f32[144,128]{1,0:T(8,128)S(1)}, u32[]{:S(2)}, u32[]{:S(2)}) collective-permute-start(f32[144,128]{1,0:T(8,128)S(1)} %add_add_fusion.2), channel_id=1, source_target_pairs={{0,16},{1,17},{2,18},{3,19},{4,20},{5,21},{6,22},{7,23},{8,24},{9,... | collective-permute-start | bytes 221192 | tf_op jit(solution)/shard_map/ppermute | solution.py:493
  169.2 5.8 %collective-permute-start.28 = (f32[144,128]{1,0:T(8,128)S(1)}, f32[144,128]{1,0:T(8,128)S(1)}, u32[]{:S(2)}, u32[]{:S(2)}) collective-permute-start(f32[144,128]{1,0:T(8,128)S(1)} %add_add_fusion.2), channel_id=1, source_target_pairs={{0,24},{1,25},{2,26},{3,27},{4,28},{5,29},{6,30},{7,31},{8,0},{9,1... | collective-permute-start | bytes 221192 | tf_op jit(solution)/shard_map/ppermute | solution.py:493
  175.0 8.4 %collective-permute-start.29 = (f32[144,128]{1,0:T(8,128)S(1)}, f32[144,128]{1,0:T(8,128)S(1)}, u32[]{:S(2)}, u32[]{:S(2)}) collective-permute-start(f32[144,128]{1,0:T(8,128)S(1)} %add_add_fusion.1), channel_id=1, source_target_pairs={{0,2},{1,3},{2,4},{3,5},{4,6},{5,7},{6,0},{7,1},{8,10},{9,11},{10,... | collective-permute-start | bytes 221192 | tf_op jit(solution)/shard_map/ppermute | solution.py:493
  175.0 10.3 %collective-permute-start.30 = (f32[144,128]{1,0:T(8,128)S(1)}, f32[144,128]{1,0:T(8,128)S(1)}, u32[]{:S(2)}, u32[]{:S(2)}) collective-permute-start(f32[144,128]{1,0:T(8,128)S(1)} %add_add_fusion.1), channel_id=1, source_target_pairs={{0,4},{1,5},{2,6},{3,7},{4,0},{5,1},{6,2},{7,3},{8,12},{9,13},{10,... | collective-permute-start | bytes 221192 | tf_op jit(solution)/shard_map/ppermute | solution.py:493
  186.0 5.3 %collective-permute-start.32 = (f32[144,128]{1,0:T(8,128)S(1)}, f32[144,128]{1,0:T(8,128)S(1)}, u32[]{:S(2)}, u32[]{:S(2)}) collective-permute-start(f32[144,128]{1,0:T(8,128)S(1)} %add_add_fusion.refs_0_), channel_id=1, source_target_pairs={{0,32},{1,33},{2,34},{3,35},{4,36},{5,37},{6,38},{7,39},{8,40},{9,... | collective-permute-start | bytes 221192 | tf_op jit(solution)/shard_map/ppermute | solution.py:493
  186.1 5.2 %collective-permute-start.33 = (f32[144,128]{1,0:T(8,128)S(1)}, f32[144,128]{1,0:T(8,128)S(1)}, u32[]{:S(2)}, u32[]{:S(2)}) collective-permute-start(f32[144,128]{1,0:T(8,128)S(1)} %add_add_fusion.refs_0_), channel_id=1, source_target_pairs={{0,64},{1,65},{2,66},{3,67},{4,68},{5,69},{6,70},{7,71},{8,72},{9,... | collective-permute-start | bytes 221192 | tf_op jit(solution)/shard_map/ppermute | solution.py:493
  186.2 5.7 %collective-permute-start.34 = (f32[144,128]{1,0:T(8,128)S(1)}, f32[144,128]{1,0:T(8,128)S(1)}, u32[]{:S(2)}, u32[]{:S(2)}) collective-permute-start(f32[144,128]{1,0:T(8,128)S(1)} %add_add_fusion.refs_0_), channel_id=1, source_target_pairs={{0,96},{1,97},{2,98},{3,99},{4,100},{5,101},{6,102},{7,103},{8,104... | collective-permute-start | bytes 221192 | tf_op jit(solution)/shard_map/ppermute | solution.py:493
  192.4 6.4 %collective-permute-start.35 = (f32[576,128]{1,0:T(8,128)S(1)}, f32[576,128]{1,0:T(8,128)S(1)}, u32[]{:S(2)}, u32[]{:S(2)}) collective-permute-start(f32[576,128]{1,0:T(8,128)S(1)} %gather_kernel.3.mine), channel_id=1, source_target_pairs={{0,1},{1,0},{2,3},{3,2},{4,5},{5,4},{6,7},{7,6},{8,9},{9,8},{10,11... | collective-permute-start | bytes 884744 | tf_op jit(solution)/shard_map/ppermute | solution.py:493
  (8 other events, 90.8 us)
